TPU v7x, 32 devices: a whole 2x2x4 slice. The times are simulated.
32 devices in a mesh: expert: 8 (over z, x), tensor: 4 (over y, core).
Axes of the slice: x: 2, y: 2, z: 4, core: 2. Of those that a mesh axis runs over, the one named last changes fastest.
Arguments:
- tokens: bfloat16 [4096, 2560], P(('expert', 'tensor')), may hold values from -6 to 6
- expert_ids: int32 [4096, 1], P(('expert', 'tensor')), may hold values from 0 to 7; in each aligned block of 128 rows (0 to 127, 128 to 255, ...) at most 24 rows name the same one
- live_counts: int32 [32], P(('expert', 'tensor')), may hold values from 1 to 128, 2560 in all
- router: bfloat16 [2560, 8], replicated, may hold values from -0.125 to 0.125
- up_weight: bfloat16 [8, 2560, 4096], P('expert', None, 'tensor'), may hold values from -0.125 to 0.125
- down_weight: bfloat16 [8, 4096, 2560], P('expert', 'tensor'), may hold values from -0.09375 to 0.09375
- out_grad: bfloat16 [4096, 2560], P(('expert', 'tensor')), may hold values from -6 to 6
Outputs:
- mixed: bfloat16 [4096, 2560], P(('expert', 'tensor'))
- token_grad: bfloat16 [4096, 2560], P(('expert', 'tensor'))
- up_grad: bfloat16 [8, 2560, 4096], P('expert', None, 'tensor')
- down_grad: bfloat16 [8, 4096, 2560], P('expert', 'tensor')
- router_grad: float32 [2560, 8], replicated
Inputs may be any that keep to these rules, and one draw needn't show every extreme that they name: `expert_ids`: within the rows of one device (aligned blocks of 128 rows) no expert is named by more than 24 rows; in every draw some expert is named by exactly 24 rows of some device. live_counts[k] real token rows lead device k's 128 rows, the rest are padding; some device holds exactly 128 real rows in every draw.
All inputs are finite; a program needn't handle non-finite values.
Results may differ from a plain program's by a relative error of at most 0.0063.
Values may be sent and summed in bfloat16 or wider, within the bound.
No kernel may reach another device: no remote copies, remote signals or barrier semaphores. Data moves between devices by JAX's collectives and lax.ppermute only.
A program may use at most 128 MiB of HBM per device.

v0:
```python
import functools

import jax
import jax.numpy as jnp
from jax import lax
from jax.experimental import pallas as pl
from jax.experimental.pallas import tpu as pltpu
from jax.sharding import PartitionSpec as P


def dot(a, b, out=jnp.float32, dims=((1,), (0,))):
    return lax.dot_general(a, b, (dims, ((), ())), preferred_element_type=jnp.float32).astype(out)


def joined(blocks):
    return jnp.concatenate(blocks, axis=0)


def after(x, *earlier):
    return lax.optimization_barrier((x,) + earlier)[0]


def added(a, b):
    return (a.astype(jnp.float32) + b.astype(jnp.float32)).astype(jnp.bfloat16)


def call(kernel, grid, in_specs, outs, out_specs, scratch=(), flops=1, moved=1, mib=20):
    return pl.pallas_call(
        kernel,
        grid=(grid,),
        in_specs=in_specs,
        out_specs=out_specs,
        out_shape=outs,
        scratch_shapes=scratch,
        compiler_params=pltpu.CompilerParams(vmem_limit_bytes=mib * 1024 * 1024),
        cost_estimate=pl.CostEstimate(flops=flops, bytes_accessed=moved, transcendentals=0),
    )


def tile_of(size, want):
    return want if size % want == 0 else size


def nt(a, b):
    return lax.dot_general(a, b, (((1,), (1,)), ((), ())), preferred_element_type=jnp.float32)


def tn(a, b):
    return lax.dot_general(a, b, (((0,), (0,)), ((), ())), preferred_element_type=jnp.float32)


def join_blocks(blocks, joint):
    count = blocks[0].shape[0]
    for i, block in enumerate(blocks):
        joint[i * count : (i + 1) * count] = block[...]


def split_blocks(value, blocks):
    count = blocks[0].shape[0]
    for i, block in enumerate(blocks):
        block[...] = value[i * count : (i + 1) * count].astype(block.dtype)


def forward_kernel(blocks, steps, tile, *refs):
    rows, (up, down) = refs[:blocks], refs[blocks : blocks + 2]
    outs = refs[blocks + 2 : -2]
    hidden, active, term = outs[:blocks], outs[blocks : 2 * blocks], outs[2 * blocks :]
    joint, held = refs[-2:]
    step = pl.program_id(0)

    @pl.when(step == 0)
    def _():
        join_blocks(rows, joint)

    @pl.when(step < steps)
    def _():
        place = pl.ds(pl.multiple_of(step * tile, tile), tile)
        value = jnp.dot(joint[...], up[...], preferred_element_type=jnp.float32)
        split_blocks(value, hidden)
        rounded = (value * jax.nn.sigmoid(value)).astype(jnp.bfloat16)
        split_blocks(rounded, active)
        held[:, place] = rounded

    @pl.when(step >= steps)
    def _():
        split_blocks(jnp.dot(held[...], down[...], preferred_element_type=jnp.float32), term)


def backward_kernel(blocks, steps, last, tile, *refs):
    cots, hidden, active, rows = (refs[k * blocks : (k + 1) * blocks] for k in range(4))
    down, up, column = refs[4 * blocks : 4 * blocks + 3]
    outs = refs[4 * blocks + 3 : -3]
    hidden_cot, term = (outs[k * blocks : (k + 1) * blocks] for k in range(2))
    total = outs[-1]
    joint, held, slope = refs[-3:]
    count = cots[0].shape[0]
    step = pl.program_id(0)

    @pl.when(step == 0)
    def _():
        join_blocks(cots, joint)
        slope[...] = jnp.zeros_like(slope)

    @pl.when(step < steps)
    def _():
        place = pl.ds(pl.multiple_of(step * tile, tile), tile)
        back_all = nt(joint[...], down[...])
        for i in range(blocks):
            back = back_all[i * count : (i + 1) * count]
            value = hidden[i][...]
            sig = jax.nn.sigmoid(value)
            rounded = (back * (sig * (1.0 + value * (1.0 - sig)))).astype(jnp.bfloat16)
            hidden_cot[i][...] = rounded
            held[i * count : (i + 1) * count, place] = rounded
            product = back * active[i][...].astype(jnp.float32)
            lanes = slope.shape[2]
            slope[i] += sum(product[:, k : k + lanes] for k in range(0, tile, lanes))

    @pl.when(step >= steps)
    def _():
        split_blocks(nt(held[...], up[...]), term)

    @pl.when(step == last)
    def _():
        add_up = jnp.zeros(total.shape, jnp.float32)
        for i in range(blocks):
            off = 1.0 - jax.nn.sigmoid(nt(rows[i][...], column[...])[:, :1])
            own = jnp.sum(slope[i], axis=1, keepdims=True) * off
            high = own.astype(jnp.bfloat16)
            rest = own - high.astype(jnp.float32)
            middle = rest.astype(jnp.bfloat16)
            least = rest - middle.astype(jnp.float32)
            lane = lax.broadcasted_iota(jnp.int32, slope.shape[1:], 1)
            split = jnp.zeros(slope.shape[1:], jnp.float32)
            for k, part in enumerate((high, middle, least)):
                split = jnp.where(lane == k, part.astype(jnp.float32), split)
            sums = tn(split.astype(jnp.bfloat16), rows[i][...])
            add_up += sums[0:1] + sums[1:2] + sums[2:3]
        total[...] = add_up


def tiles_for(rows, w_up):
    width, hidden = w_up.shape
    tile, wide = tile_of(hidden, 512), tile_of(width, 1280)
    return rows.shape[0], width, hidden, tile, wide, hidden // tile, width // wide


def whole(shape):
    return pl.BlockSpec(shape, lambda i: (0,) * len(shape), pipeline_mode=pl.Buffered(1))


def forward(rows, w_up, w_down):
    count, width, hidden, tile, wide, steps, wides = tiles_for(rows[0], w_up)
    n = len(rows)
    first, second = lambda i: jnp.minimum(i, steps - 1), lambda i: jnp.maximum(i - steps, 0)
    part = pl.BlockSpec((count, tile), lambda i: (0, first(i)))
    outs = call(
        functools.partial(forward_kernel, n, steps, tile),
        steps + wides,
        [whole((count, width))] * n
        + [
            pl.BlockSpec((width, tile), lambda i: (0, first(i))),
            pl.BlockSpec((hidden, wide), lambda i: (0, second(i))),
        ],
        [jax.ShapeDtypeStruct((count, hidden), jnp.float32)] * n
        + [jax.ShapeDtypeStruct((count, hidden), jnp.bfloat16)] * n
        + [jax.ShapeDtypeStruct((count, width), jnp.bfloat16)] * n,
        [part] * (2 * n) + [pl.BlockSpec((count, wide), lambda i: (0, second(i)))] * n,
        [
            pltpu.VMEM((n * count, width), jnp.bfloat16),
            pltpu.VMEM((n * count, hidden), jnp.bfloat16),
        ],
        mib=56,
    )(*rows, w_up, w_down)
    return list(outs[:n]), list(outs[n : 2 * n]), list(outs[2 * n :])


def backward(cots, hiddens, actives, rows, w_up, w_down, column):
    count, width, hidden, tile, wide, steps, wides = tiles_for(cots[0], w_up)
    n = len(cots)
    first, second = lambda i: jnp.minimum(i, steps - 1), lambda i: jnp.maximum(i - steps, 0)
    part = pl.BlockSpec((count, tile), lambda i: (0, first(i)))
    outs = call(
        functools.partial(backward_kernel, n, steps, steps + wides - 1, tile),
        steps + wides,
        [whole((count, width))] * n
        + [part] * (2 * n)
        + [whole((count, width))] * n
        + [
            pl.BlockSpec((tile, width), lambda i: (first(i), 0)),
            pl.BlockSpec((wide, hidden), lambda i: (second(i), 0)),
            whole(column.shape),
        ],
        [jax.ShapeDtypeStruct((count, hidden), jnp.bfloat16)] * n
        + [jax.ShapeDtypeStruct((count, width), jnp.bfloat16)] * n
        + [jax.ShapeDtypeStruct((1, width), jnp.float32)],
        [part] * n
        + [pl.BlockSpec((count, wide), lambda i: (0, second(i)))] * n
        + [pl.BlockSpec((1, width), lambda i: (0, 0))],
        [
            pltpu.VMEM((n * count, width), jnp.bfloat16),
            pltpu.VMEM((n * count, hidden), jnp.bfloat16),
            pltpu.VMEM((n, count, tile_of(tile, 128)), jnp.float32),
        ],
        mib=56,
    )(*cots, *hiddens, *actives, *rows, w_down, w_up, column)
    return list(outs[:n]), list(outs[n : 2 * n]), outs[-1]


def gradient_kernel(blocks, *refs):
    left, right, out = refs[:blocks], refs[blocks : 2 * blocks], refs[-1]
    total = sum(tn(a[...], b[...]) for a, b in zip(left, right))
    out[...] = total.astype(out.dtype)


def gradient(lefts, rights, want):
    count, height = lefts[0].shape
    width = rights[0].shape[1]
    tile = tile_of(height, want)
    return call(
        functools.partial(gradient_kernel, len(lefts)),
        height // tile,
        [pl.BlockSpec((count, tile), lambda i: (0, i))] * len(lefts)
        + [whole((count, width))] * len(rights),
        jax.ShapeDtypeStruct((height, width), jnp.bfloat16),
        pl.BlockSpec((tile, width), lambda i: (i, 0)),
        flops=2 * len(lefts) * count * height * width,
        moved=2 * (len(lefts) * count * (height + width) + height * width),
    )(*lefts, *rights)


def make(n_expert, n_tensor):
    top, low = n_tensor // 2, n_tensor // 2

    def cross(x, bit):
        return lax.ppermute(x, "tensor", [(i, i ^ bit) for i in range(n_tensor)])

    def gather_low(rows):
        held = [rows]
        bit = 1
        while bit < low:
            held = held + [cross(h, bit) for h in held]
            bit *= 2
        return held

    def sum_low(terms):
        while len(terms) > 1:
            bit = len(terms) // 2
            terms = [added(a, cross(b, bit)) for a, b in zip(terms[:bit], terms[bit:])]
        return terms[0]

    def per_device(tokens, expert_ids, live_counts, router, up_weight, down_weight, out_grad):
        tok_rows, width = tokens.shape
        experts = router.shape[1]
        most = 3 * tok_rows // (2 * experts)
        slots = experts * most
        me = lax.axis_index("expert")
        ids = expert_ids[:, 0]
        live = lax.iota(jnp.int32, tok_rows) < live_counts[0]
        chosen = ids[:, None] == lax.iota(jnp.int32, experts)[None, :]
        chosen_int = chosen.astype(jnp.int32)
        rank = jnp.sum(jnp.cumsum(chosen_int, axis=0) * chosen_int, axis=1) - 1
        target = jnp.where(live, ids * most + rank, -1)
        placing = (lax.iota(jnp.int32, slots)[:, None] == target[None, :]).astype(jnp.bfloat16)
        w_up, w_down = up_weight[0], down_weight[0]

        def swap(x):
            return lax.all_to_all(x, "expert", split_axis=0, concat_axis=0, tiled=True)

        def exchange(x):
            return swap(x.reshape(experts, most, width)).reshape(slots, width)

        tok_near = exchange(dot(placing, tokens, jnp.bfloat16))
        logits = dot(tokens, router)
        gate = jax.nn.sigmoid(jnp.sum(logits * chosen.astype(jnp.float32), axis=1))
        out_cot = (gate[:, None] * out_grad.astype(jnp.float32)).astype(jnp.bfloat16)
        cot_near = exchange(after(dot(placing, out_cot, jnp.bfloat16), tok_near))
        tok_far = cross(tok_near, top)
        cot_far = cross(cot_near, top)

        rows = gather_low(after(tok_far, cot_near)) + gather_low(tok_near)
        hidden, active, term = forward(rows, w_up, w_down)
        out_far_sum, out_near = sum_low(term[:low]), sum_low(term[low:])
        cot_far = after(cot_far, *term)
        out_far = cross(after(out_far_sum, cot_far), top)

        column = lax.dynamic_slice_in_dim(router, me, 1, axis=1).T
        column = jnp.broadcast_to(column, (16, width))
        cots = gather_low(cot_far)
        hidden_cot, far_term, far_column = backward(
            [after(x, out_far_sum) for x in cots],
            hidden[:low],
            active[:low],
            rows[:low],
            w_up,
            w_down,
            column,
        )
        out_far = after(out_far, *far_term)
        out_sum = added(out_near, out_far)
        out_home = exchange(out_sum)
        back_far_sum = sum_low([after(x, out_far) for x in far_term])
        back_far = cross(back_far_sum, top)

        near = [after(x, out_sum, back_far_sum) for x in gather_low(cot_near)]
        near_hidden_cot, near_term, near_column = backward(
            near, hidden[low:], active[low:], rows[low:], w_up, w_down, column
        )
        back_near = sum_low([after(x, back_far) for x in near_term])
        cots, hidden_cot = cots + near, hidden_cot + near_hidden_cot

        columns = far_column + near_column
        bit = 1
        while bit < n_tensor:
            columns = columns + cross(columns, bit)
            bit *= 2
        columns = after(columns, out_home)
        lanes = -(-width // (most * 128)) * 128
        high = columns.astype(jnp.bfloat16)
        rest = (columns - high.astype(jnp.float32)).astype(jnp.bfloat16)
        beside = jnp.concatenate(
            [
                jnp.pad(x, ((0, 0), (0, most * lanes - width))).reshape(1, most, lanes)
                for x in (high, rest)
            ],
            axis=2,
        )

        back_sum = added(back_near, after(back_far, out_home))

        up_grad = gradient([after(x, back_sum, columns) for x in rows], hidden_cot, 512)[None]
        down_grad = gradient([after(x, back_sum, columns) for x in active], cots, 256)[None]

        back_sum = back_sum.reshape(experts, most, width)
        beside = jnp.broadcast_to(beside, (experts, most, 2 * lanes))
        came = swap(jnp.concatenate([back_sum, beside], axis=2))
        back_home = came[:, :, :width].reshape(slots, width)
        high, rest = (
            came[:, :, k : k + lanes].reshape(experts, most * lanes)[:, :width].astype(jnp.float32)
            for k in (width, width + lanes)
        )
        router_grad = (high + rest).T

        out_rows = dot(placing, after(out_home, back_sum), jnp.bfloat16, ((0,), (0,)))
        cot_rows = dot(placing, back_home, jnp.bfloat16, ((0,), (0,)))
        out_wide = out_rows.astype(jnp.float32)
        mixed = (gate[:, None] * out_wide).astype(jnp.bfloat16)
        own_slope = jnp.sum(out_grad.astype(jnp.float32) * out_wide, axis=1) * gate * (1.0 - gate)
        named = dot(chosen.astype(jnp.bfloat16), router, dims=((1,), (1,)))
        token_grad = (cot_rows.astype(jnp.float32) + own_slope[:, None] * named).astype(jnp.bfloat16)
        return (mixed, token_grad, up_grad, down_grad, router_grad)

    return per_device


def solution(mesh):
    in_specs = (
        P(("expert", "tensor"), None),
        P(("expert", "tensor"), None),
        P(("expert", "tensor")),
        P(),
        P("expert", None, "tensor"),
        P("expert", "tensor", None),
        P(("expert", "tensor"), None),
    )
    out_specs = (
        P(("expert", "tensor"), None),
        P(("expert", "tensor"), None),
        P("expert", None, "tensor"),
        P("expert", "tensor", None),
        P(),
    )
    return jax.shard_map(
        make(mesh.shape["expert"], mesh.shape["tensor"]),
        mesh=mesh,
        in_specs=in_specs,
        out_specs=out_specs,
        check_vma=False,
    )
```

profile of v0, /device:TPU:0, one launch (start us, length us, event | category | flops | bytes accessed | tf_op | source)
XLA Modules:
  0.0 195.9 jit_solution(949422756908987957)
XLA Ops:
  0.6 0.0 copy-start
  0.6 0.0 copy-start.23
  1.4 0.7 fusion.13
  2.0 0.1 copy.12
  2.1 0.2 reduce_window_sum.11
  2.4 0.7 select_reduce_fusion
  3.1 0.7 compare_select_fusion
  3.7 1.4 convolution_convert_fusion.1
  5.1 7.3 %all-to-all-start = ((bf16[8,24,2560]{2,1,0:T(8,128)(2,1)}), bf16[8,24,2560]{2,1,0:T(8,128)(2,1)S(1)}, u32[]{:S(2)}, u32[]{:S(2)}) async-start(bf16[8,24,2560]{2,1,0:T(8,128)(2,1)} %bitcast.2), calls=%async_computation | async-start | bytes 1966080 | tf_op jit(solution)/shard_map/all_to_all | solution.py:268
  12.3 0.3 fusion.6
  12.6 1.5 convolution_convert_fusion
  14.1 22.6 %all-to-all-done = bf16[8,24,2560]{2,1,0:T(8,128)(2,1)S(1)} async-done(((bf16[8,24,2560]{2,1,0:T(8,128)(2,1)}), bf16[8,24,2560]{2,1,0:T(8,128)(2,1)S(1)}, u32[]{:S(2)}, u32[]{:S(2)}) %all-to-all-start) | async-done | bytes 983072 | tf_op jit(solution)/shard_map/all_to_all | solution.py:268
  36.7 3.6 %all-to-all-start.1 = ((bf16[8,24,2560]{2,1,0:T(8,128)(2,1)}), bf16[8,24,2560]{2,1,0:T(8,128)(2,1)S(1)}, u32[]{:S(2)}, u32[]{:S(2)}) async-start(bf16[8,24,2560]{2,1,0:T(8,128)(2,1)} %bitcast.54), calls=%async_computation.1 | async-start | bytes 1966080 | tf_op jit(solution)/shard_map/all_to_all | solution.py:268
  40.3 1.6 collective-permute-start
  41.9 0.0 collective-permute-start.2
  41.9 21.9 %collective-permute-done.refs_0_.refs_6_ = bf16[192,2560]{1,0:T(8,128)(2,1)} collective-permute-done((bf16[192,2560]{1,0:T(8,128)(2,1)S(1)}, bf16[192,2560]{1,0:T(8,128)(2,1)}, u32[]{:S(2)}, u32[]{:S(2)}) %collective-permute-start) | collective-permute-done | bytes 983072 | tf_op jit(solution)/shard_map/ppermute | solution.py:236
  63.8 1.0 all-to-all-done.1
  64.8 0.0 collective-permute-start.1
  64.8 1.5 collective-permute-start.5
  66.4 1.3 collective-permute-done.1.refs_1_.refs_7_
  67.6 0.9 copy-done.5
  68.6 15.1 %shard_map.110 = (f32[192,1024]{1,0:T(8,128)}, f32[192,1024]{1,0:T(8,128)}, f32[192,1024]{1,0:T(8,128)}, f32[192,1024]{1,0:T(8,128)}, bf16[192,1024]{1,0:T(8,128...) custom-call(bf16[192,2560]{1,0:T(8,128)(2,1)} %collective-permute-do, ...), custom_call_target="tpu_custom_call" | custom-call | flops 1 | bytes 1 | tf_op jit(solution)/shard_map/pallas_call | solution.py:157
  83.7 0.2 collective-permute-start.4
  83.9 5.2 %collective-permute-done.5.refs_0_.refs_4_ = bf16[192,2560]{1,0:T(8,128)(2,1)} collective-permute-done((bf16[192,2560]{1,0:T(8,128)(2,1)S(1)}, bf16[192,2560]{1,0:T(8,128)(2,1)}, u32[]{:S(2)}, u32[]{:S(2)}) %collective-permute-start.5) | collective-permute-done | bytes 983072 | tf_op jit(solution)/shard_map/ppermute | solution.py:236
  89.1 0.0 collective-permute-start.7
  89.1 0.0 collective-permute-done.4
  89.1 2.4 %add_convert_fusion.4 = bf16[192,2560]{1,0:T(8,128)(2,1)} fusion(bf16[192,2560]{1,0:T(8,128)(2,1)S(1)} %collective-permute-done.4, bf16[192,2560]{1,0:T(8,128)(2,1)} %get-tuple-element.55), kind=kLoop, calls=%fused_computation.13 | loop fusion | flops 1966080 | bytes 2949120 | tf_op jit(solution)/shard_map/convert_element_type | solution.py:24
  91.5 1.5 collective-permute-start.6
  93.0 0.2 collective-permute-start.3
  93.3 0.0 collective-permute-done.7.refs_1_.refs_5_
  93.3 0.7 broadcast_in_dim.15.refs_10_
  94.0 0.3 copy-done.7
  94.3 13.6 %shard_map.111 = (bf16[192,1024]{1,0:T(8,128)(2,1)}, bf16[192,1024]{1,0:T(8,128)(2,1)}, bf16[192,2560]{1,0:T(8,128)(2,1)}, bf16[192,2560]{1,0:T(8,128)(2,1)}, f32[1,2560]{1,0:T(1,128)}) custom-call(bf16[192,2560]{1,0:T(8,128)(2,1)} %collective-permute-done.5.refs_0_.refs_4_, bf16[192,2560]{1,0:T(8,128)(2,1)} %copy-done.7, ...), custom_call_target="tpu_custom_call" | custom-call | flops 1 | bytes 1 | tf_op jit(solution)/shard_map/pallas_call | solution.py:183
  107.9 8.0 %collective-permute-done.6 = bf16[192,2560]{1,0:T(8,128)(2,1)} collective-permute-done((bf16[192,2560]{1,0:T(8,128)(2,1)}, bf16[192,2560]{1,0:T(8,128)(2,1)}, u32[]{:S(2)}, u32[]{:S(2)}) %collective-permute-start.6) | collective-permute-done | bytes 983072 | tf_op jit(solution)/shard_map/ppermute | solution.py:236
  116.0 0.0 collective-permute-start.8
  116.0 0.5 collective-permute-start.9
  116.5 2.8 %add_convert_fusion.3 = bf16[192,2560]{1,0:T(8,128)(2,1)} fusion(bf16[192,2560]{1,0:T(8,128)(2,1)} %collective-permute-done.6, bf16[192,2560]{1,0:T(8,128)(2,1)} %collective-permute-done.3, bf16[192,2560]{1,0:T(8,128)(2,1)S(1)} %copy-done.20), kind=kLoop, calls=%fused_computation.12 | loop fusion | flops 3932160 | bytes 3932160 | tf_op jit(solution)/shard_map/convert_element_type | solution.py:24
  119.3 4.7 %all-to-all-start.2 = ((bf16[8,24,2560]{2,1,0:T(8,128)(2,1)}), bf16[8,24,2560]{2,1,0:T(8,128)(2,1)}, u32[]{:S(2)}, u32[]{:S(2)}) async-start(bf16[8,24,2560]{2,1,0:T(8,128)(2,1)} %bitcast.55), calls=%async_computation.2 | async-start | bytes 1966080 | tf_op jit(solution)/shard_map/all_to_all | solution.py:268
  124.0 0.0 collective-permute-done.8
  124.0 1.7 add_convert_fusion.2
  125.7 1.6 collective-permute-start.10
  127.3 1.0 copy-done.9
  128.3 13.7 %shard_map.112 = (bf16[192,1024]{1,0:T(8,128)(2,1)}, bf16[192,1024]{1,0:T(8,128)(2,1)}, bf16[192,2560]{1,0:T(8,128)(2,1)}, bf16[192,2560]{1,0:T(8,128)(2,1)}, f32[1,2560]{1,0:T(1,128)}) custom-call(bf16[192,2560]{1,0:T(8,128)(2,1)} %bitcast.45, bf16[192,2560]{1,0:T(8,128)(2,1)} %copy-done.9, f32[192,1024]{1,0:T(8,128)} %get-tuple-element.72.refs_2_, ...), custom_call_target="tpu_custom_call" | custom-call | flops 1 | bytes 1 | tf_op jit(solution)/shard_map/pallas_call | solution.py:183
  142.0 7.2 %collective-permute-done.10 = bf16[192,2560]{1,0:T(8,128)(2,1)S(1)} collective-permute-done((bf16[192,2560]{1,0:T(8,128)(2,1)S(1)}, bf16[192,2560]{1,0:T(8,128)(2,1)S(1)}, u32[]{:S(2)}, u32[]{:S(2)}) %collective-permute-start.10) | collective-permute-done | bytes 983072 | tf_op jit(solution)/shard_map/ppermute | solution.py:236
  149.2 1.0 copy-done.21
  150.2 0.7 add.71
  150.9 0.6 collective-permute-start.12
  151.5 1.3 collective-permute-done.12
  152.8 1.6 collective-permute-start.13
  154.4 2.2 %collective-permute-done.13 = f32[1,2560]{1,0:T(1,128)S(1)} collective-permute-done((f32[1,2560]{1,0:T(1,128)S(1)}, f32[1,2560]{1,0:T(1,128)S(1)}, u32[]{:S(2)}, u32[]{:S(2)}) %collective-permute-start.13) | collective-permute-done | bytes 10272 | tf_op jit(solution)/shard_map/ppermute | solution.py:236
  156.6 0.1 pad_reduce_fusion
  156.7 1.9 add_convert_fusion
  158.5 1.1 pad_maximum_fusion
  159.6 6.0 %all-to-all-start.3 = ((bf16[8,24,2816]{2,1,0:T(8,128)(2,1)}), bf16[8,24,2816]{2,1,0:T(8,128)(2,1)}, u32[]{:S(2)}, u32[]{:S(2)}) async-start(bf16[8,24,2816]{2,1,0:T(8,128)(2,1)} %pad_maximum_fusion), calls=%async_computation.3 | async-start | bytes 2162688 | tf_op jit(solution)/shard_map/all_to_all | solution.py:268
  165.6 2.8 %fusion.5 = (f32[128]{0:T(128)S(1)}, bf16[128,2560]{1,0:T(8,128)(2,1)}) fusion(bf16[128,2560]{1,0:T(8,128)(2,1)} %param.13, f32[128]{0:T(128)S(1)} %add_divide_fusion, bf16[192,2560]{1,0:T(8,128)(2,1)} %bitcast.9, s32[128]{0:T(128)S(1)} %compare_select_fusion), kind=kOutput, calls=%fused_computation.18 | convolution fusion | flops 128147328 | bytes 2295296 | tf_op jit(solution)/shard_map/dot_general | solution.py:12
  168.5 0.0 copy-start.11
  168.5 8.9 %shard_map.113 = bf16[2560,1024]{1,0:T(8,128)(2,1)} custom-call(bf16[192,2560]{1,0:T(8,128)(2,1)} %collective-permute-done.refs_0_.refs_6_, bf16[192,2560]{1,0:T(8,128)(2,1)S(1)} %copy-done.6, bf16[192,2560]{1,0:T(8,128)(2,1)S(1)} %bitcast.42, bf16[192,2560]{1,0:T(8,128)(2,1)} %collective-permute-done.2.refs_3_.refs_7_, bf16[192,1024]{1,0:T(8,128)(2,1)S(1)} %copy-done.15, ...), custom_call_target="tpu_custom_call" | custom-call | flops 4026531840 | bytes 10747904 | tf_op jit(solution)/shard_map/pallas_call | solution.py:220
  177.4 8.7 %shard_map.114 = bf16[1024,2560]{1,0:T(8,128)(2,1)} custom-call(bf16[192,1024]{1,0:T(8,128)(2,1)S(1)} %copy-done.11, bf16[192,1024]{1,0:T(8,128)(2,1)S(1)} %copy-done.12, bf16[192,1024]{1,0:T(8,128)(2,1)S(1)} %copy-done.13, bf16[192,1024]{1,0:T(8,128)(2,1)S(1)} %copy-done.14, bf16[192,2560]{1,0:T(8,128)(2,1)} %collective-permute-done.5.refs_0_.refs_4_, ...), custom_call_target="tpu_custom_call" | custom-call | flops 4026531840 | bytes 10747904 | tf_op jit(solution)/shard_map/pallas_call | solution.py:220
  186.1 5.4 %all-to-all-done.3 = bf16[8,24,2816]{2,1,0:T(8,128)(2,1)} async-done(((bf16[8,24,2816]{2,1,0:T(8,128)(2,1)}), bf16[8,24,2816]{2,1,0:T(8,128)(2,1)}, u32[]{:S(2)}, u32[]{:S(2)}) %all-to-all-start.3) | async-done | bytes 1081376 | tf_op jit(solution)/shard_map/all_to_all | solution.py:268
  191.5 0.8 slice_bitcast_fusion.1
  192.4 1.3 slice.20
  193.6 0.4 fusion.2
  194.0 0.6 add_bitcast_fusion
  194.7 1.2 fusion.1
  (60 shorter events, 0.3 us)
Async XLA Ops:
  0.6 3.1 %copy-start = (bf16[128,2560]{1,0:T(8,128)(2,1)S(1)}, bf16[128,2560]{1,0:T(8,128)(2,1)}, u32[]{:S(2)}) copy-start(bf16[128,2560]{1,0:T(8,128)(2,1)} %param.7) | copy-start | bytes 1966084
  0.6 11.7 %copy-start.23 = (s32[128,1]{0,1:T(1,128)S(1)}, s32[128,1]{0,1:T(1,128)}, u32[]{:S(2)}) copy-start(s32[128,1]{0,1:T(1,128)} %param.8) | copy-start | bytes 1540
  0.7 11.7 %copy-start.22 = (bf16[2560,8]{0,1:T(8,128)(2,1)S(1)}, bf16[2560,8]{0,1:T(8,128)(2,1)}, u32[]{:S(2)}) copy-start(bf16[2560,8]{0,1:T(8,128)(2,1)} %param.10) | copy-start | bytes 122884
  3.7 8.9 %copy-start.19 = (bf16[128,2560]{1,0:T(8,128)(2,1)S(1)}, bf16[128,2560]{1,0:T(8,128)(2,1)}, u32[]{:S(2)}) copy-start(bf16[128,2560]{1,0:T(8,128)(2,1)} %param.13) | copy-start | bytes 1966084
  5.1 31.6 %all-to-all-start = ((bf16[8,24,2560]{2,1,0:T(8,128)(2,1)}), bf16[8,24,2560]{2,1,0:T(8,128)(2,1)S(1)}, u32[]{:S(2)}, u32[]{:S(2)}) async-start(bf16[8,24,2560]{2,1,0:T(8,128)(2,1)} %bitcast.2), calls=%async_computation | async-start | bytes 1966080 | tf_op jit(solution)/shard_map/all_to_all | solution.py:268
  36.7 30.9 %copy-start.1 = (bf16[8,24,2560]{2,1,0:T(8,128)(2,1)}, bf16[8,24,2560]{2,1,0:T(8,128)(2,1)S(1)}, u32[]{:S(2)}) copy-start(bf16[8,24,2560]{2,1,0:T(8,128)(2,1)S(1)} %all-to-all-done) | copy-start | bytes 2949124
  36.7 28.1 %all-to-all-start.1 = ((bf16[8,24,2560]{2,1,0:T(8,128)(2,1)}), bf16[8,24,2560]{2,1,0:T(8,128)(2,1)S(1)}, u32[]{:S(2)}, u32[]{:S(2)}) async-start(bf16[8,24,2560]{2,1,0:T(8,128)(2,1)} %bitcast.54), calls=%async_computation.1 | async-start | bytes 1966080 | tf_op jit(solution)/shard_map/all_to_all | solution.py:268
  40.3 23.5 %collective-permute-start = (bf16[192,2560]{1,0:T(8,128)(2,1)S(1)}, bf16[192,2560]{1,0:T(8,128)(2,1)}, u32[]{:S(2)}, u32[]{:S(2)}) collective-permute-start(bf16[192,2560]{1,0:T(8,128)(2,1)S(1)} %bitcast.38), channel_id=1, source_target_pairs={{0,2},{1,3},{2,0},{3,1},{4,6},{5,7},{6,4},{7,5},{8,10},{9,11},{10,... | collective-permute-start | bytes 2949128 | tf_op jit(solution)/shard_map/ppermute | solution.py:236
  41.9 24.5 %collective-permute-start.2 = (bf16[192,2560]{1,0:T(8,128)(2,1)S(1)}, bf16[192,2560]{1,0:T(8,128)(2,1)}, u32[]{:S(2)}, u32[]{:S(2)}) collective-permute-start(bf16[192,2560]{1,0:T(8,128)(2,1)S(1)} %bitcast.39), channel_id=1, source_target_pairs={{0,1},{1,0},{2,3},{3,2},{4,5},{5,4},{6,7},{7,6},{8,9},{9,8},{10,11... | collective-permute-start | bytes 2949128 | tf_op jit(solution)/shard_map/ppermute | solution.py:236
  64.8 51.2 %copy-start.3 = (bf16[8,24,2560]{2,1,0:T(8,128)(2,1)}, bf16[8,24,2560]{2,1,0:T(8,128)(2,1)S(1)}, u32[]{:S(2)}) copy-start(bf16[8,24,2560]{2,1,0:T(8,128)(2,1)S(1)} %all-to-all-done.1) | copy-start | bytes 2949124
  64.8 2.8 %collective-permute-start.1 = (bf16[192,2560]{1,0:T(8,128)(2,1)}, bf16[192,2560]{1,0:T(8,128)(2,1)S(1)}, u32[]{:S(2)}, u32[]{:S(2)}) collective-permute-start(bf16[192,2560]{1,0:T(8,128)(2,1)} %collective-permute-done.refs_0_.refs_6_), channel_id=1, source_target_pairs={{0,1},{1,0},{2,3},{3,2},{4,5},{5,4},{6,7},{7,6},{8,9},{9,8},{10,11... | collective-permute-start | bytes 2949128 | tf_op jit(solution)/shard_map/ppermute | solution.py:236
  64.8 24.3 %collective-permute-start.5 = (bf16[192,2560]{1,0:T(8,128)(2,1)S(1)}, bf16[192,2560]{1,0:T(8,128)(2,1)}, u32[]{:S(2)}, u32[]{:S(2)}) collective-permute-start(bf16[192,2560]{1,0:T(8,128)(2,1)S(1)} %bitcast.43), channel_id=1, source_target_pairs={{0,2},{1,3},{2,0},{3,1},{4,6},{5,7},{6,4},{7,5},{8,10},{9,11},{10,... | collective-permute-start | bytes 2949128 | tf_op jit(solution)/shard_map/ppermute | solution.py:236
  67.6 0.9 copy-start.5
  83.7 5.5 %collective-permute-start.4 = (bf16[192,2560]{1,0:T(8,128)(2,1)}, bf16[192,2560]{1,0:T(8,128)(2,1)S(1)}, u32[]{:S(2)}, u32[]{:S(2)}) collective-permute-start(bf16[192,2560]{1,0:T(8,128)(2,1)} %get-tuple-element.56), channel_id=1, source_target_pairs={{0,1},{1,0},{2,3},{3,2},{4,5},{5,4},{6,7},{7,6},{8,9},{9,8},{10,11... | collective-permute-start | bytes 2949128 | tf_op jit(solution)/shard_map/ppermute | solution.py:236
  89.1 4.2 %collective-permute-start.7 = (bf16[192,2560]{1,0:T(8,128)(2,1)}, bf16[192,2560]{1,0:T(8,128)(2,1)S(1)}, u32[]{:S(2)}, u32[]{:S(2)}) collective-permute-start(bf16[192,2560]{1,0:T(8,128)(2,1)} %collective-permute-done.5.refs_0_.refs_4_), channel_id=1, source_target_pairs={{0,1},{1,0},{2,3},{3,2},{4,5},{5,4},{6,7},{7,6},{8,9},{9,8},{10,11... | collective-permute-start | bytes 2949128 | tf_op jit(solution)/shard_map/ppermute | solution.py:236
  91.5 24.5 %collective-permute-start.6 = (bf16[192,2560]{1,0:T(8,128)(2,1)}, bf16[192,2560]{1,0:T(8,128)(2,1)}, u32[]{:S(2)}, u32[]{:S(2)}) collective-permute-start(bf16[192,2560]{1,0:T(8,128)(2,1)} %add_convert_fusion.4), channel_id=1, source_target_pairs={{0,2},{1,3},{2,0},{3,1},{4,6},{5,7},{6,4},{7,5},{8,10},{9,11},{10,... | collective-permute-start | bytes 2949128 | tf_op jit(solution)/shard_map/ppermute | solution.py:236
  93.0 23.5 %collective-permute-start.3 = (bf16[192,2560]{1,0:T(8,128)(2,1)}, bf16[192,2560]{1,0:T(8,128)(2,1)}, u32[]{:S(2)}, u32[]{:S(2)}) collective-permute-start(bf16[192,2560]{1,0:T(8,128)(2,1)} %get-tuple-element.54), channel_id=1, source_target_pairs={{0,1},{1,0},{2,3},{3,2},{4,5},{5,4},{6,7},{7,6},{8,9},{9,8},{10,11... | collective-permute-start | bytes 2949128 | tf_op jit(solution)/shard_map/ppermute | solution.py:236
  93.3 1.0 copy-start.7
  94.3 22.2 %copy-start.20 = (bf16[192,2560]{1,0:T(8,128)(2,1)S(1)}, bf16[192,2560]{1,0:T(8,128)(2,1)}, u32[]{:S(2)}) copy-start(bf16[192,2560]{1,0:T(8,128)(2,1)} %get-tuple-element.53) | copy-start | bytes 2949124
  116.0 8.0 %collective-permute-start.8 = (bf16[192,2560]{1,0:T(8,128)(2,1)}, bf16[192,2560]{1,0:T(8,128)(2,1)}, u32[]{:S(2)}, u32[]{:S(2)}) collective-permute-start(bf16[192,2560]{1,0:T(8,128)(2,1)} %get-tuple-element.69), channel_id=1, source_target_pairs={{0,1},{1,0},{2,3},{3,2},{4,5},{5,4},{6,7},{7,6},{8,9},{9,8},{10,11... | collective-permute-start | bytes 2949128 | tf_op jit(solution)/shard_map/ppermute | solution.py:236
  116.0 11.3 %collective-permute-start.9 = (bf16[192,2560]{1,0:T(8,128)(2,1)S(1)}, bf16[192,2560]{1,0:T(8,128)(2,1)S(1)}, u32[]{:S(2)}, u32[]{:S(2)}) collective-permute-start(bf16[192,2560]{1,0:T(8,128)(2,1)S(1)} %bitcast.44), channel_id=1, source_target_pairs={{0,1},{1,0},{2,3},{3,2},{4,5},{5,4},{6,7},{7,6},{8,9},{9,8},{10,11... | collective-permute-start | bytes 2949128 | tf_op jit(solution)/shard_map/ppermute | solution.py:236
  119.3 37.2 %all-to-all-start.2 = ((bf16[8,24,2560]{2,1,0:T(8,128)(2,1)}), bf16[8,24,2560]{2,1,0:T(8,128)(2,1)}, u32[]{:S(2)}, u32[]{:S(2)}) async-start(bf16[8,24,2560]{2,1,0:T(8,128)(2,1)} %bitcast.55), calls=%async_computation.2 | async-start | bytes 1966080 | tf_op jit(solution)/shard_map/all_to_all | solution.py:268
  125.7 23.5 %collective-permute-start.10 = (bf16[192,2560]{1,0:T(8,128)(2,1)S(1)}, bf16[192,2560]{1,0:T(8,128)(2,1)S(1)}, u32[]{:S(2)}, u32[]{:S(2)}) collective-permute-start(bf16[192,2560]{1,0:T(8,128)(2,1)S(1)} %add_convert_fusion.2), channel_id=1, source_target_pairs={{0,2},{1,3},{2,0},{3,1},{4,6},{5,7},{6,4},{7,5},{8,10},{9,11},{10,... | collective-permute-start | bytes 2949128 | tf_op jit(solution)/shard_map/ppermute | solution.py:236
  127.3 1.0 copy-start.9
  128.3 21.9 %copy-start.24 = (f32[1,2560]{1,0:T(1,128)S(1)}, f32[1,2560]{1,0:T(1,128)}, u32[]{:S(2)}) copy-start(f32[1,2560]{1,0:T(1,128)} %get-tuple-element.82) | copy-start | bytes 30724
  149.2 1.0 copy-start.21
  150.2 6.5 %collective-permute-start.11 = (bf16[192,2560]{1,0:T(8,128)(2,1)}, bf16[192,2560]{1,0:T(8,128)(2,1)S(1)}, u32[]{:S(2)}, u32[]{:S(2)}) collective-permute-start(bf16[192,2560]{1,0:T(8,128)(2,1)} %get-tuple-element.79), channel_id=1, source_target_pairs={{0,1},{1,0},{2,3},{3,2},{4,5},{5,4},{6,7},{7,6},{8,9},{9,8},{10,11... | collective-permute-start | bytes 2949128 | tf_op jit(solution)/shard_map/ppermute | solution.py:236
  150.9 1.9 collective-permute-start.12
  152.8 3.7 %collective-permute-start.13 = (f32[1,2560]{1,0:T(1,128)S(1)}, f32[1,2560]{1,0:T(1,128)S(1)}, u32[]{:S(2)}, u32[]{:S(2)}) collective-permute-start(f32[1,2560]{1,0:T(1,128)S(1)} %add.72), channel_id=1, source_target_pairs={{0,2},{1,3},{2,0},{3,1},{4,6},{5,7},{6,4},{7,5},{8,10},{9,11},{10,... | collective-permute-start | bytes 30728 | tf_op jit(solution)/shard_map/ppermute | solution.py:236
  159.6 8.8 %copy-start.2 = (bf16[8,24,2560]{2,1,0:T(8,128)(2,1)S(1)}, bf16[8,24,2560]{2,1,0:T(8,128)(2,1)}, u32[]{:S(2)}) copy-start(bf16[8,24,2560]{2,1,0:T(8,128)(2,1)} %copy-done.1) | copy-start | bytes 2949124
  159.6 8.8 %copy-start.6 = (bf16[192,2560]{1,0:T(8,128)(2,1)S(1)}, bf16[192,2560]{1,0:T(8,128)(2,1)}, u32[]{:S(2)}) copy-start(bf16[192,2560]{1,0:T(8,128)(2,1)} %copy-done.5) | copy-start | bytes 2949124
  159.6 8.8 %copy-start.15 = (bf16[192,1024]{1,0:T(8,128)(2,1)S(1)}, bf16[192,1024]{1,0:T(8,128)(2,1)}, u32[]{:S(2)}) copy-start(bf16[192,1024]{1,0:T(8,128)(2,1)} %get-tuple-element.89.refs_4_) | copy-start | bytes 1179652
  159.6 8.8 %copy-start.16 = (bf16[192,1024]{1,0:T(8,128)(2,1)S(1)}, bf16[192,1024]{1,0:T(8,128)(2,1)}, u32[]{:S(2)}) copy-start(bf16[192,1024]{1,0:T(8,128)(2,1)} %get-tuple-element.90.refs_5_) | copy-start | bytes 1179652
  159.6 31.9 %all-to-all-start.3 = ((bf16[8,24,2816]{2,1,0:T(8,128)(2,1)}), bf16[8,24,2816]{2,1,0:T(8,128)(2,1)}, u32[]{:S(2)}, u32[]{:S(2)}) async-start(bf16[8,24,2816]{2,1,0:T(8,128)(2,1)} %pad_maximum_fusion), calls=%async_computation.3 | async-start | bytes 2162688 | tf_op jit(solution)/shard_map/all_to_all | solution.py:268
  165.6 2.9 %copy-start.17 = (bf16[192,1024]{1,0:T(8,128)(2,1)S(1)}, bf16[192,1024]{1,0:T(8,128)(2,1)}, u32[]{:S(2)}) copy-start(bf16[192,1024]{1,0:T(8,128)(2,1)} %get-tuple-element.91.refs_6_) | copy-start | bytes 1179652
  165.6 2.9 %copy-start.18 = (bf16[192,1024]{1,0:T(8,128)(2,1)S(1)}, bf16[192,1024]{1,0:T(8,128)(2,1)}, u32[]{:S(2)}) copy-start(bf16[192,1024]{1,0:T(8,128)(2,1)} %get-tuple-element.92.refs_7_) | copy-start | bytes 1179652
  168.4 8.9 %copy-start.4 = (bf16[8,24,2560]{2,1,0:T(8,128)(2,1)S(1)}, bf16[8,24,2560]{2,1,0:T(8,128)(2,1)}, u32[]{:S(2)}) copy-start(bf16[8,24,2560]{2,1,0:T(8,128)(2,1)} %copy-done.3) | copy-start | bytes 2949124
  168.4 8.9 %copy-start.8 = (bf16[192,2560]{1,0:T(8,128)(2,1)S(1)}, bf16[192,2560]{1,0:T(8,128)(2,1)}, u32[]{:S(2)}) copy-start(bf16[192,2560]{1,0:T(8,128)(2,1)} %copy-done.7) | copy-start | bytes 2949124
  168.4 8.9 %copy-start.10 = (bf16[192,2560]{1,0:T(8,128)(2,1)S(1)}, bf16[192,2560]{1,0:T(8,128)(2,1)}, u32[]{:S(2)}) copy-start(bf16[192,2560]{1,0:T(8,128)(2,1)} %copy-done.9) | copy-start | bytes 2949124
  168.5 8.9 %copy-start.11 = (bf16[192,1024]{1,0:T(8,128)(2,1)S(1)}, bf16[192,1024]{1,0:T(8,128)(2,1)}, u32[]{:S(2)}) copy-start(bf16[192,1024]{1,0:T(8,128)(2,1)} %get-tuple-element.93.refs_4_.refs_0_) | copy-start | bytes 1179652
  168.5 8.9 %copy-start.12 = (bf16[192,1024]{1,0:T(8,128)(2,1)S(1)}, bf16[192,1024]{1,0:T(8,128)(2,1)}, u32[]{:S(2)}) copy-start(bf16[192,1024]{1,0:T(8,128)(2,1)} %get-tuple-element.94.refs_5_.refs_1_) | copy-start | bytes 1179652
  168.5 8.9 %copy-start.13 = (bf16[192,1024]{1,0:T(8,128)(2,1)S(1)}, bf16[192,1024]{1,0:T(8,128)(2,1)}, u32[]{:S(2)}) copy-start(bf16[192,1024]{1,0:T(8,128)(2,1)} %get-tuple-element.95.refs_4_.refs_2_) | copy-start | bytes 1179652
  168.5 8.9 %copy-start.14 = (bf16[192,1024]{1,0:T(8,128)(2,1)S(1)}, bf16[192,1024]{1,0:T(8,128)(2,1)}, u32[]{:S(2)}) copy-start(bf16[192,1024]{1,0:T(8,128)(2,1)} %get-tuple-element.96.refs_5_.refs_3_) | copy-start | bytes 1179652
where the time goes:
time: 197 us; the launch traced here: 196 us
  waiting for transfers between devices  76.2 us (39%)
  Pallas kernels  60 us (30%)
  starting transfers between devices  30.8 us (16%)
  other arithmetic  13.5 us (7%)
  matrix products  7.48 us (4%)
  local copies, waits for them, and re-layouts  6.38 us (3%)
    ppermute x14, waiting for transfers between devices, cross(): return lax.ppermute(x, 'tensor', [(i, i ^ bit) for i in range(n_tensor)])  47.1 us
    all_to_all x4, waiting for transfers between devices, swap(): return lax.all_to_all(x, 'expert', split_axis=0, concat_axis=0, tiled=True)  29 us
    pallas_call x2, Pallas kernels, backward(): call(functools.partial(backward_kernel, n, steps, steps + wides - 1, tile...  27.3 us
    all_to_all x4, starting transfers between devices, swap(): return lax.all_to_all(x, 'expert', split_axis=0, concat_axis=0, tiled=True)  21.5 us
    pallas_call x2, Pallas kernels, gradient(): call(functools.partial(gradient_kernel, len(lefts)), height // tile, [pl....  17.6 us
    pallas_call x1, Pallas kernels, forward(): call(functools.partial(forward_kernel, n, steps, tile), steps + wides, [w...  15.1 us
    ppermute x14, starting transfers between devices, cross(): return lax.ppermute(x, 'tensor', [(i, i ^ bit) for i in range(n_tensor)])  9.32 us
    convert_element_type x4, other arithmetic, added(): return (a.astype(jnp.float32) + b.astype(jnp.float32)).astype(jnp.bfloat16)  8.77 us
  transfers between devices with their start and end apart: 18, of which 10 were waited for; matrix products, arithmetic and copies ran while one was open for 7% of the time, Pallas kernels for 31%

commit v1 on v0

--- a/solution.py
+++ b/solution.py
@@ -243,6 +243,15 @@
             bit *= 2
         return held
 
+    def sum_low_after(terms, earlier):
+        while len(terms) > 1:
+            bit = len(terms) // 2
+            came = [cross(b, bit) for b in terms[bit:]]
+            if bit == 1:
+                came = [after(c, earlier) for c in came]
+            terms = [added(a, c) for a, c in zip(terms[:bit], came)]
+        return terms[0]
+
     def sum_low(terms):
         while len(terms) > 1:
             bit = len(terms) // 2
@@ -299,7 +308,7 @@
         out_far = after(out_far, *far_term)
         out_sum = added(out_near, out_far)
         out_home = exchange(out_sum)
-        back_far_sum = sum_low([after(x, out_far) for x in far_term])
+        back_far_sum = sum_low_after(far_term, out_far)
         back_far = cross(back_far_sum, top)
 
         near = [after(x, out_sum, back_far_sum) for x in gather_low(cot_near)]
@@ -334,7 +343,7 @@
         back_sum = back_sum.reshape(experts, most, width)
         beside = jnp.broadcast_to(beside, (experts, most, 2 * lanes))
         came = swap(jnp.concatenate([back_sum, beside], axis=2))
-        back_home = came[:, :, :width].reshape(slots, width)
+        back_home = came.reshape(slots, width + 2 * lanes)
         high, rest = (
             came[:, :, k : k + lanes].reshape(experts, most * lanes)[:, :width].astype(jnp.float32)
             for k in (width, width + lanes)
@@ -342,7 +351,7 @@
         router_grad = (high + rest).T
 
         out_rows = dot(placing, after(out_home, back_sum), jnp.bfloat16, ((0,), (0,)))
-        cot_rows = dot(placing, back_home, jnp.bfloat16, ((0,), (0,)))
+        cot_rows = dot(placing, back_home, jnp.bfloat16, ((0,), (0,)))[:, :width]
         out_wide = out_rows.astype(jnp.float32)
         mixed = (gate[:, None] * out_wide).astype(jnp.bfloat16)
         own_slope = jnp.sum(out_grad.astype(jnp.float32) * out_wide, axis=1) * gate * (1.0 - gate)

time: 197 us -> 196 us (level)
  no operation moved by 1% of the time
where the time goes in v1:
time: 196 us; the launch traced here: 195 us
  waiting for transfers between devices  75.3 us (38%)
  Pallas kernels  60 us (31%)
  starting transfers between devices  30.8 us (16%)
  other arithmetic  13.5 us (7%)
  matrix products  8.74 us (4%)
  local copies, waits for them, and re-layouts  5.1 us (3%)
    ppermute x14, waiting for transfers between devices, cross(): return lax.ppermute(x, 'tensor', [(i, i ^ bit) for i in range(n_tensor)])  46.3 us
    all_to_all x4, waiting for transfers between devices, swap(): return lax.all_to_all(x, 'expert', split_axis=0, concat_axis=0, tiled=True)  29 us
    pallas_call x2, Pallas kernels, backward(): call(functools.partial(backward_kernel, n, steps, steps + wides - 1, tile...  27.3 us
    all_to_all x4, starting transfers between devices, swap(): return lax.all_to_all(x, 'expert', split_axis=0, concat_axis=0, tiled=True)  21.5 us
    pallas_call x2, Pallas kernels, gradient(): call(functools.partial(gradient_kernel, len(lefts)), height // tile, [pl....  17.6 us
    pallas_call x1, Pallas kernels, forward(): call(functools.partial(forward_kernel, n, steps, tile), steps + wides, [w...  15.1 us
    ppermute x14, starting transfers between devices, cross(): return lax.ppermute(x, 'tensor', [(i, i ^ bit) for i in range(n_tensor)])  9.37 us
    convert_element_type x4, other arithmetic, added(): return (a.astype(jnp.float32) + b.astype(jnp.float32)).astype(jnp.bfloat16)  8.77 us
  transfers between devices with their start and end apart: 18, of which 10 were waited for; matrix products, arithmetic and copies ran while one was open for 7% of the time, Pallas kernels for 31%

profile of v1, /device:TPU:0, one launch (start us, length us, event | category | flops | bytes accessed | tf_op | source)
XLA Modules:
  0.0 195.1 jit_solution(17349021636249647211)
XLA Ops:
  0.6 0.0 copy-start
  0.6 0.0 copy-start.24
  1.4 0.7 fusion.13
  2.0 0.1 copy.12
  2.1 0.2 reduce_window_sum.11
  2.4 0.7 select_reduce_fusion
  3.1 0.7 compare_select_fusion
  3.7 1.4 convolution_convert_fusion.1
  5.1 7.3 %all-to-all-start = ((bf16[8,24,2560]{2,1,0:T(8,128)(2,1)}), bf16[8,24,2560]{2,1,0:T(8,128)(2,1)S(1)}, u32[]{:S(2)}, u32[]{:S(2)}) async-start(bf16[8,24,2560]{2,1,0:T(8,128)(2,1)} %bitcast.2), calls=%async_computation | async-start | bytes 1966080 | tf_op jit(solution)/shard_map/all_to_all | solution.py:277
  12.3 0.3 fusion.5
  12.6 1.5 convolution_convert_fusion
  14.1 22.6 %all-to-all-done = bf16[8,24,2560]{2,1,0:T(8,128)(2,1)S(1)} async-done(((bf16[8,24,2560]{2,1,0:T(8,128)(2,1)}), bf16[8,24,2560]{2,1,0:T(8,128)(2,1)S(1)}, u32[]{:S(2)}, u32[]{:S(2)}) %all-to-all-start) | async-done | bytes 983072 | tf_op jit(solution)/shard_map/all_to_all | solution.py:277
  36.7 3.6 %all-to-all-start.1 = ((bf16[8,24,2560]{2,1,0:T(8,128)(2,1)}), bf16[8,24,2560]{2,1,0:T(8,128)(2,1)S(1)}, u32[]{:S(2)}, u32[]{:S(2)}) async-start(bf16[8,24,2560]{2,1,0:T(8,128)(2,1)} %bitcast.53), calls=%async_computation.1 | async-start | bytes 1966080 | tf_op jit(solution)/shard_map/all_to_all | solution.py:277
  40.3 1.6 collective-permute-start
  41.9 0.0 collective-permute-start.2
  41.9 21.9 %collective-permute-done.refs_0_.refs_6_ = bf16[192,2560]{1,0:T(8,128)(2,1)} collective-permute-done((bf16[192,2560]{1,0:T(8,128)(2,1)S(1)}, bf16[192,2560]{1,0:T(8,128)(2,1)}, u32[]{:S(2)}, u32[]{:S(2)}) %collective-permute-start) | collective-permute-done | bytes 983072 | tf_op jit(solution)/shard_map/ppermute | solution.py:236
  63.8 1.0 all-to-all-done.1
  64.8 0.0 collective-permute-start.1
  64.8 1.5 collective-permute-start.5
  66.4 0.0 collective-permute-done.2.refs_3_.refs_7_
  66.4 1.3 collective-permute-done.1.refs_1_.refs_7_
  67.6 0.9 copy-done.5
  68.6 15.1 %shard_map.110 = (f32[192,1024]{1,0:T(8,128)}, f32[192,1024]{1,0:T(8,128)}, f32[192,1024]{1,0:T(8,128)}, f32[192,1024]{1,0:T(8,128)}, bf16[192,1024]{1,0:T(8,128...) custom-call(bf16[192,2560]{1,0:T(8,128)(2,1)} %collective-permute-do, ...), custom_call_target="tpu_custom_call" | custom-call | flops 1 | bytes 1 | tf_op jit(solution)/shard_map/pallas_call | solution.py:157
  83.7 0.2 collective-permute-start.4
  83.9 5.2 %collective-permute-done.5.refs_0_.refs_4_ = bf16[192,2560]{1,0:T(8,128)(2,1)} collective-permute-done((bf16[192,2560]{1,0:T(8,128)(2,1)S(1)}, bf16[192,2560]{1,0:T(8,128)(2,1)}, u32[]{:S(2)}, u32[]{:S(2)}) %collective-permute-start.5) | collective-permute-done | bytes 983072 | tf_op jit(solution)/shard_map/ppermute | solution.py:236
  89.1 0.0 collective-permute-start.7
  89.1 0.0 collective-permute-done.4
  89.1 2.4 %add_convert_fusion.4 = bf16[192,2560]{1,0:T(8,128)(2,1)} fusion(bf16[192,2560]{1,0:T(8,128)(2,1)S(1)} %collective-permute-done.4, bf16[192,2560]{1,0:T(8,128)(2,1)} %get-tuple-element.54), kind=kLoop, calls=%fused_computation.11 | loop fusion | flops 1966080 | bytes 2949120 | tf_op jit(solution)/shard_map/convert_element_type | solution.py:24
  91.5 1.5 collective-permute-start.6
  93.0 0.2 collective-permute-start.3
  93.3 0.0 collective-permute-done.7.refs_1_.refs_5_
  93.3 0.7 broadcast_in_dim.15.refs_10_
  94.0 0.3 copy-done.7
  94.3 13.7 %shard_map.111 = (bf16[192,1024]{1,0:T(8,128)(2,1)}, bf16[192,1024]{1,0:T(8,128)(2,1)}, bf16[192,2560]{1,0:T(8,128)(2,1)}, bf16[192,2560]{1,0:T(8,128)(2,1)}, f32[1,2560]{1,0:T(1,128)}) custom-call(bf16[192,2560]{1,0:T(8,128)(2,1)} %collective-permute-done.5.refs_0_.refs_4_, bf16[192,2560]{1,0:T(8,128)(2,1)} %copy-done.7, ...), custom_call_target="tpu_custom_call" | custom-call | flops 1 | bytes 1 | tf_op jit(solution)/shard_map/pallas_call | solution.py:183
  108.0 0.3 collective-permute-start.8
  108.3 0.2 collective-permute-start.9
  108.5 7.4 %collective-permute-done.6 = bf16[192,2560]{1,0:T(8,128)(2,1)} collective-permute-done((bf16[192,2560]{1,0:T(8,128)(2,1)}, bf16[192,2560]{1,0:T(8,128)(2,1)}, u32[]{:S(2)}, u32[]{:S(2)}) %collective-permute-start.6) | collective-permute-done | bytes 983072 | tf_op jit(solution)/shard_map/ppermute | solution.py:236
  116.0 2.8 %add_convert_fusion.3 = bf16[192,2560]{1,0:T(8,128)(2,1)} fusion(bf16[192,2560]{1,0:T(8,128)(2,1)} %collective-permute-done.6, bf16[192,2560]{1,0:T(8,128)(2,1)} %collective-permute-done.3, bf16[192,2560]{1,0:T(8,128)(2,1)S(1)} %copy-done.20), kind=kLoop, calls=%fused_computation.10 | loop fusion | flops 3932160 | bytes 3932160 | tf_op jit(solution)/shard_map/convert_element_type | solution.py:24
  118.8 4.7 %all-to-all-start.2 = ((bf16[8,24,2560]{2,1,0:T(8,128)(2,1)}), bf16[8,24,2560]{2,1,0:T(8,128)(2,1)}, u32[]{:S(2)}, u32[]{:S(2)}) async-start(bf16[8,24,2560]{2,1,0:T(8,128)(2,1)} %bitcast.54), calls=%async_computation.2 | async-start | bytes 1966080 | tf_op jit(solution)/shard_map/all_to_all | solution.py:277
  123.5 0.0 collective-permute-done.8
  123.5 1.7 add_convert_fusion.2
  125.2 1.6 collective-permute-start.10
  126.8 1.0 copy-done.9
  127.8 13.6 %shard_map.112 = (bf16[192,1024]{1,0:T(8,128)(2,1)}, bf16[192,1024]{1,0:T(8,128)(2,1)}, bf16[192,2560]{1,0:T(8,128)(2,1)}, bf16[192,2560]{1,0:T(8,128)(2,1)}, f32[1,2560]{1,0:T(1,128)}) custom-call(bf16[192,2560]{1,0:T(8,128)(2,1)} %bitcast.45, bf16[192,2560]{1,0:T(8,128)(2,1)} %copy-done.9, f32[192,1024]{1,0:T(8,128)} %get-tuple-element.70.refs_2_, ...), custom_call_target="tpu_custom_call" | custom-call | flops 1 | bytes 1 | tf_op jit(solution)/shard_map/pallas_call | solution.py:183
  141.4 7.0 %collective-permute-done.10 = bf16[192,2560]{1,0:T(8,128)(2,1)S(1)} collective-permute-done((bf16[192,2560]{1,0:T(8,128)(2,1)S(1)}, bf16[192,2560]{1,0:T(8,128)(2,1)S(1)}, u32[]{:S(2)}, u32[]{:S(2)}) %collective-permute-start.10) | collective-permute-done | bytes 983072 | tf_op jit(solution)/shard_map/ppermute | solution.py:236
  148.4 1.0 copy-done.21
  149.4 0.7 add.71
  150.1 0.6 collective-permute-start.12
  150.7 1.3 collective-permute-done.12
  152.0 1.6 collective-permute-start.13
  153.6 2.2 %collective-permute-done.13 = f32[1,2560]{1,0:T(1,128)S(1)} collective-permute-done((f32[1,2560]{1,0:T(1,128)S(1)}, f32[1,2560]{1,0:T(1,128)S(1)}, u32[]{:S(2)}, u32[]{:S(2)}) %collective-permute-start.13) | collective-permute-done | bytes 10272 | tf_op jit(solution)/shard_map/ppermute | solution.py:236
  155.8 0.1 pad_reduce_fusion
  155.9 1.9 add_convert_fusion
  157.7 1.1 pad_maximum_fusion
  158.8 6.0 %all-to-all-start.3 = ((bf16[8,24,2816]{2,1,0:T(8,128)(2,1)}), bf16[8,24,2816]{2,1,0:T(8,128)(2,1)}, u32[]{:S(2)}, u32[]{:S(2)}) async-start(bf16[8,24,2816]{2,1,0:T(8,128)(2,1)} %pad_maximum_fusion), calls=%async_computation.3 | async-start | bytes 2162688 | tf_op jit(solution)/shard_map/all_to_all | solution.py:277
  164.8 2.8 %fusion.4 = (f32[128]{0:T(128)S(1)}, bf16[128,2560]{1,0:T(8,128)(2,1)}) fusion(bf16[128,2560]{1,0:T(8,128)(2,1)} %param.13, f32[128]{0:T(128)S(1)} %add_divide_fusion, bf16[192,2560]{1,0:T(8,128)(2,1)} %bitcast.9, s32[128]{0:T(128)S(1)} %compare_select_fusion), kind=kOutput, calls=%fused_computation.16 | convolution fusion | flops 128147328 | bytes 2295296 | tf_op jit(solution)/shard_map/dot_general | solution.py:12
  167.6 0.0 copy-start.11
  167.7 8.9 %shard_map.113 = bf16[2560,1024]{1,0:T(8,128)(2,1)} custom-call(bf16[192,2560]{1,0:T(8,128)(2,1)} %collective-permute-done.refs_0_.refs_6_, bf16[192,2560]{1,0:T(8,128)(2,1)S(1)} %copy-done.6, bf16[192,2560]{1,0:T(8,128)(2,1)S(1)} %bitcast.42, bf16[192,2560]{1,0:T(8,128)(2,1)} %collective-permute-done.2.refs_3_.refs_7_, bf16[192,1024]{1,0:T(8,128)(2,1)S(1)} %copy-done.15, ...), custom_call_target="tpu_custom_call" | custom-call | flops 4026531840 | bytes 10747904 | tf_op jit(solution)/shard_map/pallas_call | solution.py:220
  176.6 8.7 %shard_map.114 = bf16[1024,2560]{1,0:T(8,128)(2,1)} custom-call(bf16[192,1024]{1,0:T(8,128)(2,1)S(1)} %copy-done.11, bf16[192,1024]{1,0:T(8,128)(2,1)S(1)} %copy-done.12, bf16[192,1024]{1,0:T(8,128)(2,1)S(1)} %copy-done.13, bf16[192,1024]{1,0:T(8,128)(2,1)S(1)} %copy-done.14, bf16[192,2560]{1,0:T(8,128)(2,1)} %collective-permute-done.5.refs_0_.refs_4_, ...), custom_call_target="tpu_custom_call" | custom-call | flops 4026531840 | bytes 10747904 | tf_op jit(solution)/shard_map/pallas_call | solution.py:220
  185.3 5.4 %all-to-all-done.3 = bf16[8,24,2816]{2,1,0:T(8,128)(2,1)} async-done(((bf16[8,24,2816]{2,1,0:T(8,128)(2,1)}), bf16[8,24,2816]{2,1,0:T(8,128)(2,1)}, u32[]{:S(2)}, u32[]{:S(2)}) %all-to-all-start.3) | async-done | bytes 1081376 | tf_op jit(solution)/shard_map/all_to_all | solution.py:277
  190.7 0.8 slice_bitcast_fusion.1
  191.6 1.6 fusion.8
  193.2 0.6 add_bitcast_fusion
  193.9 1.2 fusion.1
  (59 shorter events, 0.3 us)
Async XLA Ops:
  0.6 3.1 %copy-start = (bf16[128,2560]{1,0:T(8,128)(2,1)S(1)}, bf16[128,2560]{1,0:T(8,128)(2,1)}, u32[]{:S(2)}) copy-start(bf16[128,2560]{1,0:T(8,128)(2,1)} %param.7) | copy-start | bytes 1966084
  0.6 11.7 %copy-start.24 = (s32[128,1]{0,1:T(1,128)S(1)}, s32[128,1]{0,1:T(1,128)}, u32[]{:S(2)}) copy-start(s32[128,1]{0,1:T(1,128)} %param.8) | copy-start | bytes 1540
  0.7 11.7 %copy-start.22 = (bf16[2560,8]{0,1:T(8,128)(2,1)S(1)}, bf16[2560,8]{0,1:T(8,128)(2,1)}, u32[]{:S(2)}) copy-start(bf16[2560,8]{0,1:T(8,128)(2,1)} %param.10) | copy-start | bytes 122884
  3.7 8.9 %copy-start.19 = (bf16[128,2560]{1,0:T(8,128)(2,1)S(1)}, bf16[128,2560]{1,0:T(8,128)(2,1)}, u32[]{:S(2)}) copy-start(bf16[128,2560]{1,0:T(8,128)(2,1)} %param.13) | copy-start | bytes 1966084
  5.1 31.6 %all-to-all-start = ((bf16[8,24,2560]{2,1,0:T(8,128)(2,1)}), bf16[8,24,2560]{2,1,0:T(8,128)(2,1)S(1)}, u32[]{:S(2)}, u32[]{:S(2)}) async-start(bf16[8,24,2560]{2,1,0:T(8,128)(2,1)} %bitcast.2), calls=%async_computation | async-start | bytes 1966080 | tf_op jit(solution)/shard_map/all_to_all | solution.py:277
  36.7 30.9 %copy-start.1 = (bf16[8,24,2560]{2,1,0:T(8,128)(2,1)}, bf16[8,24,2560]{2,1,0:T(8,128)(2,1)S(1)}, u32[]{:S(2)}) copy-start(bf16[8,24,2560]{2,1,0:T(8,128)(2,1)S(1)} %all-to-all-done) | copy-start | bytes 2949124
  36.7 28.1 %all-to-all-start.1 = ((bf16[8,24,2560]{2,1,0:T(8,128)(2,1)}), bf16[8,24,2560]{2,1,0:T(8,128)(2,1)S(1)}, u32[]{:S(2)}, u32[]{:S(2)}) async-start(bf16[8,24,2560]{2,1,0:T(8,128)(2,1)} %bitcast.53), calls=%async_computation.1 | async-start | bytes 1966080 | tf_op jit(solution)/shard_map/all_to_all | solution.py:277
  40.3 23.5 %collective-permute-start = (bf16[192,2560]{1,0:T(8,128)(2,1)S(1)}, bf16[192,2560]{1,0:T(8,128)(2,1)}, u32[]{:S(2)}, u32[]{:S(2)}) collective-permute-start(bf16[192,2560]{1,0:T(8,128)(2,1)S(1)} %bitcast.38), channel_id=1, source_target_pairs={{0,2},{1,3},{2,0},{3,1},{4,6},{5,7},{6,4},{7,5},{8,10},{9,11},{10,... | collective-permute-start | bytes 2949128 | tf_op jit(solution)/shard_map/ppermute | solution.py:236
  41.9 24.5 %collective-permute-start.2 = (bf16[192,2560]{1,0:T(8,128)(2,1)S(1)}, bf16[192,2560]{1,0:T(8,128)(2,1)}, u32[]{:S(2)}, u32[]{:S(2)}) collective-permute-start(bf16[192,2560]{1,0:T(8,128)(2,1)S(1)} %bitcast.39), channel_id=1, source_target_pairs={{0,1},{1,0},{2,3},{3,2},{4,5},{5,4},{6,7},{7,6},{8,9},{9,8},{10,11... | collective-permute-start | bytes 2949128 | tf_op jit(solution)/shard_map/ppermute | solution.py:236
  64.8 43.5 %copy-start.3 = (bf16[8,24,2560]{2,1,0:T(8,128)(2,1)}, bf16[8,24,2560]{2,1,0:T(8,128)(2,1)S(1)}, u32[]{:S(2)}) copy-start(bf16[8,24,2560]{2,1,0:T(8,128)(2,1)S(1)} %all-to-all-done.1) | copy-start | bytes 2949124
  64.8 2.8 %collective-permute-start.1 = (bf16[192,2560]{1,0:T(8,128)(2,1)}, bf16[192,2560]{1,0:T(8,128)(2,1)S(1)}, u32[]{:S(2)}, u32[]{:S(2)}) collective-permute-start(bf16[192,2560]{1,0:T(8,128)(2,1)} %collective-permute-done.refs_0_.refs_6_), channel_id=1, source_target_pairs={{0,1},{1,0},{2,3},{3,2},{4,5},{5,4},{6,7},{7,6},{8,9},{9,8},{10,11... | collective-permute-start | bytes 2949128 | tf_op jit(solution)/shard_map/ppermute | solution.py:236
  64.8 24.3 %collective-permute-start.5 = (bf16[192,2560]{1,0:T(8,128)(2,1)S(1)}, bf16[192,2560]{1,0:T(8,128)(2,1)}, u32[]{:S(2)}, u32[]{:S(2)}) collective-permute-start(bf16[192,2560]{1,0:T(8,128)(2,1)S(1)} %bitcast.43), channel_id=1, source_target_pairs={{0,2},{1,3},{2,0},{3,1},{4,6},{5,7},{6,4},{7,5},{8,10},{9,11},{10,... | collective-permute-start | bytes 2949128 | tf_op jit(solution)/shard_map/ppermute | solution.py:236
  67.6 0.9 copy-start.5
  83.7 5.4 %collective-permute-start.4 = (bf16[192,2560]{1,0:T(8,128)(2,1)}, bf16[192,2560]{1,0:T(8,128)(2,1)S(1)}, u32[]{:S(2)}, u32[]{:S(2)}) collective-permute-start(bf16[192,2560]{1,0:T(8,128)(2,1)} %get-tuple-element.55), channel_id=1, source_target_pairs={{0,1},{1,0},{2,3},{3,2},{4,5},{5,4},{6,7},{7,6},{8,9},{9,8},{10,11... | collective-permute-start | bytes 2949128 | tf_op jit(solution)/shard_map/ppermute | solution.py:236
  89.1 4.2 %collective-permute-start.7 = (bf16[192,2560]{1,0:T(8,128)(2,1)}, bf16[192,2560]{1,0:T(8,128)(2,1)S(1)}, u32[]{:S(2)}, u32[]{:S(2)}) collective-permute-start(bf16[192,2560]{1,0:T(8,128)(2,1)} %collective-permute-done.5.refs_0_.refs_4_), channel_id=1, source_target_pairs={{0,1},{1,0},{2,3},{3,2},{4,5},{5,4},{6,7},{7,6},{8,9},{9,8},{10,11... | collective-permute-start | bytes 2949128 | tf_op jit(solution)/shard_map/ppermute | solution.py:236
  91.5 24.5 %collective-permute-start.6 = (bf16[192,2560]{1,0:T(8,128)(2,1)}, bf16[192,2560]{1,0:T(8,128)(2,1)}, u32[]{:S(2)}, u32[]{:S(2)}) collective-permute-start(bf16[192,2560]{1,0:T(8,128)(2,1)} %add_convert_fusion.4), channel_id=1, source_target_pairs={{0,2},{1,3},{2,0},{3,1},{4,6},{5,7},{6,4},{7,5},{8,10},{9,11},{10,... | collective-permute-start | bytes 2949128 | tf_op jit(solution)/shard_map/ppermute | solution.py:236
  93.0 23.0 %collective-permute-start.3 = (bf16[192,2560]{1,0:T(8,128)(2,1)}, bf16[192,2560]{1,0:T(8,128)(2,1)}, u32[]{:S(2)}, u32[]{:S(2)}) collective-permute-start(bf16[192,2560]{1,0:T(8,128)(2,1)} %get-tuple-element.53), channel_id=1, source_target_pairs={{0,1},{1,0},{2,3},{3,2},{4,5},{5,4},{6,7},{7,6},{8,9},{9,8},{10,11... | collective-permute-start | bytes 2949128 | tf_op jit(solution)/shard_map/ppermute | solution.py:236
  93.3 1.0 copy-start.7
  94.3 21.7 %copy-start.20 = (bf16[192,2560]{1,0:T(8,128)(2,1)S(1)}, bf16[192,2560]{1,0:T(8,128)(2,1)}, u32[]{:S(2)}) copy-start(bf16[192,2560]{1,0:T(8,128)(2,1)} %get-tuple-element.52) | copy-start | bytes 2949124
  108.0 15.5 %collective-permute-start.8 = (bf16[192,2560]{1,0:T(8,128)(2,1)}, bf16[192,2560]{1,0:T(8,128)(2,1)}, u32[]{:S(2)}, u32[]{:S(2)}) collective-permute-start(bf16[192,2560]{1,0:T(8,128)(2,1)} %get-tuple-element.65), channel_id=1, source_target_pairs={{0,1},{1,0},{2,3},{3,2},{4,5},{5,4},{6,7},{7,6},{8,9},{9,8},{10,11... | collective-permute-start | bytes 2949128 | tf_op jit(solution)/shard_map/ppermute | solution.py:236
  108.3 18.5 %collective-permute-start.9 = (bf16[192,2560]{1,0:T(8,128)(2,1)S(1)}, bf16[192,2560]{1,0:T(8,128)(2,1)S(1)}, u32[]{:S(2)}, u32[]{:S(2)}) collective-permute-start(bf16[192,2560]{1,0:T(8,128)(2,1)S(1)} %bitcast.44), channel_id=1, source_target_pairs={{0,1},{1,0},{2,3},{3,2},{4,5},{5,4},{6,7},{7,6},{8,9},{9,8},{10,11... | collective-permute-start | bytes 2949128 | tf_op jit(solution)/shard_map/ppermute | solution.py:236
  118.8 36.9 %all-to-all-start.2 = ((bf16[8,24,2560]{2,1,0:T(8,128)(2,1)}), bf16[8,24,2560]{2,1,0:T(8,128)(2,1)}, u32[]{:S(2)}, u32[]{:S(2)}) async-start(bf16[8,24,2560]{2,1,0:T(8,128)(2,1)} %bitcast.54), calls=%async_computation.2 | async-start | bytes 1966080 | tf_op jit(solution)/shard_map/all_to_all | solution.py:277
  125.2 23.2 %collective-permute-start.10 = (bf16[192,2560]{1,0:T(8,128)(2,1)S(1)}, bf16[192,2560]{1,0:T(8,128)(2,1)S(1)}, u32[]{:S(2)}, u32[]{:S(2)}) collective-permute-start(bf16[192,2560]{1,0:T(8,128)(2,1)S(1)} %add_convert_fusion.2), channel_id=1, source_target_pairs={{0,2},{1,3},{2,0},{3,1},{4,6},{5,7},{6,4},{7,5},{8,10},{9,11},{10,... | collective-permute-start | bytes 2949128 | tf_op jit(solution)/shard_map/ppermute | solution.py:236
  126.8 1.0 copy-start.9
  127.8 21.6 %copy-start.23 = (f32[1,2560]{1,0:T(1,128)S(1)}, f32[1,2560]{1,0:T(1,128)}, u32[]{:S(2)}) copy-start(f32[1,2560]{1,0:T(1,128)} %get-tuple-element.80) | copy-start | bytes 30724
  148.4 1.0 copy-start.21
  149.4 6.5 %collective-permute-start.11 = (bf16[192,2560]{1,0:T(8,128)(2,1)}, bf16[192,2560]{1,0:T(8,128)(2,1)S(1)}, u32[]{:S(2)}, u32[]{:S(2)}) collective-permute-start(bf16[192,2560]{1,0:T(8,128)(2,1)} %get-tuple-element.77), channel_id=1, source_target_pairs={{0,1},{1,0},{2,3},{3,2},{4,5},{5,4},{6,7},{7,6},{8,9},{9,8},{10,11... | collective-permute-start | bytes 2949128 | tf_op jit(solution)/shard_map/ppermute | solution.py:236
  150.1 1.9 collective-permute-start.12
  152.0 3.7 %collective-permute-start.13 = (f32[1,2560]{1,0:T(1,128)S(1)}, f32[1,2560]{1,0:T(1,128)S(1)}, u32[]{:S(2)}, u32[]{:S(2)}) collective-permute-start(f32[1,2560]{1,0:T(1,128)S(1)} %add.72), channel_id=1, source_target_pairs={{0,2},{1,3},{2,0},{3,1},{4,6},{5,7},{6,4},{7,5},{8,10},{9,11},{10,... | collective-permute-start | bytes 30728 | tf_op jit(solution)/shard_map/ppermute | solution.py:236
  158.8 8.8 %copy-start.2 = (bf16[8,24,2560]{2,1,0:T(8,128)(2,1)S(1)}, bf16[8,24,2560]{2,1,0:T(8,128)(2,1)}, u32[]{:S(2)}) copy-start(bf16[8,24,2560]{2,1,0:T(8,128)(2,1)} %copy-done.1) | copy-start | bytes 2949124
  158.8 8.8 %copy-start.6 = (bf16[192,2560]{1,0:T(8,128)(2,1)S(1)}, bf16[192,2560]{1,0:T(8,128)(2,1)}, u32[]{:S(2)}) copy-start(bf16[192,2560]{1,0:T(8,128)(2,1)} %copy-done.5) | copy-start | bytes 2949124
  158.8 8.8 %copy-start.15 = (bf16[192,1024]{1,0:T(8,128)(2,1)S(1)}, bf16[192,1024]{1,0:T(8,128)(2,1)}, u32[]{:S(2)}) copy-start(bf16[192,1024]{1,0:T(8,128)(2,1)} %get-tuple-element.87.refs_4_) | copy-start | bytes 1179652
  158.8 8.8 %copy-start.16 = (bf16[192,1024]{1,0:T(8,128)(2,1)S(1)}, bf16[192,1024]{1,0:T(8,128)(2,1)}, u32[]{:S(2)}) copy-start(bf16[192,1024]{1,0:T(8,128)(2,1)} %get-tuple-element.88.refs_5_) | copy-start | bytes 1179652
  158.8 31.9 %all-to-all-start.3 = ((bf16[8,24,2816]{2,1,0:T(8,128)(2,1)}), bf16[8,24,2816]{2,1,0:T(8,128)(2,1)}, u32[]{:S(2)}, u32[]{:S(2)}) async-start(bf16[8,24,2816]{2,1,0:T(8,128)(2,1)} %pad_maximum_fusion), calls=%async_computation.3 | async-start | bytes 2162688 | tf_op jit(solution)/shard_map/all_to_all | solution.py:277
  164.7 2.9 %copy-start.17 = (bf16[192,1024]{1,0:T(8,128)(2,1)S(1)}, bf16[192,1024]{1,0:T(8,128)(2,1)}, u32[]{:S(2)}) copy-start(bf16[192,1024]{1,0:T(8,128)(2,1)} %get-tuple-element.89.refs_6_) | copy-start | bytes 1179652
  164.7 2.9 %copy-start.18 = (bf16[192,1024]{1,0:T(8,128)(2,1)S(1)}, bf16[192,1024]{1,0:T(8,128)(2,1)}, u32[]{:S(2)}) copy-start(bf16[192,1024]{1,0:T(8,128)(2,1)} %get-tuple-element.90.refs_7_) | copy-start | bytes 1179652
  167.6 8.9 %copy-start.4 = (bf16[8,24,2560]{2,1,0:T(8,128)(2,1)S(1)}, bf16[8,24,2560]{2,1,0:T(8,128)(2,1)}, u32[]{:S(2)}) copy-start(bf16[8,24,2560]{2,1,0:T(8,128)(2,1)} %copy-done.3) | copy-start | bytes 2949124
  167.6 8.9 %copy-start.8 = (bf16[192,2560]{1,0:T(8,128)(2,1)S(1)}, bf16[192,2560]{1,0:T(8,128)(2,1)}, u32[]{:S(2)}) copy-start(bf16[192,2560]{1,0:T(8,128)(2,1)} %copy-done.7) | copy-start | bytes 2949124
  167.6 8.9 %copy-start.10 = (bf16[192,2560]{1,0:T(8,128)(2,1)S(1)}, bf16[192,2560]{1,0:T(8,128)(2,1)}, u32[]{:S(2)}) copy-start(bf16[192,2560]{1,0:T(8,128)(2,1)} %copy-done.9) | copy-start | bytes 2949124
  167.6 8.9 %copy-start.11 = (bf16[192,1024]{1,0:T(8,128)(2,1)S(1)}, bf16[192,1024]{1,0:T(8,128)(2,1)}, u32[]{:S(2)}) copy-start(bf16[192,1024]{1,0:T(8,128)(2,1)} %get-tuple-element.91.refs_4_.refs_0_) | copy-start | bytes 1179652
  167.7 8.9 %copy-start.12 = (bf16[192,1024]{1,0:T(8,128)(2,1)S(1)}, bf16[192,1024]{1,0:T(8,128)(2,1)}, u32[]{:S(2)}) copy-start(bf16[192,1024]{1,0:T(8,128)(2,1)} %get-tuple-element.92.refs_5_.refs_1_) | copy-start | bytes 1179652
  167.7 8.9 %copy-start.13 = (bf16[192,1024]{1,0:T(8,128)(2,1)S(1)}, bf16[192,1024]{1,0:T(8,128)(2,1)}, u32[]{:S(2)}) copy-start(bf16[192,1024]{1,0:T(8,128)(2,1)} %get-tuple-element.93.refs_4_.refs_2_) | copy-start | bytes 1179652
  167.7 8.9 %copy-start.14 = (bf16[192,1024]{1,0:T(8,128)(2,1)S(1)}, bf16[192,1024]{1,0:T(8,128)(2,1)}, u32[]{:S(2)}) copy-start(bf16[192,1024]{1,0:T(8,128)(2,1)} %get-tuple-element.94.refs_5_.refs_3_) | copy-start | bytes 1179652

commit v2 on v1

--- a/solution.py
+++ b/solution.py
@@ -20,8 +20,8 @@
     return lax.optimization_barrier((x,) + earlier)[0]
 
 
-def added(a, b):
-    return (a.astype(jnp.float32) + b.astype(jnp.float32)).astype(jnp.bfloat16)
+def added(*parts):
+    return sum(part.astype(jnp.float32) for part in parts).astype(jnp.bfloat16)
 
 
 def call(kernel, grid, in_specs, outs, out_specs, scratch=(), flops=1, moved=1, mib=20):
@@ -244,13 +244,24 @@
         return held
 
     def sum_low_after(terms, earlier):
-        while len(terms) > 1:
+        count = terms[0].shape[0] // 2
+        halves = []
+        for k in (0, count):
+            cut = [t[k : k + count] for t in terms]
+            while len(cut) > 1:
+                bit = len(cut) // 2
+                came = [cross(b, bit) for b in cut[bit:]]
+                if bit == 1:
+                    came = [after(c, earlier) for c in came]
+                cut = [added(a, c) for a, c in zip(cut[:bit], came)]
+            halves.append(cut[0])
+        return joined(halves)
+
+    def last_two(terms):
+        while len(terms) > 2:
             bit = len(terms) // 2
-            came = [cross(b, bit) for b in terms[bit:]]
-            if bit == 1:
-                came = [after(c, earlier) for c in came]
-            terms = [added(a, c) for a, c in zip(terms[:bit], came)]
-        return terms[0]
+            terms = [added(a, cross(b, bit)) for a, b in zip(terms[:bit], terms[bit:])]
+        return terms if len(terms) == 1 else [terms[0], cross(terms[1], 1)]
 
     def sum_low(terms):
         while len(terms) > 1:
@@ -277,7 +288,7 @@
             return lax.all_to_all(x, "expert", split_axis=0, concat_axis=0, tiled=True)
 
         def exchange(x):
-            return swap(x.reshape(experts, most, width)).reshape(slots, width)
+            return swap(x.reshape(experts, most, x.shape[1])).reshape(x.shape)
 
         tok_near = exchange(dot(placing, tokens, jnp.bfloat16))
         logits = dot(tokens, router)
@@ -289,9 +300,12 @@
 
         rows = gather_low(after(tok_far, cot_near)) + gather_low(tok_near)
         hidden, active, term = forward(rows, w_up, w_down)
-        out_far_sum, out_near = sum_low(term[:low]), sum_low(term[low:])
+        out_far_sum, out_near = sum_low(term[:low]), last_two(term[low:])
         cot_far = after(cot_far, *term)
-        out_far = cross(after(out_far_sum, cot_far), top)
+        cut = width // 2
+        out_far = after(out_far_sum, cot_far)
+        out_far_left = cross(out_far[:, :cut], top)
+        out_far_right = cross(out_far[:, cut:], top)
 
         column = lax.dynamic_slice_in_dim(router, me, 1, axis=1).T
         column = jnp.broadcast_to(column, (16, width))
@@ -305,11 +319,13 @@
             w_down,
             column,
         )
-        out_far = after(out_far, *far_term)
-        out_sum = added(out_near, out_far)
-        out_home = exchange(out_sum)
-        back_far_sum = sum_low_after(far_term, out_far)
+        out_far_left = after(out_far_left, *far_term)
+        out_home_left = exchange(added(*[x[:, :cut] for x in out_near], out_far_left))
+        back_far_sum = sum_low_after(far_term, out_far_left)
         back_far = cross(back_far_sum, top)
+        out_far_right = after(out_far_right, back_far_sum)
+        out_sum = added(*[x[:, cut:] for x in out_near], out_far_right)
+        out_home_right = exchange(out_sum)
 
         near = [after(x, out_sum, back_far_sum) for x in gather_low(cot_near)]
         near_hidden_cot, near_term, near_column = backward(
@@ -323,7 +339,7 @@
         while bit < n_tensor:
             columns = columns + cross(columns, bit)
             bit *= 2
-        columns = after(columns, out_home)
+        columns = after(columns, out_home_left, out_home_right)
         lanes = -(-width // (most * 128)) * 128
         high = columns.astype(jnp.bfloat16)
         rest = (columns - high.astype(jnp.float32)).astype(jnp.bfloat16)
@@ -335,7 +351,7 @@
             axis=2,
         )
 
-        back_sum = added(back_near, after(back_far, out_home))
+        back_sum = added(back_near, after(back_far, out_home_left, out_home_right))
 
         up_grad = gradient([after(x, back_sum, columns) for x in rows], hidden_cot, 512)[None]
         down_grad = gradient([after(x, back_sum, columns) for x in active], cots, 256)[None]
@@ -350,7 +366,8 @@
         )
         router_grad = (high + rest).T
 
-        out_rows = dot(placing, after(out_home, back_sum), jnp.bfloat16, ((0,), (0,)))
+        out_home = jnp.concatenate([after(out_home_left, back_sum), out_home_right], axis=1)
+        out_rows = dot(placing, out_home, jnp.bfloat16, ((0,), (0,)))
         cot_rows = dot(placing, back_home, jnp.bfloat16, ((0,), (0,)))[:, :width]
         out_wide = out_rows.astype(jnp.float32)
         mixed = (gate[:, None] * out_wide).astype(jnp.bfloat16)

time: 196 us -> 206 us (1.051)
  waiting for transfers between devices: 75.3 us -> 87.7 us
  starting transfers between devices: 30.8 us -> 33.5 us
  other arithmetic: 13.5 us -> 10.9 us
    all_to_all x4 -> x5, waiting for transfers between devices: 29 us -> 42.1 us  [swap(): return lax.all_to_all(x, 'expert', split_axis=0, concat_axis=0, tiled=True)]
    all_to_all x4 -> x5, starting transfers between devices: 21.5 us -> 25.7 us  [swap(): return lax.all_to_all(x, 'expert', split_axis=0, concat_axis=0, tiled=True)]
    convert_element_type x4, other arithmetic: 8.77 us -> 5.16 us  [added(): sum((part.astype(jnp.float32) for part in parts)).astype(jnp.bfloat16)]
    unnamed x53 -> x55, local copies, waits for them, and re-layouts: 4.12 us -> 2.02 us
    ppermute x14 -> x16, starting transfers between devices: 9.37 us -> 7.89 us  [cross(): return lax.ppermute(x, 'tensor', [(i, i ^ bit) for i in range(n_tensor)])]
    ppermute x14 -> x16, waiting for transfers between devices: 46.3 us -> 45.6 us  [cross(): return lax.ppermute(x, 'tensor', [(i, i ^ bit) for i in range(n_tensor)])]
  transfers between devices with their start and end apart: 18 -> 21, of which waited for: 10 -> 13; matrix products, arithmetic and copies ran while one was open for 7% -> 5% of each run, Pallas kernels for 31% -> 29%
where the time goes in v2:
time: 206 us
  waiting for transfers between devices  87.7 us (43%)
  Pallas kernels  59.9 us (29%)
  starting transfers between devices  33.5 us (16%)
  other arithmetic  10.9 us (5%)
  matrix products  7.37 us (4%)
  local copies, waits for them, and re-layouts  4.39 us (2%)
    ppermute x16, waiting for transfers between devices, cross(): return lax.ppermute(x, 'tensor', [(i, i ^ bit) for i in range(n_tensor)])  45.6 us
    all_to_all x5, waiting for transfers between devices, swap(): return lax.all_to_all(x, 'expert', split_axis=0, concat_axis=0, tiled=True)  42.1 us
    pallas_call x2, Pallas kernels, backward(): call(functools.partial(backward_kernel, n, steps, steps + wides - 1, tile...  27.2 us
    all_to_all x5, starting transfers between devices, swap(): return lax.all_to_all(x, 'expert', split_axis=0, concat_axis=0, tiled=True)  25.7 us
    pallas_call x2, Pallas kernels, gradient(): call(functools.partial(gradient_kernel, len(lefts)), height // tile, [pl....  17.6 us
    pallas_call x1, Pallas kernels, forward(): call(functools.partial(forward_kernel, n, steps, tile), steps + wides, [w...  15.2 us
    ppermute x16, starting transfers between devices, cross(): return lax.ppermute(x, 'tensor', [(i, i ^ bit) for i in range(n_tensor)])  7.89 us
    dot_general x6, matrix products, dot(): lax.dot_general(a, b, (dims, ((), ())), preferred_element_type=jnp.float32)  7.37 us
  transfers between devices with their start and end apart: 21, of which 13 were waited for; matrix products, arithmetic and copies ran while one was open for 5% of the time, Pallas kernels for 29%

profile of v2, /device:TPU:0, one launch (start us, length us, event | category | flops | bytes accessed | tf_op | source)
XLA Modules:
  0.0 205.6 jit_solution(14754399183578706413)
XLA Ops:
  0.6 0.0 copy-start
  0.6 0.0 copy-start.24
  1.4 0.7 fusion.16
  2.0 0.1 copy.12
  2.1 0.2 reduce_window_sum.11
  2.4 0.7 select_reduce_fusion
  3.1 0.7 compare_select_fusion
  3.7 1.4 convolution_convert_fusion.1
  5.1 7.3 %all-to-all-start = ((bf16[8,24,2560]{2,1,0:T(8,128)(2,1)}), bf16[8,24,2560]{2,1,0:T(8,128)(2,1)S(1)}, u32[]{:S(2)}, u32[]{:S(2)}) async-start(bf16[8,24,2560]{2,1,0:T(8,128)(2,1)} %bitcast.2), calls=%async_computation | async-start | bytes 1966080 | tf_op jit(solution)/shard_map/all_to_all | solution.py:288
  12.3 0.3 fusion.5
  12.6 1.5 convolution_convert_fusion
  14.1 22.6 %all-to-all-done = bf16[8,24,2560]{2,1,0:T(8,128)(2,1)S(1)} async-done(((bf16[8,24,2560]{2,1,0:T(8,128)(2,1)}), bf16[8,24,2560]{2,1,0:T(8,128)(2,1)S(1)}, u32[]{:S(2)}, u32[]{:S(2)}) %all-to-all-start) | async-done | bytes 983072 | tf_op jit(solution)/shard_map/all_to_all | solution.py:288
  36.7 3.6 %all-to-all-start.1 = ((bf16[8,24,2560]{2,1,0:T(8,128)(2,1)}), bf16[8,24,2560]{2,1,0:T(8,128)(2,1)S(1)}, u32[]{:S(2)}, u32[]{:S(2)}) async-start(bf16[8,24,2560]{2,1,0:T(8,128)(2,1)} %bitcast.55), calls=%async_computation.1 | async-start | bytes 1966080 | tf_op jit(solution)/shard_map/all_to_all | solution.py:288
  40.3 1.6 collective-permute-start
  41.9 21.9 %collective-permute-done.refs_0_.refs_6_ = bf16[192,2560]{1,0:T(8,128)(2,1)} collective-permute-done((bf16[192,2560]{1,0:T(8,128)(2,1)S(1)}, bf16[192,2560]{1,0:T(8,128)(2,1)}, u32[]{:S(2)}, u32[]{:S(2)}) %collective-permute-start) | collective-permute-done | bytes 983072 | tf_op jit(solution)/shard_map/ppermute | solution.py:236
  63.8 1.0 all-to-all-done.1
  64.8 1.5 collective-permute-start.5
  66.4 1.3 collective-permute-done.1.refs_1_.refs_7_
  67.6 0.9 copy-done.5
  68.6 15.2 %shard_map.110 = (f32[192,1024]{1,0:T(8,128)}, f32[192,1024]{1,0:T(8,128)}, f32[192,1024]{1,0:T(8,128)}, f32[192,1024]{1,0:T(8,128)}, bf16[192,1024]{1,0:T(8,128...) custom-call(bf16[192,2560]{1,0:T(8,128)(2,1)} %collective-permute-do, ...), custom_call_target="tpu_custom_call" | custom-call | flops 1 | bytes 1 | tf_op jit(solution)/shard_map/pallas_call | solution.py:157
  83.7 0.2 collective-permute-start.4
  83.9 5.2 %collective-permute-done.5.refs_0_.refs_4_ = bf16[192,2560]{1,0:T(8,128)(2,1)} collective-permute-done((bf16[192,2560]{1,0:T(8,128)(2,1)S(1)}, bf16[192,2560]{1,0:T(8,128)(2,1)}, u32[]{:S(2)}, u32[]{:S(2)}) %collective-permute-start.5) | collective-permute-done | bytes 983072 | tf_op jit(solution)/shard_map/ppermute | solution.py:236
  89.2 1.7 add_convert_fusion.2
  90.9 1.0 collective-permute-done.7.refs_1_.refs_5_
  91.9 0.1 fusion.20
  92.0 1.6 collective-permute-start.6
  93.5 0.6 broadcast_in_dim.15.refs_10_
  94.2 13.6 %shard_map.111 = (bf16[192,1024]{1,0:T(8,128)(2,1)}, bf16[192,1024]{1,0:T(8,128)(2,1)}, bf16[192,2560]{1,0:T(8,128)(2,1)}, bf16[192,2560]{1,0:T(8,128)(2,1)}, f32[1,2560]{1,0:T(1,128)}) custom-call(bf16[192,2560]{1,0:T(8,128)(2,1)} %collective-permute-done.5.refs_0_.refs_4_, bf16[192,2560]{1,0:T(8,128)(2,1)} %copy-done.7, ...), custom_call_target="tpu_custom_call" | custom-call | flops 1 | bytes 1 | tf_op jit(solution)/shard_map/pallas_call | solution.py:183
  107.8 1.4 fusion.19
  109.2 0.1 collective-permute-start.9
  109.3 0.5 collective-permute-start.10
  109.8 0.1 collective-permute-start.3
  109.8 0.5 collective-permute-start.8
  110.4 0.8 collective-permute-done.9
  111.1 0.7 collective-permute-done.10
  111.8 0.2 add_convert_fusion.5
  112.1 1.0 pad_maximum_fusion.1
  113.1 10.3 %collective-permute-done.8 = bf16[192,1280]{1,0:T(8,128)(2,1)S(1)} collective-permute-done((bf16[192,1280]{1,0:T(8,128)(2,1)S(1)}, bf16[192,1280]{1,0:T(8,128)(2,1)S(1)}, u32[]{:S(2)}, u32[]{:S(2)}) %collective-permute-start.8) | collective-permute-done | bytes 491552 | tf_op jit(solution)/shard_map/ppermute | solution.py:236
  123.4 1.4 add_convert_fusion.6
  124.8 4.7 %all-to-all-start.3 = ((bf16[8,24,1280]{2,1,0:T(8,128)(2,1)}), bf16[8,24,1280]{2,1,0:T(8,128)(2,1)}, u32[]{:S(2)}, u32[]{:S(2)}) async-start(bf16[8,24,1280]{2,1,0:T(8,128)(2,1)} %bitcast.10), calls=%async_computation.3 | async-start | bytes 983040 | tf_op jit(solution)/shard_map/all_to_all | solution.py:288
  129.5 0.1 collective-permute-start.11
  129.5 0.6 collective-permute-start.12
  130.1 13.1 %all-to-all-done.3 = bf16[8,24,1280]{2,1,0:T(8,128)(2,1)} async-done(((bf16[8,24,1280]{2,1,0:T(8,128)(2,1)}), bf16[8,24,1280]{2,1,0:T(8,128)(2,1)}, u32[]{:S(2)}, u32[]{:S(2)}) %all-to-all-start.3) | async-done | bytes 491552 | tf_op jit(solution)/shard_map/all_to_all | solution.py:288
  143.2 4.3 %all-to-all-start.2 = ((bf16[8,24,1280]{2,1,0:T(8,128)(2,1)}), bf16[8,24,1280]{2,1,0:T(8,128)(2,1)}, u32[]{:S(2)}, u32[]{:S(2)}) async-start(bf16[8,24,1280]{2,1,0:T(8,128)(2,1)} %bitcast.8), calls=%async_computation.2 | async-start | bytes 983040 | tf_op jit(solution)/shard_map/all_to_all | solution.py:288
  147.5 0.9 copy-done.9
  148.5 13.6 %shard_map.112 = (bf16[192,1024]{1,0:T(8,128)(2,1)}, bf16[192,1024]{1,0:T(8,128)(2,1)}, bf16[192,2560]{1,0:T(8,128)(2,1)}, bf16[192,2560]{1,0:T(8,128)(2,1)}, f32[1,2560]{1,0:T(1,128)}) custom-call(bf16[192,2560]{1,0:T(8,128)(2,1)} %bitcast.46, bf16[192,2560]{1,0:T(8,128)(2,1)} %copy-done.9, f32[192,1024]{1,0:T(8,128)} %get-tuple-element.74.refs_2_, ...), custom_call_target="tpu_custom_call" | custom-call | flops 1 | bytes 1 | tf_op jit(solution)/shard_map/pallas_call | solution.py:183
  162.1 0.1 collective-permute-start.13
  162.2 0.7 add.83
  162.9 0.6 collective-permute-start.14
  163.4 1.3 collective-permute-done.14
  164.7 0.6 collective-permute-start.15
  165.3 3.2 %collective-permute-done.15 = f32[1,2560]{1,0:T(1,128)S(1)} collective-permute-done((f32[1,2560]{1,0:T(1,128)S(1)}, f32[1,2560]{1,0:T(1,128)S(1)}, u32[]{:S(2)}, u32[]{:S(2)}) %collective-permute-start.15) | collective-permute-done | bytes 10272 | tf_op jit(solution)/shard_map/ppermute | solution.py:236
  168.5 0.1 pad_reduce_fusion
  168.6 1.9 add_convert_fusion
  170.5 1.1 pad_maximum_fusion
  171.5 5.9 %all-to-all-start.4 = ((bf16[8,24,2816]{2,1,0:T(8,128)(2,1)}), bf16[8,24,2816]{2,1,0:T(8,128)(2,1)S(1)}, u32[]{:S(2)}, u32[]{:S(2)}) async-start(bf16[8,24,2816]{2,1,0:T(8,128)(2,1)} %pad_maximum_fusion), calls=%async_computation.4 | async-start | bytes 2162688 | tf_op jit(solution)/shard_map/all_to_all | solution.py:288
  177.4 0.0 copy-start.6
  177.4 2.7 %fusion.4 = (f32[128]{0:T(128)S(1)}, bf16[128,2560]{1,0:T(8,128)(2,1)}) fusion(bf16[128,2560]{1,0:T(8,128)(2,1)S(1)} %copy-done.21, f32[128]{0:T(128)S(1)} %add_divide_fusion, bf16[192,1280]{1,0:T(8,128)(2,1)} %bitcast.11, bf16[192,1280]{1,0:T(8,128)(2,1)} %bitcast.9, s32[128]{0:T(128)S(1)} %compare_select_fusion), kind=kOutput, calls=%fused_computation.13 | convolution fusion | flops 130113408 | bytes 2295296 | tf_op jit(solution)/shard_map/dot_general | solution.py:12
  180.3 8.9 %shard_map.113 = bf16[2560,1024]{1,0:T(8,128)(2,1)} custom-call(bf16[192,2560]{1,0:T(8,128)(2,1)} %collective-permute-done.refs_0_.refs_6_, bf16[192,2560]{1,0:T(8,128)(2,1)S(1)} %copy-done.6, bf16[192,2560]{1,0:T(8,128)(2,1)S(1)} %bitcast.43, bf16[192,2560]{1,0:T(8,128)(2,1)} %collective-permute-done.2.refs_3_.refs_7_, bf16[192,1024]{1,0:T(8,128)(2,1)S(1)} %copy-done.15, ...), custom_call_target="tpu_custom_call" | custom-call | flops 4026531840 | bytes 10747904 | tf_op jit(solution)/shard_map/pallas_call | solution.py:220
  189.2 8.7 %shard_map.114 = bf16[1024,2560]{1,0:T(8,128)(2,1)} custom-call(bf16[192,1024]{1,0:T(8,128)(2,1)S(1)} %copy-done.11, bf16[192,1024]{1,0:T(8,128)(2,1)S(1)} %copy-done.12, bf16[192,1024]{1,0:T(8,128)(2,1)S(1)} %copy-done.13, bf16[192,1024]{1,0:T(8,128)(2,1)S(1)} %copy-done.14, bf16[192,2560]{1,0:T(8,128)(2,1)} %collective-permute-done.5.refs_0_.refs_4_, ...), custom_call_target="tpu_custom_call" | custom-call | flops 4026531840 | bytes 10747904 | tf_op jit(solution)/shard_map/pallas_call | solution.py:220
  197.9 5.4 %all-to-all-done.4 = bf16[8,24,2816]{2,1,0:T(8,128)(2,1)S(1)} async-done(((bf16[8,24,2816]{2,1,0:T(8,128)(2,1)}), bf16[8,24,2816]{2,1,0:T(8,128)(2,1)S(1)}, u32[]{:S(2)}, u32[]{:S(2)}) %all-to-all-start.4) | async-done | bytes 1081376 | tf_op jit(solution)/shard_map/all_to_all | solution.py:288
  203.3 0.4 fusion.11
  203.7 0.6 add_bitcast_fusion
  204.4 1.2 fusion.1
  (70 shorter events, 0.3 us)
Async XLA Ops:
  0.6 3.1 %copy-start = (bf16[128,2560]{1,0:T(8,128)(2,1)S(1)}, bf16[128,2560]{1,0:T(8,128)(2,1)}, u32[]{:S(2)}) copy-start(bf16[128,2560]{1,0:T(8,128)(2,1)} %param.7) | copy-start | bytes 1966084
  0.6 11.7 %copy-start.24 = (s32[128,1]{0,1:T(1,128)S(1)}, s32[128,1]{0,1:T(1,128)}, u32[]{:S(2)}) copy-start(s32[128,1]{0,1:T(1,128)} %param.8) | copy-start | bytes 1540
  0.7 11.7 %copy-start.22 = (bf16[2560,8]{0,1:T(8,128)(2,1)S(1)}, bf16[2560,8]{0,1:T(8,128)(2,1)}, u32[]{:S(2)}) copy-start(bf16[2560,8]{0,1:T(8,128)(2,1)} %param.10) | copy-start | bytes 122884
  3.7 8.9 %copy-start.21 = (bf16[128,2560]{1,0:T(8,128)(2,1)S(1)}, bf16[128,2560]{1,0:T(8,128)(2,1)}, u32[]{:S(2)}) copy-start(bf16[128,2560]{1,0:T(8,128)(2,1)} %param.13) | copy-start | bytes 1966084
  5.1 31.6 %all-to-all-start = ((bf16[8,24,2560]{2,1,0:T(8,128)(2,1)}), bf16[8,24,2560]{2,1,0:T(8,128)(2,1)S(1)}, u32[]{:S(2)}, u32[]{:S(2)}) async-start(bf16[8,24,2560]{2,1,0:T(8,128)(2,1)} %bitcast.2), calls=%async_computation | async-start | bytes 1966080 | tf_op jit(solution)/shard_map/all_to_all | solution.py:288
  36.7 30.9 %copy-start.1 = (bf16[8,24,2560]{2,1,0:T(8,128)(2,1)}, bf16[8,24,2560]{2,1,0:T(8,128)(2,1)S(1)}, u32[]{:S(2)}) copy-start(bf16[8,24,2560]{2,1,0:T(8,128)(2,1)S(1)} %all-to-all-done) | copy-start | bytes 2949124
  36.7 28.1 %all-to-all-start.1 = ((bf16[8,24,2560]{2,1,0:T(8,128)(2,1)}), bf16[8,24,2560]{2,1,0:T(8,128)(2,1)S(1)}, u32[]{:S(2)}, u32[]{:S(2)}) async-start(bf16[8,24,2560]{2,1,0:T(8,128)(2,1)} %bitcast.55), calls=%async_computation.1 | async-start | bytes 1966080 | tf_op jit(solution)/shard_map/all_to_all | solution.py:288
  40.3 23.5 %collective-permute-start = (bf16[192,2560]{1,0:T(8,128)(2,1)S(1)}, bf16[192,2560]{1,0:T(8,128)(2,1)}, u32[]{:S(2)}, u32[]{:S(2)}) collective-permute-start(bf16[192,2560]{1,0:T(8,128)(2,1)S(1)} %bitcast.39), channel_id=1, source_target_pairs={{0,2},{1,3},{2,0},{3,1},{4,6},{5,7},{6,4},{7,5},{8,10},{9,11},{10,... | collective-permute-start | bytes 2949128 | tf_op jit(solution)/shard_map/ppermute | solution.py:236
  41.9 24.5 %collective-permute-start.2 = (bf16[192,2560]{1,0:T(8,128)(2,1)S(1)}, bf16[192,2560]{1,0:T(8,128)(2,1)}, u32[]{:S(2)}, u32[]{:S(2)}) collective-permute-start(bf16[192,2560]{1,0:T(8,128)(2,1)S(1)} %bitcast.40), channel_id=1, source_target_pairs={{0,1},{1,0},{2,3},{3,2},{4,5},{5,4},{6,7},{7,6},{8,9},{9,8},{10,11... | collective-permute-start | bytes 2949128 | tf_op jit(solution)/shard_map/ppermute | solution.py:236
  64.8 64.6 %copy-start.3 = (bf16[8,24,2560]{2,1,0:T(8,128)(2,1)}, bf16[8,24,2560]{2,1,0:T(8,128)(2,1)S(1)}, u32[]{:S(2)}) copy-start(bf16[8,24,2560]{2,1,0:T(8,128)(2,1)S(1)} %all-to-all-done.1) | copy-start | bytes 2949124
  64.8 2.8 %collective-permute-start.1 = (bf16[192,2560]{1,0:T(8,128)(2,1)}, bf16[192,2560]{1,0:T(8,128)(2,1)S(1)}, u32[]{:S(2)}, u32[]{:S(2)}) collective-permute-start(bf16[192,2560]{1,0:T(8,128)(2,1)} %collective-permute-done.refs_0_.refs_6_), channel_id=1, source_target_pairs={{0,1},{1,0},{2,3},{3,2},{4,5},{5,4},{6,7},{7,6},{8,9},{9,8},{10,11... | collective-permute-start | bytes 2949128 | tf_op jit(solution)/shard_map/ppermute | solution.py:236
  64.8 24.3 %collective-permute-start.5 = (bf16[192,2560]{1,0:T(8,128)(2,1)S(1)}, bf16[192,2560]{1,0:T(8,128)(2,1)}, u32[]{:S(2)}, u32[]{:S(2)}) collective-permute-start(bf16[192,2560]{1,0:T(8,128)(2,1)S(1)} %bitcast.44), channel_id=1, source_target_pairs={{0,2},{1,3},{2,0},{3,1},{4,6},{5,7},{6,4},{7,5},{8,10},{9,11},{10,... | collective-permute-start | bytes 2949128 | tf_op jit(solution)/shard_map/ppermute | solution.py:236
  67.6 0.9 copy-start.5
  83.7 5.4 %collective-permute-start.4 = (bf16[192,2560]{1,0:T(8,128)(2,1)}, bf16[192,2560]{1,0:T(8,128)(2,1)}, u32[]{:S(2)}, u32[]{:S(2)}) collective-permute-start(bf16[192,2560]{1,0:T(8,128)(2,1)} %get-tuple-element.57), channel_id=1, source_target_pairs={{0,1},{1,0},{2,3},{3,2},{4,5},{5,4},{6,7},{7,6},{8,9},{9,8},{10,11... | collective-permute-start | bytes 2949128 | tf_op jit(solution)/shard_map/ppermute | solution.py:236
  89.1 2.8 %collective-permute-start.7 = (bf16[192,2560]{1,0:T(8,128)(2,1)}, bf16[192,2560]{1,0:T(8,128)(2,1)S(1)}, u32[]{:S(2)}, u32[]{:S(2)}) collective-permute-start(bf16[192,2560]{1,0:T(8,128)(2,1)} %collective-permute-done.5.refs_0_.refs_4_), channel_id=1, source_target_pairs={{0,1},{1,0},{2,3},{3,2},{4,5},{5,4},{6,7},{7,6},{8,9},{9,8},{10,11... | collective-permute-start | bytes 2949128 | tf_op jit(solution)/shard_map/ppermute | solution.py:236
  91.9 2.3 %copy-start.7 = (bf16[192,2560]{1,0:T(8,128)(2,1)}, bf16[192,2560]{1,0:T(8,128)(2,1)S(1)}, u32[]{:S(2)}) copy-start(bf16[192,2560]{1,0:T(8,128)(2,1)S(1)} %collective-permute-done.7.refs_1_.refs_5_) | copy-start | bytes 2949124
  92.0 18.4 %collective-permute-start.6 = (bf16[192,1280]{1,0:T(8,128)(2,1)S(1)}, bf16[192,1280]{1,0:T(8,128)(2,1)S(1)}, u32[]{:S(2)}, u32[]{:S(2)}) collective-permute-start(bf16[192,1280]{1,0:T(8,128)(2,1)S(1)} %get-tuple-element.109), channel_id=1, source_target_pairs={{0,2},{1,3},{2,0},{3,1},{4,6},{5,7},{6,4},{7,5},{8,10},{9,11},{10,... | collective-permute-start | bytes 1474568 | tf_op jit(solution)/shard_map/ppermute | solution.py:236
  107.8 2.0 copy-start.25
  107.8 4.0 %copy-start.19 = (bf16[192,2560]{1,0:T(8,128)(2,1)S(1)}, bf16[192,2560]{1,0:T(8,128)(2,1)}, u32[]{:S(2)}) copy-start(bf16[192,2560]{1,0:T(8,128)(2,1)} %get-tuple-element.66) | copy-start | bytes 2949124
  109.2 1.9 collective-permute-start.9
  109.3 2.6 %collective-permute-start.10 = (bf16[96,2560]{1,0:T(8,128)(2,1)S(1)}, bf16[96,2560]{1,0:T(8,128)(2,1)S(1)}, u32[]{:S(2)}, u32[]{:S(2)}) collective-permute-start(bf16[96,2560]{1,0:T(8,128)(2,1)S(1)} %get-tuple-element.108), channel_id=1, source_target_pairs={{0,1},{1,0},{2,3},{3,2},{4,5},{5,4},{6,7},{7,6},{8,9},{9,8},{10,11... | collective-permute-start | bytes 1474568 | tf_op jit(solution)/shard_map/ppermute | solution.py:236
  109.8 13.7 %collective-permute-start.3 = (bf16[192,2560]{1,0:T(8,128)(2,1)S(1)}, bf16[192,2560]{1,0:T(8,128)(2,1)S(1)}, u32[]{:S(2)}, u32[]{:S(2)}) collective-permute-start(bf16[192,2560]{1,0:T(8,128)(2,1)S(1)} %copy-done.25), channel_id=1, source_target_pairs={{0,1},{1,0},{2,3},{3,2},{4,5},{5,4},{6,7},{7,6},{8,9},{9,8},{10,11... | collective-permute-start | bytes 2949128 | tf_op jit(solution)/shard_map/ppermute | solution.py:236
  109.8 13.6 %collective-permute-start.8 = (bf16[192,1280]{1,0:T(8,128)(2,1)S(1)}, bf16[192,1280]{1,0:T(8,128)(2,1)S(1)}, u32[]{:S(2)}, u32[]{:S(2)}) collective-permute-start(bf16[192,1280]{1,0:T(8,128)(2,1)S(1)} %get-tuple-element.110), channel_id=1, source_target_pairs={{0,2},{1,3},{2,0},{3,1},{4,6},{5,7},{6,4},{7,5},{8,10},{9,11},{10,... | collective-permute-start | bytes 1474568 | tf_op jit(solution)/shard_map/ppermute | solution.py:236
  110.4 13.1 %copy-start.20 = (bf16[192,2560]{1,0:T(8,128)(2,1)S(1)}, bf16[192,2560]{1,0:T(8,128)(2,1)}, u32[]{:S(2)}) copy-start(bf16[192,2560]{1,0:T(8,128)(2,1)} %get-tuple-element.54) | copy-start | bytes 2949124
  124.8 18.4 %all-to-all-start.3 = ((bf16[8,24,1280]{2,1,0:T(8,128)(2,1)}), bf16[8,24,1280]{2,1,0:T(8,128)(2,1)}, u32[]{:S(2)}, u32[]{:S(2)}) async-start(bf16[8,24,1280]{2,1,0:T(8,128)(2,1)} %bitcast.10), calls=%async_computation.3 | async-start | bytes 983040 | tf_op jit(solution)/shard_map/all_to_all | solution.py:288
  129.5 18.1 %collective-permute-start.11 = (bf16[192,2560]{1,0:T(8,128)(2,1)S(1)}, bf16[192,2560]{1,0:T(8,128)(2,1)S(1)}, u32[]{:S(2)}, u32[]{:S(2)}) collective-permute-start(bf16[192,2560]{1,0:T(8,128)(2,1)S(1)} %bitcast.45), channel_id=1, source_target_pairs={{0,1},{1,0},{2,3},{3,2},{4,5},{5,4},{6,7},{7,6},{8,9},{9,8},{10,11... | collective-permute-start | bytes 2949128 | tf_op jit(solution)/shard_map/ppermute | solution.py:236
  129.5 32.5 %collective-permute-start.12 = (bf16[192,2560]{1,0:T(8,128)(2,1)}, bf16[192,2560]{1,0:T(8,128)(2,1)}, u32[]{:S(2)}, u32[]{:S(2)}) collective-permute-start(bf16[192,2560]{1,0:T(8,128)(2,1)} %pad_maximum_fusion.1), channel_id=1, source_target_pairs={{0,2},{1,3},{2,0},{3,1},{4,6},{5,7},{6,4},{7,5},{8,10},{9,11},{10,... | collective-permute-start | bytes 2949128 | tf_op jit(solution)/shard_map/ppermute | solution.py:236
  143.2 25.3 %all-to-all-start.2 = ((bf16[8,24,1280]{2,1,0:T(8,128)(2,1)}), bf16[8,24,1280]{2,1,0:T(8,128)(2,1)}, u32[]{:S(2)}, u32[]{:S(2)}) async-start(bf16[8,24,1280]{2,1,0:T(8,128)(2,1)} %bitcast.8), calls=%async_computation.2 | async-start | bytes 983040 | tf_op jit(solution)/shard_map/all_to_all | solution.py:288
  147.5 0.9 copy-start.9
  148.5 13.7 %copy-start.23 = (f32[1,2560]{1,0:T(1,128)S(1)}, f32[1,2560]{1,0:T(1,128)}, u32[]{:S(2)}) copy-start(f32[1,2560]{1,0:T(1,128)} %get-tuple-element.84) | copy-start | bytes 30724
  162.1 6.5 %collective-permute-start.13 = (bf16[192,2560]{1,0:T(8,128)(2,1)}, bf16[192,2560]{1,0:T(8,128)(2,1)S(1)}, u32[]{:S(2)}, u32[]{:S(2)}) collective-permute-start(bf16[192,2560]{1,0:T(8,128)(2,1)} %get-tuple-element.81), channel_id=1, source_target_pairs={{0,1},{1,0},{2,3},{3,2},{4,5},{5,4},{6,7},{7,6},{8,9},{9,8},{10,11... | collective-permute-start | bytes 2949128 | tf_op jit(solution)/shard_map/ppermute | solution.py:236
  162.9 1.8 collective-permute-start.14
  164.7 3.7 %collective-permute-start.15 = (f32[1,2560]{1,0:T(1,128)S(1)}, f32[1,2560]{1,0:T(1,128)S(1)}, u32[]{:S(2)}, u32[]{:S(2)}) collective-permute-start(f32[1,2560]{1,0:T(1,128)S(1)} %add.84), channel_id=1, source_target_pairs={{0,2},{1,3},{2,0},{3,1},{4,6},{5,7},{6,4},{7,5},{8,10},{9,11},{10,... | collective-permute-start | bytes 30728 | tf_op jit(solution)/shard_map/ppermute | solution.py:236
  171.5 8.6 %copy-start.18 = (bf16[192,1024]{1,0:T(8,128)(2,1)S(1)}, bf16[192,1024]{1,0:T(8,128)(2,1)}, u32[]{:S(2)}) copy-start(bf16[192,1024]{1,0:T(8,128)(2,1)} %get-tuple-element.94.refs_7_) | copy-start | bytes 1179652
  171.5 31.7 %all-to-all-start.4 = ((bf16[8,24,2816]{2,1,0:T(8,128)(2,1)}), bf16[8,24,2816]{2,1,0:T(8,128)(2,1)S(1)}, u32[]{:S(2)}, u32[]{:S(2)}) async-start(bf16[8,24,2816]{2,1,0:T(8,128)(2,1)} %pad_maximum_fusion), calls=%async_computation.4 | async-start | bytes 2162688 | tf_op jit(solution)/shard_map/all_to_all | solution.py:288
  177.4 2.7 %copy-start.2 = (bf16[8,24,2560]{2,1,0:T(8,128)(2,1)S(1)}, bf16[8,24,2560]{2,1,0:T(8,128)(2,1)}, u32[]{:S(2)}) copy-start(bf16[8,24,2560]{2,1,0:T(8,128)(2,1)} %copy-done.1) | copy-start | bytes 2949124
  177.4 2.7 %copy-start.6 = (bf16[192,2560]{1,0:T(8,128)(2,1)S(1)}, bf16[192,2560]{1,0:T(8,128)(2,1)}, u32[]{:S(2)}) copy-start(bf16[192,2560]{1,0:T(8,128)(2,1)} %copy-done.5) | copy-start | bytes 2949124
  177.4 2.7 %copy-start.15 = (bf16[192,1024]{1,0:T(8,128)(2,1)S(1)}, bf16[192,1024]{1,0:T(8,128)(2,1)}, u32[]{:S(2)}) copy-start(bf16[192,1024]{1,0:T(8,128)(2,1)} %get-tuple-element.91.refs_4_) | copy-start | bytes 1179652
  177.4 2.7 %copy-start.16 = (bf16[192,1024]{1,0:T(8,128)(2,1)S(1)}, bf16[192,1024]{1,0:T(8,128)(2,1)}, u32[]{:S(2)}) copy-start(bf16[192,1024]{1,0:T(8,128)(2,1)} %get-tuple-element.92.refs_5_) | copy-start | bytes 1179652
  177.4 2.7 %copy-start.17 = (bf16[192,1024]{1,0:T(8,128)(2,1)S(1)}, bf16[192,1024]{1,0:T(8,128)(2,1)}, u32[]{:S(2)}) copy-start(bf16[192,1024]{1,0:T(8,128)(2,1)} %get-tuple-element.93.refs_6_) | copy-start | bytes 1179652
  180.2 8.9 %copy-start.4 = (bf16[8,24,2560]{2,1,0:T(8,128)(2,1)S(1)}, bf16[8,24,2560]{2,1,0:T(8,128)(2,1)}, u32[]{:S(2)}) copy-start(bf16[8,24,2560]{2,1,0:T(8,128)(2,1)} %copy-done.3) | copy-start | bytes 2949124
  180.2 8.9 %copy-start.8 = (bf16[192,2560]{1,0:T(8,128)(2,1)S(1)}, bf16[192,2560]{1,0:T(8,128)(2,1)}, u32[]{:S(2)}) copy-start(bf16[192,2560]{1,0:T(8,128)(2,1)} %copy-done.7) | copy-start | bytes 2949124
  180.2 8.9 %copy-start.10 = (bf16[192,2560]{1,0:T(8,128)(2,1)S(1)}, bf16[192,2560]{1,0:T(8,128)(2,1)}, u32[]{:S(2)}) copy-start(bf16[192,2560]{1,0:T(8,128)(2,1)} %copy-done.9) | copy-start | bytes 2949124
  180.2 8.9 %copy-start.11 = (bf16[192,1024]{1,0:T(8,128)(2,1)S(1)}, bf16[192,1024]{1,0:T(8,128)(2,1)}, u32[]{:S(2)}) copy-start(bf16[192,1024]{1,0:T(8,128)(2,1)} %get-tuple-element.95.refs_4_.refs_0_) | copy-start | bytes 1179652
  180.2 8.9 %copy-start.12 = (bf16[192,1024]{1,0:T(8,128)(2,1)S(1)}, bf16[192,1024]{1,0:T(8,128)(2,1)}, u32[]{:S(2)}) copy-start(bf16[192,1024]{1,0:T(8,128)(2,1)} %get-tuple-element.96.refs_5_.refs_1_) | copy-start | bytes 1179652
  180.2 8.9 %copy-start.13 = (bf16[192,1024]{1,0:T(8,128)(2,1)S(1)}, bf16[192,1024]{1,0:T(8,128)(2,1)}, u32[]{:S(2)}) copy-start(bf16[192,1024]{1,0:T(8,128)(2,1)} %get-tuple-element.97.refs_4_.refs_2_) | copy-start | bytes 1179652
  180.2 8.9 %copy-start.14 = (bf16[192,1024]{1,0:T(8,128)(2,1)S(1)}, bf16[192,1024]{1,0:T(8,128)(2,1)}, u32[]{:S(2)}) copy-start(bf16[192,1024]{1,0:T(8,128)(2,1)} %get-tuple-element.98.refs_5_.refs_3_) | copy-start | bytes 1179652

commit v3 on v2

--- a/solution.py
+++ b/solution.py
@@ -320,14 +320,15 @@
             column,
         )
         out_far_left = after(out_far_left, *far_term)
-        out_home_left = exchange(added(*[x[:, :cut] for x in out_near], out_far_left))
+        out_left = added(*[x[:, :cut] for x in out_near], out_far_left)
+        out_home_left = exchange(out_left)
         back_far_sum = sum_low_after(far_term, out_far_left)
         back_far = cross(back_far_sum, top)
-        out_far_right = after(out_far_right, back_far_sum)
+        out_far_right = after(out_far_right, back_far_sum, out_home_left)
         out_sum = added(*[x[:, cut:] for x in out_near], out_far_right)
         out_home_right = exchange(out_sum)
 
-        near = [after(x, out_sum, back_far_sum) for x in gather_low(cot_near)]
+        near = [after(x, out_left, back_far_sum) for x in gather_low(cot_near)]
         near_hidden_cot, near_term, near_column = backward(
             near, hidden[low:], active[low:], rows[low:], w_up, w_down, column
         )

time: 206 us -> 197 us (0.956)
  waiting for transfers between devices: 87.7 us -> 72.1 us
  starting transfers between devices: 33.5 us -> 36 us
  other arithmetic: 10.9 us -> 13.2 us
    ppermute x16, waiting for transfers between devices: 45.6 us -> 32.3 us  [cross(): return lax.ppermute(x, 'tensor', [(i, i ^ bit) for i in range(n_tensor)])]
    convert_element_type x4 -> x5, other arithmetic: 5.16 us -> 8.36 us  [added(): sum((part.astype(jnp.float32) for part in parts)).astype(jnp.bfloat16)]
    ppermute x16, starting transfers between devices: 7.89 us -> 10.3 us  [cross(): return lax.ppermute(x, 'tensor', [(i, i ^ bit) for i in range(n_tensor)])]
    all_to_all x5, waiting for transfers between devices: 42.1 us -> 39.7 us  [swap(): return lax.all_to_all(x, 'expert', split_axis=0, concat_axis=0, tiled=True)]
  transfers between devices with their start and end apart: 21 -> 21, of which waited for: 13 -> 10; matrix products, arithmetic and copies ran while one was open for 5% -> 8% of each run, Pallas kernels for 29% -> 31%
where the time goes in v3:
time: 197 us; the launch traced here: 196 us
  waiting for transfers between devices  72.1 us (37%)
  Pallas kernels  60.2 us (31%)
  starting transfers between devices  36 us (18%)
  other arithmetic  13.2 us (7%)
  matrix products  7.39 us (4%)
  local copies, waits for them, and re-layouts  5.25 us (3%)
    all_to_all x5, waiting for transfers between devices, swap(): return lax.all_to_all(x, 'expert', split_axis=0, concat_axis=0, tiled=True)  39.7 us
    ppermute x16, waiting for transfers between devices, cross(): return lax.ppermute(x, 'tensor', [(i, i ^ bit) for i in range(n_tensor)])  32.3 us
    pallas_call x2, Pallas kernels, backward(): call(functools.partial(backward_kernel, n, steps, steps + wides - 1, tile...  27.2 us
    all_to_all x5, starting transfers between devices, swap(): return lax.all_to_all(x, 'expert', split_axis=0, concat_axis=0, tiled=True)  25.7 us
    pallas_call x2, Pallas kernels, gradient(): call(functools.partial(gradient_kernel, len(lefts)), height // tile, [pl....  17.9 us
    pallas_call x1, Pallas kernels, forward(): call(functools.partial(forward_kernel, n, steps, tile), steps + wides, [w...  15.1 us
    ppermute x16, starting transfers between devices, cross(): return lax.ppermute(x, 'tensor', [(i, i ^ bit) for i in range(n_tensor)])  10.3 us
    convert_element_type x5, other arithmetic, added(): sum((part.astype(jnp.float32) for part in parts)).astype(jnp.bfloat16)  8.36 us
  transfers between devices with their start and end apart: 21, of which 10 were waited for; matrix products, arithmetic and copies ran while one was open for 8% of the time, Pallas kernels for 31%

profile of v3, /device:TPU:0, one launch (start us, length us, event | category | flops | bytes accessed | tf_op | source)
XLA Modules:
  0.0 195.8 jit_solution(11423662204765174634)
XLA Ops:
  0.6 0.0 copy-start
  0.6 0.0 copy-start.23
  1.4 0.7 fusion.16
  2.0 0.1 copy.12
  2.1 0.2 reduce_window_sum.11
  2.4 0.7 select_reduce_fusion
  3.1 0.7 compare_select_fusion
  3.7 1.4 convolution_convert_fusion.1
  5.1 7.3 %all-to-all-start = ((bf16[8,24,2560]{2,1,0:T(8,128)(2,1)}), bf16[8,24,2560]{2,1,0:T(8,128)(2,1)S(1)}, u32[]{:S(2)}, u32[]{:S(2)}) async-start(bf16[8,24,2560]{2,1,0:T(8,128)(2,1)} %bitcast.2), calls=%async_computation | async-start | bytes 1966080 | tf_op jit(solution)/shard_map/all_to_all | solution.py:288
  12.3 0.3 fusion.5
  12.6 1.5 convolution_convert_fusion
  14.1 22.6 %all-to-all-done = bf16[8,24,2560]{2,1,0:T(8,128)(2,1)S(1)} async-done(((bf16[8,24,2560]{2,1,0:T(8,128)(2,1)}), bf16[8,24,2560]{2,1,0:T(8,128)(2,1)S(1)}, u32[]{:S(2)}, u32[]{:S(2)}) %all-to-all-start) | async-done | bytes 983072 | tf_op jit(solution)/shard_map/all_to_all | solution.py:288
  36.7 3.6 %all-to-all-start.1 = ((bf16[8,24,2560]{2,1,0:T(8,128)(2,1)}), bf16[8,24,2560]{2,1,0:T(8,128)(2,1)S(1)}, u32[]{:S(2)}, u32[]{:S(2)}) async-start(bf16[8,24,2560]{2,1,0:T(8,128)(2,1)} %bitcast.55), calls=%async_computation.1 | async-start | bytes 1966080 | tf_op jit(solution)/shard_map/all_to_all | solution.py:288
  40.3 1.6 collective-permute-start
  41.9 0.0 collective-permute-start.2
  41.9 21.9 %collective-permute-done.refs_0_.refs_6_ = bf16[192,2560]{1,0:T(8,128)(2,1)} collective-permute-done((bf16[192,2560]{1,0:T(8,128)(2,1)S(1)}, bf16[192,2560]{1,0:T(8,128)(2,1)}, u32[]{:S(2)}, u32[]{:S(2)}) %collective-permute-start) | collective-permute-done | bytes 983072 | tf_op jit(solution)/shard_map/ppermute | solution.py:236
  63.8 1.0 all-to-all-done.1
  64.8 0.0 collective-permute-start.1
  64.8 1.5 collective-permute-start.5
  66.4 0.0 collective-permute-done.2.refs_3_.refs_7_
  66.4 1.3 collective-permute-done.1.refs_1_.refs_7_
  67.6 0.9 copy-done.5
  68.6 15.1 %shard_map.110 = (f32[192,1024]{1,0:T(8,128)}, f32[192,1024]{1,0:T(8,128)}, f32[192,1024]{1,0:T(8,128)}, f32[192,1024]{1,0:T(8,128)}, bf16[192,1024]{1,0:T(8,128...) custom-call(bf16[192,2560]{1,0:T(8,128)(2,1)} %collective-permute-do, ...), custom_call_target="tpu_custom_call" | custom-call | flops 1 | bytes 1 | tf_op jit(solution)/shard_map/pallas_call | solution.py:157
  83.7 0.2 collective-permute-start.4
  83.9 5.2 %collective-permute-done.5.refs_0_.refs_4_ = bf16[192,2560]{1,0:T(8,128)(2,1)} collective-permute-done((bf16[192,2560]{1,0:T(8,128)(2,1)S(1)}, bf16[192,2560]{1,0:T(8,128)(2,1)}, u32[]{:S(2)}, u32[]{:S(2)}) %collective-permute-start.5) | collective-permute-done | bytes 983072 | tf_op jit(solution)/shard_map/ppermute | solution.py:236
  89.2 0.6 collective-permute-start.10
  89.7 0.1 collective-permute-start.3
  89.8 0.0 collective-permute-done.4
  89.8 1.7 add_convert_fusion.2
  91.5 0.5 collective-permute-done.7.refs_1_.refs_5_
  92.0 0.9 fusion.20
  92.9 1.5 collective-permute-start.6
  94.5 0.5 collective-permute-start.13
  95.0 0.6 broadcast_in_dim.15.refs_10_
  95.6 13.6 %shard_map.111 = (bf16[192,1024]{1,0:T(8,128)(2,1)}, bf16[192,1024]{1,0:T(8,128)(2,1)}, bf16[192,2560]{1,0:T(8,128)(2,1)}, bf16[192,2560]{1,0:T(8,128)(2,1)}, f32[1,2560]{1,0:T(1,128)}) custom-call(bf16[192,2560]{1,0:T(8,128)(2,1)} %collective-permute-done.5.refs_0_.refs_4_, bf16[192,2560]{1,0:T(8,128)(2,1)} %copy-done.7, ...), custom_call_target="tpu_custom_call" | custom-call | flops 1 | bytes 1 | tf_op jit(solution)/shard_map/pallas_call | solution.py:183
  109.2 2.3 %fusion.19 = (bf16[96,2560]{1,0:T(8,128)(2,1)}, bf16[96,2560]{1,0:T(8,128)(2,1)}) fusion(bf16[192,2560]{1,0:T(8,128)(2,1)} %get-tuple-element.67), kind=kLoop, calls=%fused_computation.52 | loop fusion | bytes 1966080 | tf_op jit(solution)/shard_map/slice | solution.py:250
  111.6 0.5 collective-permute-start.9
  112.1 1.1 add_convert_fusion.6
  113.2 4.7 %all-to-all-start.2 = ((bf16[8,24,1280]{2,1,0:T(8,128)(2,1)}), bf16[8,24,1280]{2,1,0:T(8,128)(2,1)}, u32[]{:S(2)}, u32[]{:S(2)}) async-start(bf16[8,24,1280]{2,1,0:T(8,128)(2,1)} %bitcast.8), calls=%async_computation.2 | async-start | bytes 983040 | tf_op jit(solution)/shard_map/all_to_all | solution.py:288
  117.9 1.4 add_convert_fusion.5
  119.3 0.1 pad_maximum_fusion.1
  119.4 1.6 collective-permute-start.11
  121.0 11.0 %all-to-all-done.2 = bf16[8,24,1280]{2,1,0:T(8,128)(2,1)} async-done(((bf16[8,24,1280]{2,1,0:T(8,128)(2,1)}), bf16[8,24,1280]{2,1,0:T(8,128)(2,1)}, u32[]{:S(2)}, u32[]{:S(2)}) %all-to-all-start.2) | async-done | bytes 491552 | tf_op jit(solution)/shard_map/all_to_all | solution.py:288
  132.0 2.3 %add_convert_fusion.3 = bf16[192,1280]{1,0:T(8,128)(2,1)} fusion(bf16[192,1280]{1,0:T(8,128)(2,1)} %collective-permute-done.13, bf16[192,2560]{1,0:T(8,128)(2,1)} %copy-done.19, bf16[192,2560]{1,0:T(8,128)(2,1)} %get-tuple-element.54), kind=kLoop, calls=%fused_computation.23 | loop fusion | flops 1474560 | bytes 1966080 | tf_op jit(solution)/shard_map/convert_element_type | solution.py:24
  134.3 4.3 %all-to-all-start.3 = ((bf16[8,24,1280]{2,1,0:T(8,128)(2,1)}), bf16[8,24,1280]{2,1,0:T(8,128)(2,1)}, u32[]{:S(2)}, u32[]{:S(2)}) async-start(bf16[8,24,1280]{2,1,0:T(8,128)(2,1)} %bitcast.10), calls=%async_computation.3 | async-start | bytes 983040 | tf_op jit(solution)/shard_map/all_to_all | solution.py:288
  138.6 13.6 %shard_map.112 = (bf16[192,1024]{1,0:T(8,128)(2,1)}, bf16[192,1024]{1,0:T(8,128)(2,1)}, bf16[192,2560]{1,0:T(8,128)(2,1)}, bf16[192,2560]{1,0:T(8,128)(2,1)}, f32[1,2560]{1,0:T(1,128)}) custom-call(bf16[192,2560]{1,0:T(8,128)(2,1)} %bitcast.46, bf16[192,2560]{1,0:T(8,128)(2,1)} %collective-permute-done.10.refs_1_.refs_7_, ...), custom_call_target="tpu_custom_call" | custom-call | flops 1 | bytes 1 | tf_op jit(solution)/shard_map/pallas_call | solution.py:183
  152.2 0.1 collective-permute-start.12
  152.3 0.7 add.83
  153.0 0.6 collective-permute-start.14
  153.6 1.3 collective-permute-done.14
  154.9 1.6 collective-permute-start.15
  156.5 2.1 %collective-permute-done.15 = f32[1,2560]{1,0:T(1,128)S(1)} collective-permute-done((f32[1,2560]{1,0:T(1,128)S(1)}, f32[1,2560]{1,0:T(1,128)S(1)}, u32[]{:S(2)}, u32[]{:S(2)}) %collective-permute-start.15) | collective-permute-done | bytes 10272 | tf_op jit(solution)/shard_map/ppermute | solution.py:236
  158.7 0.1 pad_reduce_fusion
  158.8 1.9 add_convert_fusion
  160.6 1.1 pad_maximum_fusion
  161.8 5.9 %all-to-all-start.4 = ((bf16[8,24,2816]{2,1,0:T(8,128)(2,1)}), bf16[8,24,2816]{2,1,0:T(8,128)(2,1)S(1)}, u32[]{:S(2)}, u32[]{:S(2)}) async-start(bf16[8,24,2816]{2,1,0:T(8,128)(2,1)} %pad_maximum_fusion), calls=%async_computation.4 | async-start | bytes 2162688 | tf_op jit(solution)/shard_map/all_to_all | solution.py:288
  167.6 0.0 copy-start.6
  167.7 2.7 %fusion.4 = (f32[128]{0:T(128)S(1)}, bf16[128,2560]{1,0:T(8,128)(2,1)}) fusion(bf16[128,2560]{1,0:T(8,128)(2,1)S(1)} %copy-done.20, f32[128]{0:T(128)S(1)} %add_divide_fusion, bf16[192,1280]{1,0:T(8,128)(2,1)} %bitcast.11, bf16[192,1280]{1,0:T(8,128)(2,1)} %bitcast.9, s32[128]{0:T(128)S(1)} %compare_select_fusion), kind=kOutput, calls=%fused_computation.13 | convolution fusion | flops 130113408 | bytes 2295296 | tf_op jit(solution)/shard_map/dot_general | solution.py:12
  170.5 8.9 %shard_map.113 = bf16[2560,1024]{1,0:T(8,128)(2,1)} custom-call(bf16[192,2560]{1,0:T(8,128)(2,1)} %collective-permute-done.refs_0_.refs_6_, bf16[192,2560]{1,0:T(8,128)(2,1)S(1)} %copy-done.6, bf16[192,2560]{1,0:T(8,128)(2,1)S(1)} %bitcast.43, bf16[192,2560]{1,0:T(8,128)(2,1)} %collective-permute-done.2.refs_3_.refs_7_, bf16[192,1024]{1,0:T(8,128)(2,1)S(1)} %copy-done.13, ...), custom_call_target="tpu_custom_call" | custom-call | flops 4026531840 | bytes 10747904 | tf_op jit(solution)/shard_map/pallas_call | solution.py:220
  179.4 9.0 %shard_map.114 = bf16[1024,2560]{1,0:T(8,128)(2,1)} custom-call(bf16[192,1024]{1,0:T(8,128)(2,1)S(1)} %copy-done.9, bf16[192,1024]{1,0:T(8,128)(2,1)S(1)} %copy-done.10, bf16[192,1024]{1,0:T(8,128)(2,1)S(1)} %copy-done.11, bf16[192,1024]{1,0:T(8,128)(2,1)S(1)} %copy-done.12, bf16[192,2560]{1,0:T(8,128)(2,1)} %collective-permute-done.5.refs_0_.refs_4_, ...), custom_call_target="tpu_custom_call" | custom-call | flops 4026531840 | bytes 10747904 | tf_op jit(solution)/shard_map/pallas_call | solution.py:220
  188.4 5.1 %all-to-all-done.4 = bf16[8,24,2816]{2,1,0:T(8,128)(2,1)S(1)} async-done(((bf16[8,24,2816]{2,1,0:T(8,128)(2,1)}), bf16[8,24,2816]{2,1,0:T(8,128)(2,1)S(1)}, u32[]{:S(2)}, u32[]{:S(2)}) %all-to-all-start.4) | async-done | bytes 1081376 | tf_op jit(solution)/shard_map/all_to_all | solution.py:288
  193.5 0.4 fusion.11
  193.9 0.6 add_bitcast_fusion
  194.6 1.2 fusion.1
  (67 shorter events, 0.3 us)
Async XLA Ops:
  0.6 3.1 %copy-start = (bf16[128,2560]{1,0:T(8,128)(2,1)S(1)}, bf16[128,2560]{1,0:T(8,128)(2,1)}, u32[]{:S(2)}) copy-start(bf16[128,2560]{1,0:T(8,128)(2,1)} %param.7) | copy-start | bytes 1966084
  0.6 11.7 %copy-start.23 = (s32[128,1]{0,1:T(1,128)S(1)}, s32[128,1]{0,1:T(1,128)}, u32[]{:S(2)}) copy-start(s32[128,1]{0,1:T(1,128)} %param.8) | copy-start | bytes 1540
  0.7 11.7 %copy-start.21 = (bf16[2560,8]{0,1:T(8,128)(2,1)S(1)}, bf16[2560,8]{0,1:T(8,128)(2,1)}, u32[]{:S(2)}) copy-start(bf16[2560,8]{0,1:T(8,128)(2,1)} %param.10) | copy-start | bytes 122884
  3.7 8.9 %copy-start.20 = (bf16[128,2560]{1,0:T(8,128)(2,1)S(1)}, bf16[128,2560]{1,0:T(8,128)(2,1)}, u32[]{:S(2)}) copy-start(bf16[128,2560]{1,0:T(8,128)(2,1)} %param.13) | copy-start | bytes 1966084
  5.1 31.6 %all-to-all-start = ((bf16[8,24,2560]{2,1,0:T(8,128)(2,1)}), bf16[8,24,2560]{2,1,0:T(8,128)(2,1)S(1)}, u32[]{:S(2)}, u32[]{:S(2)}) async-start(bf16[8,24,2560]{2,1,0:T(8,128)(2,1)} %bitcast.2), calls=%async_computation | async-start | bytes 1966080 | tf_op jit(solution)/shard_map/all_to_all | solution.py:288
  36.7 30.9 %copy-start.1 = (bf16[8,24,2560]{2,1,0:T(8,128)(2,1)}, bf16[8,24,2560]{2,1,0:T(8,128)(2,1)S(1)}, u32[]{:S(2)}) copy-start(bf16[8,24,2560]{2,1,0:T(8,128)(2,1)S(1)} %all-to-all-done) | copy-start | bytes 2949124
  36.7 28.1 %all-to-all-start.1 = ((bf16[8,24,2560]{2,1,0:T(8,128)(2,1)}), bf16[8,24,2560]{2,1,0:T(8,128)(2,1)S(1)}, u32[]{:S(2)}, u32[]{:S(2)}) async-start(bf16[8,24,2560]{2,1,0:T(8,128)(2,1)} %bitcast.55), calls=%async_computation.1 | async-start | bytes 1966080 | tf_op jit(solution)/shard_map/all_to_all | solution.py:288
  40.3 23.5 %collective-permute-start = (bf16[192,2560]{1,0:T(8,128)(2,1)S(1)}, bf16[192,2560]{1,0:T(8,128)(2,1)}, u32[]{:S(2)}, u32[]{:S(2)}) collective-permute-start(bf16[192,2560]{1,0:T(8,128)(2,1)S(1)} %bitcast.39), channel_id=1, source_target_pairs={{0,2},{1,3},{2,0},{3,1},{4,6},{5,7},{6,4},{7,5},{8,10},{9,11},{10,... | collective-permute-start | bytes 2949128 | tf_op jit(solution)/shard_map/ppermute | solution.py:236
  41.9 24.5 %collective-permute-start.2 = (bf16[192,2560]{1,0:T(8,128)(2,1)S(1)}, bf16[192,2560]{1,0:T(8,128)(2,1)}, u32[]{:S(2)}, u32[]{:S(2)}) collective-permute-start(bf16[192,2560]{1,0:T(8,128)(2,1)S(1)} %bitcast.40), channel_id=1, source_target_pairs={{0,1},{1,0},{2,3},{3,2},{4,5},{5,4},{6,7},{7,6},{8,9},{9,8},{10,11... | collective-permute-start | bytes 2949128 | tf_op jit(solution)/shard_map/ppermute | solution.py:236
  64.8 24.3 %copy-start.3 = (bf16[8,24,2560]{2,1,0:T(8,128)(2,1)}, bf16[8,24,2560]{2,1,0:T(8,128)(2,1)S(1)}, u32[]{:S(2)}) copy-start(bf16[8,24,2560]{2,1,0:T(8,128)(2,1)S(1)} %all-to-all-done.1) | copy-start | bytes 2949124
  64.8 2.8 %collective-permute-start.1 = (bf16[192,2560]{1,0:T(8,128)(2,1)}, bf16[192,2560]{1,0:T(8,128)(2,1)S(1)}, u32[]{:S(2)}, u32[]{:S(2)}) collective-permute-start(bf16[192,2560]{1,0:T(8,128)(2,1)} %collective-permute-done.refs_0_.refs_6_), channel_id=1, source_target_pairs={{0,1},{1,0},{2,3},{3,2},{4,5},{5,4},{6,7},{7,6},{8,9},{9,8},{10,11... | collective-permute-start | bytes 2949128 | tf_op jit(solution)/shard_map/ppermute | solution.py:236
  64.8 24.3 %collective-permute-start.5 = (bf16[192,2560]{1,0:T(8,128)(2,1)S(1)}, bf16[192,2560]{1,0:T(8,128)(2,1)}, u32[]{:S(2)}, u32[]{:S(2)}) collective-permute-start(bf16[192,2560]{1,0:T(8,128)(2,1)S(1)} %bitcast.44), channel_id=1, source_target_pairs={{0,2},{1,3},{2,0},{3,1},{4,6},{5,7},{6,4},{7,5},{8,10},{9,11},{10,... | collective-permute-start | bytes 2949128 | tf_op jit(solution)/shard_map/ppermute | solution.py:236
  67.6 0.9 copy-start.5
  83.7 6.1 %collective-permute-start.4 = (bf16[192,2560]{1,0:T(8,128)(2,1)}, bf16[192,2560]{1,0:T(8,128)(2,1)}, u32[]{:S(2)}, u32[]{:S(2)}) collective-permute-start(bf16[192,2560]{1,0:T(8,128)(2,1)} %get-tuple-element.57), channel_id=1, source_target_pairs={{0,1},{1,0},{2,3},{3,2},{4,5},{5,4},{6,7},{7,6},{8,9},{9,8},{10,11... | collective-permute-start | bytes 2949128 | tf_op jit(solution)/shard_map/ppermute | solution.py:236
  89.1 2.9 %collective-permute-start.7 = (bf16[192,2560]{1,0:T(8,128)(2,1)}, bf16[192,2560]{1,0:T(8,128)(2,1)S(1)}, u32[]{:S(2)}, u32[]{:S(2)}) collective-permute-start(bf16[192,2560]{1,0:T(8,128)(2,1)} %collective-permute-done.5.refs_0_.refs_4_), channel_id=1, source_target_pairs={{0,1},{1,0},{2,3},{3,2},{4,5},{5,4},{6,7},{7,6},{8,9},{9,8},{10,11... | collective-permute-start | bytes 2949128 | tf_op jit(solution)/shard_map/ppermute | solution.py:236
  89.2 49.4 %collective-permute-start.10 = (bf16[192,2560]{1,0:T(8,128)(2,1)S(1)}, bf16[192,2560]{1,0:T(8,128)(2,1)}, u32[]{:S(2)}, u32[]{:S(2)}) collective-permute-start(bf16[192,2560]{1,0:T(8,128)(2,1)S(1)} %bitcast.45), channel_id=1, source_target_pairs={{0,1},{1,0},{2,3},{3,2},{4,5},{5,4},{6,7},{7,6},{8,9},{9,8},{10,11... | collective-permute-start | bytes 2949128 | tf_op jit(solution)/shard_map/ppermute | solution.py:236
  89.7 22.3 %collective-permute-start.3 = (bf16[192,2560]{1,0:T(8,128)(2,1)}, bf16[192,2560]{1,0:T(8,128)(2,1)S(1)}, u32[]{:S(2)}, u32[]{:S(2)}) collective-permute-start(bf16[192,2560]{1,0:T(8,128)(2,1)} %get-tuple-element.55), channel_id=1, source_target_pairs={{0,1},{1,0},{2,3},{3,2},{4,5},{5,4},{6,7},{7,6},{8,9},{9,8},{10,11... | collective-permute-start | bytes 2949128 | tf_op jit(solution)/shard_map/ppermute | solution.py:236
  92.0 3.6 %copy-start.7 = (bf16[192,2560]{1,0:T(8,128)(2,1)}, bf16[192,2560]{1,0:T(8,128)(2,1)S(1)}, u32[]{:S(2)}) copy-start(bf16[192,2560]{1,0:T(8,128)(2,1)S(1)} %collective-permute-done.7.refs_1_.refs_5_) | copy-start | bytes 2949124
  92.9 18.6 %collective-permute-start.6 = (bf16[192,1280]{1,0:T(8,128)(2,1)S(1)}, bf16[192,1280]{1,0:T(8,128)(2,1)S(1)}, u32[]{:S(2)}, u32[]{:S(2)}) collective-permute-start(bf16[192,1280]{1,0:T(8,128)(2,1)S(1)} %get-tuple-element.107), channel_id=1, source_target_pairs={{0,2},{1,3},{2,0},{3,1},{4,6},{5,7},{6,4},{7,5},{8,10},{9,11},{10,... | collective-permute-start | bytes 1474568 | tf_op jit(solution)/shard_map/ppermute | solution.py:236
  94.5 26.5 %collective-permute-start.13 = (bf16[192,1280]{1,0:T(8,128)(2,1)}, bf16[192,1280]{1,0:T(8,128)(2,1)}, u32[]{:S(2)}, u32[]{:S(2)}) collective-permute-start(bf16[192,1280]{1,0:T(8,128)(2,1)} %get-tuple-element.108), channel_id=1, source_target_pairs={{0,2},{1,3},{2,0},{3,1},{4,6},{5,7},{6,4},{7,5},{8,10},{9,11},{10,... | collective-permute-start | bytes 1474568 | tf_op jit(solution)/shard_map/ppermute | solution.py:236
  109.2 2.9 %copy-start.18 = (bf16[192,2560]{1,0:T(8,128)(2,1)S(1)}, bf16[192,2560]{1,0:T(8,128)(2,1)}, u32[]{:S(2)}) copy-start(bf16[192,2560]{1,0:T(8,128)(2,1)} %get-tuple-element.54) | copy-start | bytes 2949124
  111.5 6.3 %copy-start.17 = (bf16[192,2560]{1,0:T(8,128)(2,1)S(1)}, bf16[192,2560]{1,0:T(8,128)(2,1)}, u32[]{:S(2)}) copy-start(bf16[192,2560]{1,0:T(8,128)(2,1)} %get-tuple-element.66) | copy-start | bytes 2949124
  111.5 6.3 %collective-permute-start.8 = (bf16[96,2560]{1,0:T(8,128)(2,1)}, bf16[96,2560]{1,0:T(8,128)(2,1)}, u32[]{:S(2)}, u32[]{:S(2)}) collective-permute-start(bf16[96,2560]{1,0:T(8,128)(2,1)} %get-tuple-element.105), channel_id=1, source_target_pairs={{0,1},{1,0},{2,3},{3,2},{4,5},{5,4},{6,7},{7,6},{8,9},{9,8},{10,11... | collective-permute-start | bytes 1474568 | tf_op jit(solution)/shard_map/ppermute | solution.py:236
  111.6 6.3 %collective-permute-start.9 = (bf16[96,2560]{1,0:T(8,128)(2,1)}, bf16[96,2560]{1,0:T(8,128)(2,1)}, u32[]{:S(2)}, u32[]{:S(2)}) collective-permute-start(bf16[96,2560]{1,0:T(8,128)(2,1)} %get-tuple-element.106), channel_id=1, source_target_pairs={{0,1},{1,0},{2,3},{3,2},{4,5},{5,4},{6,7},{7,6},{8,9},{9,8},{10,11... | collective-permute-start | bytes 1474568 | tf_op jit(solution)/shard_map/ppermute | solution.py:236
  112.1 1.1 copy-start.19
  113.2 18.8 %all-to-all-start.2 = ((bf16[8,24,1280]{2,1,0:T(8,128)(2,1)}), bf16[8,24,1280]{2,1,0:T(8,128)(2,1)}, u32[]{:S(2)}, u32[]{:S(2)}) async-start(bf16[8,24,1280]{2,1,0:T(8,128)(2,1)} %bitcast.8), calls=%async_computation.2 | async-start | bytes 983040 | tf_op jit(solution)/shard_map/all_to_all | solution.py:288
  119.4 32.9 %collective-permute-start.11 = (bf16[192,2560]{1,0:T(8,128)(2,1)S(1)}, bf16[192,2560]{1,0:T(8,128)(2,1)}, u32[]{:S(2)}, u32[]{:S(2)}) collective-permute-start(bf16[192,2560]{1,0:T(8,128)(2,1)S(1)} %pad_maximum_fusion.1), channel_id=1, source_target_pairs={{0,2},{1,3},{2,0},{3,1},{4,6},{5,7},{6,4},{7,5},{8,10},{9,11},{10,... | collective-permute-start | bytes 2949128 | tf_op jit(solution)/shard_map/ppermute | solution.py:236
  134.3 24.4 %all-to-all-start.3 = ((bf16[8,24,1280]{2,1,0:T(8,128)(2,1)}), bf16[8,24,1280]{2,1,0:T(8,128)(2,1)}, u32[]{:S(2)}, u32[]{:S(2)}) async-start(bf16[8,24,1280]{2,1,0:T(8,128)(2,1)} %bitcast.10), calls=%async_computation.3 | async-start | bytes 983040 | tf_op jit(solution)/shard_map/all_to_all | solution.py:288
  138.6 13.7 %copy-start.22 = (f32[1,2560]{1,0:T(1,128)S(1)}, f32[1,2560]{1,0:T(1,128)}, u32[]{:S(2)}) copy-start(f32[1,2560]{1,0:T(1,128)} %get-tuple-element.84) | copy-start | bytes 30724
  152.2 6.5 %collective-permute-start.12 = (bf16[192,2560]{1,0:T(8,128)(2,1)}, bf16[192,2560]{1,0:T(8,128)(2,1)S(1)}, u32[]{:S(2)}, u32[]{:S(2)}) collective-permute-start(bf16[192,2560]{1,0:T(8,128)(2,1)} %get-tuple-element.80), channel_id=1, source_target_pairs={{0,1},{1,0},{2,3},{3,2},{4,5},{5,4},{6,7},{7,6},{8,9},{9,8},{10,11... | collective-permute-start | bytes 2949128 | tf_op jit(solution)/shard_map/ppermute | solution.py:236
  153.0 1.8 collective-permute-start.14
  154.9 3.7 %collective-permute-start.15 = (f32[1,2560]{1,0:T(1,128)S(1)}, f32[1,2560]{1,0:T(1,128)S(1)}, u32[]{:S(2)}, u32[]{:S(2)}) collective-permute-start(f32[1,2560]{1,0:T(1,128)S(1)} %add.84), channel_id=1, source_target_pairs={{0,2},{1,3},{2,0},{3,1},{4,6},{5,7},{6,4},{7,5},{8,10},{9,11},{10,... | collective-permute-start | bytes 30728 | tf_op jit(solution)/shard_map/ppermute | solution.py:236
  161.8 8.6 %copy-start.16 = (bf16[192,1024]{1,0:T(8,128)(2,1)S(1)}, bf16[192,1024]{1,0:T(8,128)(2,1)}, u32[]{:S(2)}) copy-start(bf16[192,1024]{1,0:T(8,128)(2,1)} %get-tuple-element.94.refs_7_) | copy-start | bytes 1179652
  161.8 31.7 %all-to-all-start.4 = ((bf16[8,24,2816]{2,1,0:T(8,128)(2,1)}), bf16[8,24,2816]{2,1,0:T(8,128)(2,1)S(1)}, u32[]{:S(2)}, u32[]{:S(2)}) async-start(bf16[8,24,2816]{2,1,0:T(8,128)(2,1)} %pad_maximum_fusion), calls=%async_computation.4 | async-start | bytes 2162688 | tf_op jit(solution)/shard_map/all_to_all | solution.py:288
  167.6 2.7 %copy-start.2 = (bf16[8,24,2560]{2,1,0:T(8,128)(2,1)S(1)}, bf16[8,24,2560]{2,1,0:T(8,128)(2,1)}, u32[]{:S(2)}) copy-start(bf16[8,24,2560]{2,1,0:T(8,128)(2,1)} %copy-done.1) | copy-start | bytes 2949124
  167.6 2.7 %copy-start.6 = (bf16[192,2560]{1,0:T(8,128)(2,1)S(1)}, bf16[192,2560]{1,0:T(8,128)(2,1)}, u32[]{:S(2)}) copy-start(bf16[192,2560]{1,0:T(8,128)(2,1)} %copy-done.5) | copy-start | bytes 2949124
  167.6 2.7 %copy-start.13 = (bf16[192,1024]{1,0:T(8,128)(2,1)S(1)}, bf16[192,1024]{1,0:T(8,128)(2,1)}, u32[]{:S(2)}) copy-start(bf16[192,1024]{1,0:T(8,128)(2,1)} %get-tuple-element.91.refs_4_) | copy-start | bytes 1179652
  167.6 2.7 %copy-start.14 = (bf16[192,1024]{1,0:T(8,128)(2,1)S(1)}, bf16[192,1024]{1,0:T(8,128)(2,1)}, u32[]{:S(2)}) copy-start(bf16[192,1024]{1,0:T(8,128)(2,1)} %get-tuple-element.92.refs_5_) | copy-start | bytes 1179652
  167.7 2.7 %copy-start.15 = (bf16[192,1024]{1,0:T(8,128)(2,1)S(1)}, bf16[192,1024]{1,0:T(8,128)(2,1)}, u32[]{:S(2)}) copy-start(bf16[192,1024]{1,0:T(8,128)(2,1)} %get-tuple-element.93.refs_6_) | copy-start | bytes 1179652
  170.4 8.9 %copy-start.4 = (bf16[8,24,2560]{2,1,0:T(8,128)(2,1)S(1)}, bf16[8,24,2560]{2,1,0:T(8,128)(2,1)}, u32[]{:S(2)}) copy-start(bf16[8,24,2560]{2,1,0:T(8,128)(2,1)} %copy-done.3) | copy-start | bytes 2949124
  170.4 8.9 %copy-start.8 = (bf16[192,2560]{1,0:T(8,128)(2,1)S(1)}, bf16[192,2560]{1,0:T(8,128)(2,1)}, u32[]{:S(2)}) copy-start(bf16[192,2560]{1,0:T(8,128)(2,1)} %copy-done.7) | copy-start | bytes 2949124
  170.4 8.9 %copy-start.9 = (bf16[192,1024]{1,0:T(8,128)(2,1)S(1)}, bf16[192,1024]{1,0:T(8,128)(2,1)}, u32[]{:S(2)}) copy-start(bf16[192,1024]{1,0:T(8,128)(2,1)} %get-tuple-element.95.refs_4_.refs_0_) | copy-start | bytes 1179652
  170.4 8.9 %copy-start.10 = (bf16[192,1024]{1,0:T(8,128)(2,1)S(1)}, bf16[192,1024]{1,0:T(8,128)(2,1)}, u32[]{:S(2)}) copy-start(bf16[192,1024]{1,0:T(8,128)(2,1)} %get-tuple-element.96.refs_5_.refs_1_) | copy-start | bytes 1179652
  170.4 8.9 %copy-start.11 = (bf16[192,1024]{1,0:T(8,128)(2,1)S(1)}, bf16[192,1024]{1,0:T(8,128)(2,1)}, u32[]{:S(2)}) copy-start(bf16[192,1024]{1,0:T(8,128)(2,1)} %get-tuple-element.97.refs_4_.refs_2_) | copy-start | bytes 1179652
  170.5 8.9 %copy-start.12 = (bf16[192,1024]{1,0:T(8,128)(2,1)S(1)}, bf16[192,1024]{1,0:T(8,128)(2,1)}, u32[]{:S(2)}) copy-start(bf16[192,1024]{1,0:T(8,128)(2,1)} %get-tuple-element.98.refs_5_.refs_3_) | copy-start | bytes 1179652

commit v4 on v3

--- a/solution.py
+++ b/solution.py
@@ -324,14 +324,14 @@
         out_home_left = exchange(out_left)
         back_far_sum = sum_low_after(far_term, out_far_left)
         back_far = cross(back_far_sum, top)
-        out_far_right = after(out_far_right, back_far_sum, out_home_left)
-        out_sum = added(*[x[:, cut:] for x in out_near], out_far_right)
-        out_home_right = exchange(out_sum)
 
         near = [after(x, out_left, back_far_sum) for x in gather_low(cot_near)]
         near_hidden_cot, near_term, near_column = backward(
             near, hidden[low:], active[low:], rows[low:], w_up, w_down, column
         )
+        out_far_right = after(out_far_right, back_far_sum, out_home_left, *near_term)
+        out_sum = added(*[x[:, cut:] for x in out_near], out_far_right)
+        out_home_right = exchange(out_sum)
         back_near = sum_low([after(x, back_far) for x in near_term])
         cots, hidden_cot = cots + near, hidden_cot + near_hidden_cot
 
@@ -340,7 +340,7 @@
         while bit < n_tensor:
             columns = columns + cross(columns, bit)
             bit *= 2
-        columns = after(columns, out_home_left, out_home_right)
+        columns = after(columns, out_home_left)
         lanes = -(-width // (most * 128)) * 128
         high = columns.astype(jnp.bfloat16)
         rest = (columns - high.astype(jnp.float32)).astype(jnp.bfloat16)
@@ -352,14 +352,16 @@
             axis=2,
         )
 
-        back_sum = added(back_near, after(back_far, out_home_left, out_home_right))
-
-        up_grad = gradient([after(x, back_sum, columns) for x in rows], hidden_cot, 512)[None]
-        down_grad = gradient([after(x, back_sum, columns) for x in active], cots, 256)[None]
+        back_sum = added(back_near, after(back_far, out_home_left))
 
         back_sum = back_sum.reshape(experts, most, width)
         beside = jnp.broadcast_to(beside, (experts, most, 2 * lanes))
-        came = swap(jnp.concatenate([back_sum, beside], axis=2))
+        ready = after(jnp.concatenate([back_sum, beside], axis=2), out_home_right)
+        came = swap(ready)
+
+        up_grad = gradient([after(x, ready) for x in rows], hidden_cot, 512)[None]
+        down_grad = gradient([after(x, ready) for x in active], cots, 256)[None]
+
         back_home = came.reshape(slots, width + 2 * lanes)
         high, rest = (
             came[:, :, k : k + lanes].reshape(experts, most * lanes)[:, :width].astype(jnp.float32)
@@ -367,7 +369,7 @@
         )
         router_grad = (high + rest).T
 
-        out_home = jnp.concatenate([after(out_home_left, back_sum), out_home_right], axis=1)
+        out_home = jnp.concatenate([after(out_home_left, ready), out_home_right], axis=1)
         out_rows = dot(placing, out_home, jnp.bfloat16, ((0,), (0,)))
         cot_rows = dot(placing, back_home, jnp.bfloat16, ((0,), (0,)))[:, :width]
         out_wide = out_rows.astype(jnp.float32)

time: 197 us -> 204 us (1.036)
  waiting for transfers between devices: 72.1 us -> 82.9 us
  starting transfers between devices: 36 us -> 32.6 us
    ppermute x16, waiting for transfers between devices: 32.3 us -> 41.6 us  [cross(): return lax.ppermute(x, 'tensor', [(i, i ^ bit) for i in range(n_tensor)])]
  transfers between devices with their start and end apart: 21 -> 21, of which waited for: 10 -> 13; matrix products, arithmetic and copies ran while one was open for 8% -> 8% of each run, Pallas kernels for 31% -> 30%
where the time goes in v4:
time: 204 us; the launch traced here: 203 us
  waiting for transfers between devices  82.9 us (41%)
  Pallas kernels  60.1 us (29%)
  starting transfers between devices  32.6 us (16%)
  other arithmetic  12.9 us (6%)
  matrix products  7.38 us (4%)
  local copies, waits for them, and re-layouts  5.29 us (3%)
    ppermute x16, waiting for transfers between devices, cross(): return lax.ppermute(x, 'tensor', [(i, i ^ bit) for i in range(n_tensor)])  41.6 us
    all_to_all x5, waiting for transfers between devices, swap(): return lax.all_to_all(x, 'expert', split_axis=0, concat_axis=0, tiled=True)  41.3 us
    pallas_call x2, Pallas kernels, backward(): call(functools.partial(backward_kernel, n, steps, steps + wides - 1, tile...  27.4 us
    all_to_all x5, starting transfers between devices, swap(): return lax.all_to_all(x, 'expert', split_axis=0, concat_axis=0, tiled=True)  23.9 us
    pallas_call x2, Pallas kernels, gradient(): call(functools.partial(gradient_kernel, len(lefts)), height // tile, [pl....  17.6 us
    pallas_call x1, Pallas kernels, forward(): call(functools.partial(forward_kernel, n, steps, tile), steps + wides, [w...  15.2 us
    ppermute x16, starting transfers between devices, cross(): return lax.ppermute(x, 'tensor', [(i, i ^ bit) for i in range(n_tensor)])  8.65 us
    dot_general x6, matrix products, dot(): lax.dot_general(a, b, (dims, ((), ())), preferred_element_type=jnp.float32)  7.38 us
  transfers between devices with their start and end apart: 21, of which 13 were waited for; matrix products, arithmetic and copies ran while one was open for 8% of the time, Pallas kernels for 30%

profile of v4, /device:TPU:0, one launch (start us, length us, event | category | flops | bytes accessed | tf_op | source)
XLA Modules:
  0.0 203.0 jit_solution(6342619971593892937)
XLA Ops:
  0.6 0.0 copy-start
  1.4 0.7 fusion.16
  2.0 0.1 copy.12
  2.1 0.2 reduce_window_sum.11
  2.4 0.7 select_reduce_fusion
  3.1 0.7 compare_select_fusion
  3.7 1.4 convolution_convert_fusion.1
  5.1 7.3 %all-to-all-start = ((bf16[8,24,2560]{2,1,0:T(8,128)(2,1)}), bf16[8,24,2560]{2,1,0:T(8,128)(2,1)S(1)}, u32[]{:S(2)}, u32[]{:S(2)}) async-start(bf16[8,24,2560]{2,1,0:T(8,128)(2,1)} %bitcast.2), calls=%async_computation | async-start | bytes 1966080 | tf_op jit(solution)/shard_map/all_to_all | solution.py:288
  12.3 0.3 fusion.5
  12.6 1.5 convolution_convert_fusion
  14.1 22.6 %all-to-all-done = bf16[8,24,2560]{2,1,0:T(8,128)(2,1)S(1)} async-done(((bf16[8,24,2560]{2,1,0:T(8,128)(2,1)}), bf16[8,24,2560]{2,1,0:T(8,128)(2,1)S(1)}, u32[]{:S(2)}, u32[]{:S(2)}) %all-to-all-start) | async-done | bytes 983072 | tf_op jit(solution)/shard_map/all_to_all | solution.py:288
  36.7 3.6 %all-to-all-start.1 = ((bf16[8,24,2560]{2,1,0:T(8,128)(2,1)}), bf16[8,24,2560]{2,1,0:T(8,128)(2,1)S(1)}, u32[]{:S(2)}, u32[]{:S(2)}) async-start(bf16[8,24,2560]{2,1,0:T(8,128)(2,1)} %bitcast.55), calls=%async_computation.1 | async-start | bytes 1966080 | tf_op jit(solution)/shard_map/all_to_all | solution.py:288
  40.3 1.6 collective-permute-start
  41.9 21.9 %collective-permute-done.refs_0_.refs_6_ = bf16[192,2560]{1,0:T(8,128)(2,1)} collective-permute-done((bf16[192,2560]{1,0:T(8,128)(2,1)S(1)}, bf16[192,2560]{1,0:T(8,128)(2,1)}, u32[]{:S(2)}, u32[]{:S(2)}) %collective-permute-start) | collective-permute-done | bytes 983072 | tf_op jit(solution)/shard_map/ppermute | solution.py:236
  63.8 1.0 all-to-all-done.1
  64.8 1.5 collective-permute-start.5
  66.4 1.3 collective-permute-done.1.refs_1_.refs_7_
  67.6 0.9 copy-done.5
  68.6 15.2 %shard_map.110 = (f32[192,1024]{1,0:T(8,128)}, f32[192,1024]{1,0:T(8,128)}, f32[192,1024]{1,0:T(8,128)}, f32[192,1024]{1,0:T(8,128)}, bf16[192,1024]{1,0:T(8,128...) custom-call(bf16[192,2560]{1,0:T(8,128)(2,1)} %collective-permute-do, ...), custom_call_target="tpu_custom_call" | custom-call | flops 1 | bytes 1 | tf_op jit(solution)/shard_map/pallas_call | solution.py:157
  83.7 0.2 collective-permute-start.4
  83.9 5.2 %collective-permute-done.5.refs_0_.refs_4_ = bf16[192,2560]{1,0:T(8,128)(2,1)} collective-permute-done((bf16[192,2560]{1,0:T(8,128)(2,1)S(1)}, bf16[192,2560]{1,0:T(8,128)(2,1)}, u32[]{:S(2)}, u32[]{:S(2)}) %collective-permute-start.5) | collective-permute-done | bytes 983072 | tf_op jit(solution)/shard_map/ppermute | solution.py:236
  89.2 1.7 add_convert_fusion.2
  90.9 1.0 collective-permute-done.7.refs_1_.refs_5_
  91.9 0.9 fusion.20
  92.8 1.5 collective-permute-start.6
  94.3 0.6 broadcast_in_dim.15.refs_10_
  95.0 13.6 %shard_map.111 = (bf16[192,1024]{1,0:T(8,128)(2,1)}, bf16[192,1024]{1,0:T(8,128)(2,1)}, bf16[192,2560]{1,0:T(8,128)(2,1)}, bf16[192,2560]{1,0:T(8,128)(2,1)}, f32[1,2560]{1,0:T(1,128)}) custom-call(bf16[192,2560]{1,0:T(8,128)(2,1)} %collective-permute-done.5.refs_0_.refs_4_, bf16[192,2560]{1,0:T(8,128)(2,1)} %copy-done.7, ...), custom_call_target="tpu_custom_call" | custom-call | flops 1 | bytes 1 | tf_op jit(solution)/shard_map/pallas_call | solution.py:183
  108.6 1.4 fusion.19
  110.0 0.1 collective-permute-start.8
  110.1 0.5 collective-permute-start.9
  110.6 0.1 collective-permute-start.10
  110.7 0.4 collective-permute-start.3
  111.1 0.8 collective-permute-done.8
  111.9 0.7 collective-permute-done.9
  112.7 0.2 add_convert_fusion.5
  112.9 1.0 pad_maximum_fusion.1
  113.9 0.5 collective-permute-start.11
  114.4 1.0 collective-permute-done.3
  115.5 1.1 add_convert_fusion.6
  116.6 4.7 %all-to-all-start.2 = ((bf16[8,24,1280]{2,1,0:T(8,128)(2,1)}), bf16[8,24,1280]{2,1,0:T(8,128)(2,1)}, u32[]{:S(2)}, u32[]{:S(2)}) async-start(bf16[8,24,1280]{2,1,0:T(8,128)(2,1)} %bitcast.8), calls=%async_computation.2 | async-start | bytes 983040 | tf_op jit(solution)/shard_map/all_to_all | solution.py:288
  121.2 0.5 collective-permute-start.15
  121.8 1.0 copy-done.9
  122.7 13.8 %shard_map.112 = (bf16[192,1024]{1,0:T(8,128)(2,1)}, bf16[192,1024]{1,0:T(8,128)(2,1)}, bf16[192,2560]{1,0:T(8,128)(2,1)}, bf16[192,2560]{1,0:T(8,128)(2,1)}, f32[1,2560]{1,0:T(1,128)}) custom-call(bf16[192,2560]{1,0:T(8,128)(2,1)} %bitcast.46, bf16[192,2560]{1,0:T(8,128)(2,1)} %copy-done.9, f32[192,1024]{1,0:T(8,128)} %get-tuple-element.74.refs_2_, ...), custom_call_target="tpu_custom_call" | custom-call | flops 1 | bytes 1 | tf_op jit(solution)/shard_map/pallas_call | solution.py:183
  136.5 0.8 add.81
  137.3 0.1 collective-permute-start.13
  137.4 1.2 collective-permute-done.13
  138.6 1.6 collective-permute-start.14
  140.1 8.5 %collective-permute-done.14 = f32[1,2560]{1,0:T(1,128)S(1)} collective-permute-done((f32[1,2560]{1,0:T(1,128)S(1)}, f32[1,2560]{1,0:T(1,128)S(1)}, u32[]{:S(2)}, u32[]{:S(2)}) %collective-permute-start.14) | collective-permute-done | bytes 10272 | tf_op jit(solution)/shard_map/ppermute | solution.py:236
  148.7 0.1 collective-permute-start.12
  148.8 2.1 %add_convert_fusion.3 = bf16[192,1280]{1,0:T(8,128)(2,1)} fusion(bf16[192,1280]{1,0:T(8,128)(2,1)} %collective-permute-done.15, bf16[192,2560]{1,0:T(8,128)(2,1)} %copy-done.22, bf16[192,2560]{1,0:T(8,128)(2,1)S(1)} %copy-done.21), kind=kLoop, calls=%fused_computation.23 | loop fusion | flops 1474560 | bytes 1966080 | tf_op jit(solution)/shard_map/convert_element_type | solution.py:24
  151.0 4.7 %all-to-all-start.3 = ((bf16[8,24,1280]{2,1,0:T(8,128)(2,1)}), bf16[8,24,1280]{2,1,0:T(8,128)(2,1)}, u32[]{:S(2)}, u32[]{:S(2)}) async-start(bf16[8,24,1280]{2,1,0:T(8,128)(2,1)} %bitcast.12), calls=%async_computation.3 | async-start | bytes 983040 | tf_op jit(solution)/shard_map/all_to_all | solution.py:288
  155.7 0.1 pad_reduce_fusion
  155.8 1.9 add_convert_fusion
  157.6 1.1 pad_maximum_fusion
  158.7 11.5 %all-to-all-done.3 = bf16[8,24,1280]{2,1,0:T(8,128)(2,1)} async-done(((bf16[8,24,1280]{2,1,0:T(8,128)(2,1)}), bf16[8,24,1280]{2,1,0:T(8,128)(2,1)}, u32[]{:S(2)}, u32[]{:S(2)}) %all-to-all-start.3) | async-done | bytes 491552 | tf_op jit(solution)/shard_map/all_to_all | solution.py:288
  170.2 3.8 %all-to-all-start.4 = ((bf16[8,24,2816]{2,1,0:T(8,128)(2,1)}), bf16[8,24,2816]{2,1,0:T(8,128)(2,1)S(1)}, u32[]{:S(2)}, u32[]{:S(2)}) async-start(bf16[8,24,2816]{2,1,0:T(8,128)(2,1)} %pad_maximum_fusion), calls=%async_computation.4 | async-start | bytes 2162688 | tf_op jit(solution)/shard_map/all_to_all | solution.py:288
  174.0 0.0 copy-start.6
  174.0 2.7 %fusion.4 = (f32[128]{0:T(128)S(1)}, bf16[128,2560]{1,0:T(8,128)(2,1)}) fusion(bf16[128,2560]{1,0:T(8,128)(2,1)S(1)} %copy-done.24, f32[128]{0:T(128)S(1)} %add_divide_fusion, bf16[192,1280]{1,0:T(8,128)(2,1)} %bitcast.13, bf16[192,1280]{1,0:T(8,128)(2,1)} %bitcast.9, s32[128]{0:T(128)S(1)} %compare_select_fusion), kind=kOutput, calls=%fused_computation.13 | convolution fusion | flops 130113408 | bytes 2295296 | tf_op jit(solution)/shard_map/dot_general | solution.py:12
  176.8 8.9 %shard_map.113 = bf16[2560,1024]{1,0:T(8,128)(2,1)} custom-call(bf16[192,2560]{1,0:T(8,128)(2,1)} %collective-permute-done.refs_0_.refs_6_, bf16[192,2560]{1,0:T(8,128)(2,1)S(1)} %copy-done.6, bf16[192,2560]{1,0:T(8,128)(2,1)S(1)} %bitcast.43, bf16[192,2560]{1,0:T(8,128)(2,1)} %collective-permute-done.2.refs_3_.refs_7_, bf16[192,1024]{1,0:T(8,128)(2,1)S(1)} %copy-done.15, ...), custom_call_target="tpu_custom_call" | custom-call | flops 4026531840 | bytes 10747904 | tf_op jit(solution)/shard_map/pallas_call | solution.py:220
  185.7 8.7 %shard_map.114 = bf16[1024,2560]{1,0:T(8,128)(2,1)} custom-call(bf16[192,1024]{1,0:T(8,128)(2,1)S(1)} %copy-done.11, bf16[192,1024]{1,0:T(8,128)(2,1)S(1)} %copy-done.12, bf16[192,1024]{1,0:T(8,128)(2,1)S(1)} %copy-done.13, bf16[192,1024]{1,0:T(8,128)(2,1)S(1)} %copy-done.14, bf16[192,2560]{1,0:T(8,128)(2,1)} %collective-permute-done.5.refs_0_.refs_4_, ...), custom_call_target="tpu_custom_call" | custom-call | flops 4026531840 | bytes 10747904 | tf_op jit(solution)/shard_map/pallas_call | solution.py:220
  194.4 6.2 %all-to-all-done.4 = bf16[8,24,2816]{2,1,0:T(8,128)(2,1)S(1)} async-done(((bf16[8,24,2816]{2,1,0:T(8,128)(2,1)}), bf16[8,24,2816]{2,1,0:T(8,128)(2,1)S(1)}, u32[]{:S(2)}, u32[]{:S(2)}) %all-to-all-start.4) | async-done | bytes 1081376 | tf_op jit(solution)/shard_map/all_to_all | solution.py:288
  200.7 0.4 fusion.11
  201.1 0.6 add_bitcast_fusion
  201.7 1.2 fusion.1
  (77 shorter events, 0.4 us)
Async XLA Ops:
  0.6 3.1 %copy-start = (bf16[128,2560]{1,0:T(8,128)(2,1)S(1)}, bf16[128,2560]{1,0:T(8,128)(2,1)}, u32[]{:S(2)}) copy-start(bf16[128,2560]{1,0:T(8,128)(2,1)} %param.7) | copy-start | bytes 1966084
  0.6 11.7 %copy-start.27 = (s32[128,1]{0,1:T(1,128)S(1)}, s32[128,1]{0,1:T(1,128)}, u32[]{:S(2)}) copy-start(s32[128,1]{0,1:T(1,128)} %param.8) | copy-start | bytes 1540
  0.7 11.7 %copy-start.25 = (bf16[2560,8]{0,1:T(8,128)(2,1)S(1)}, bf16[2560,8]{0,1:T(8,128)(2,1)}, u32[]{:S(2)}) copy-start(bf16[2560,8]{0,1:T(8,128)(2,1)} %param.10) | copy-start | bytes 122884
  3.7 8.9 %copy-start.24 = (bf16[128,2560]{1,0:T(8,128)(2,1)S(1)}, bf16[128,2560]{1,0:T(8,128)(2,1)}, u32[]{:S(2)}) copy-start(bf16[128,2560]{1,0:T(8,128)(2,1)} %param.13) | copy-start | bytes 1966084
  5.1 31.6 %all-to-all-start = ((bf16[8,24,2560]{2,1,0:T(8,128)(2,1)}), bf16[8,24,2560]{2,1,0:T(8,128)(2,1)S(1)}, u32[]{:S(2)}, u32[]{:S(2)}) async-start(bf16[8,24,2560]{2,1,0:T(8,128)(2,1)} %bitcast.2), calls=%async_computation | async-start | bytes 1966080 | tf_op jit(solution)/shard_map/all_to_all | solution.py:288
  36.7 30.9 %copy-start.1 = (bf16[8,24,2560]{2,1,0:T(8,128)(2,1)}, bf16[8,24,2560]{2,1,0:T(8,128)(2,1)S(1)}, u32[]{:S(2)}) copy-start(bf16[8,24,2560]{2,1,0:T(8,128)(2,1)S(1)} %all-to-all-done) | copy-start | bytes 2949124
  36.7 28.1 %all-to-all-start.1 = ((bf16[8,24,2560]{2,1,0:T(8,128)(2,1)}), bf16[8,24,2560]{2,1,0:T(8,128)(2,1)S(1)}, u32[]{:S(2)}, u32[]{:S(2)}) async-start(bf16[8,24,2560]{2,1,0:T(8,128)(2,1)} %bitcast.55), calls=%async_computation.1 | async-start | bytes 1966080 | tf_op jit(solution)/shard_map/all_to_all | solution.py:288
  40.3 23.5 %collective-permute-start = (bf16[192,2560]{1,0:T(8,128)(2,1)S(1)}, bf16[192,2560]{1,0:T(8,128)(2,1)}, u32[]{:S(2)}, u32[]{:S(2)}) collective-permute-start(bf16[192,2560]{1,0:T(8,128)(2,1)S(1)} %bitcast.39), channel_id=1, source_target_pairs={{0,2},{1,3},{2,0},{3,1},{4,6},{5,7},{6,4},{7,5},{8,10},{9,11},{10,... | collective-permute-start | bytes 2949128 | tf_op jit(solution)/shard_map/ppermute | solution.py:236
  41.9 24.5 %collective-permute-start.2 = (bf16[192,2560]{1,0:T(8,128)(2,1)S(1)}, bf16[192,2560]{1,0:T(8,128)(2,1)}, u32[]{:S(2)}, u32[]{:S(2)}) collective-permute-start(bf16[192,2560]{1,0:T(8,128)(2,1)S(1)} %bitcast.40), channel_id=1, source_target_pairs={{0,1},{1,0},{2,3},{3,2},{4,5},{5,4},{6,7},{7,6},{8,9},{9,8},{10,11... | collective-permute-start | bytes 2949128 | tf_op jit(solution)/shard_map/ppermute | solution.py:236
  64.8 45.8 %copy-start.3 = (bf16[8,24,2560]{2,1,0:T(8,128)(2,1)}, bf16[8,24,2560]{2,1,0:T(8,128)(2,1)S(1)}, u32[]{:S(2)}) copy-start(bf16[8,24,2560]{2,1,0:T(8,128)(2,1)S(1)} %all-to-all-done.1) | copy-start | bytes 2949124
  64.8 2.8 %collective-permute-start.1 = (bf16[192,2560]{1,0:T(8,128)(2,1)}, bf16[192,2560]{1,0:T(8,128)(2,1)S(1)}, u32[]{:S(2)}, u32[]{:S(2)}) collective-permute-start(bf16[192,2560]{1,0:T(8,128)(2,1)} %collective-permute-done.refs_0_.refs_6_), channel_id=1, source_target_pairs={{0,1},{1,0},{2,3},{3,2},{4,5},{5,4},{6,7},{7,6},{8,9},{9,8},{10,11... | collective-permute-start | bytes 2949128 | tf_op jit(solution)/shard_map/ppermute | solution.py:236
  64.8 24.3 %collective-permute-start.5 = (bf16[192,2560]{1,0:T(8,128)(2,1)S(1)}, bf16[192,2560]{1,0:T(8,128)(2,1)}, u32[]{:S(2)}, u32[]{:S(2)}) collective-permute-start(bf16[192,2560]{1,0:T(8,128)(2,1)S(1)} %bitcast.44), channel_id=1, source_target_pairs={{0,2},{1,3},{2,0},{3,1},{4,6},{5,7},{6,4},{7,5},{8,10},{9,11},{10,... | collective-permute-start | bytes 2949128 | tf_op jit(solution)/shard_map/ppermute | solution.py:236
  67.6 0.9 copy-start.5
  83.7 5.4 %collective-permute-start.4 = (bf16[192,2560]{1,0:T(8,128)(2,1)}, bf16[192,2560]{1,0:T(8,128)(2,1)}, u32[]{:S(2)}, u32[]{:S(2)}) collective-permute-start(bf16[192,2560]{1,0:T(8,128)(2,1)} %get-tuple-element.58), channel_id=1, source_target_pairs={{0,1},{1,0},{2,3},{3,2},{4,5},{5,4},{6,7},{7,6},{8,9},{9,8},{10,11... | collective-permute-start | bytes 2949128 | tf_op jit(solution)/shard_map/ppermute | solution.py:236
  89.1 2.8 %collective-permute-start.7 = (bf16[192,2560]{1,0:T(8,128)(2,1)}, bf16[192,2560]{1,0:T(8,128)(2,1)S(1)}, u32[]{:S(2)}, u32[]{:S(2)}) collective-permute-start(bf16[192,2560]{1,0:T(8,128)(2,1)} %collective-permute-done.5.refs_0_.refs_4_), channel_id=1, source_target_pairs={{0,1},{1,0},{2,3},{3,2},{4,5},{5,4},{6,7},{7,6},{8,9},{9,8},{10,11... | collective-permute-start | bytes 2949128 | tf_op jit(solution)/shard_map/ppermute | solution.py:236
  91.9 3.1 %copy-start.7 = (bf16[192,2560]{1,0:T(8,128)(2,1)}, bf16[192,2560]{1,0:T(8,128)(2,1)S(1)}, u32[]{:S(2)}) copy-start(bf16[192,2560]{1,0:T(8,128)(2,1)S(1)} %collective-permute-done.7.refs_1_.refs_5_) | copy-start | bytes 2949124
  92.8 18.3 %collective-permute-start.6 = (bf16[192,1280]{1,0:T(8,128)(2,1)S(1)}, bf16[192,1280]{1,0:T(8,128)(2,1)S(1)}, u32[]{:S(2)}, u32[]{:S(2)}) collective-permute-start(bf16[192,1280]{1,0:T(8,128)(2,1)S(1)} %get-tuple-element.109), channel_id=1, source_target_pairs={{0,2},{1,3},{2,0},{3,1},{4,6},{5,7},{6,4},{7,5},{8,10},{9,11},{10,... | collective-permute-start | bytes 1474568 | tf_op jit(solution)/shard_map/ppermute | solution.py:236
  108.6 2.1 %copy-start.28 = (bf16[192,2560]{1,0:T(8,128)(2,1)S(1)}, bf16[192,2560]{1,0:T(8,128)(2,1)}, u32[]{:S(2)}) copy-start(bf16[192,2560]{1,0:T(8,128)(2,1)} %get-tuple-element.56) | copy-start | bytes 2949124
  108.6 4.0 %copy-start.19 = (bf16[192,2560]{1,0:T(8,128)(2,1)S(1)}, bf16[192,2560]{1,0:T(8,128)(2,1)}, u32[]{:S(2)}) copy-start(bf16[192,2560]{1,0:T(8,128)(2,1)} %get-tuple-element.67) | copy-start | bytes 2949124
  110.0 1.9 collective-permute-start.8
  110.1 2.6 %collective-permute-start.9 = (bf16[96,2560]{1,0:T(8,128)(2,1)S(1)}, bf16[96,2560]{1,0:T(8,128)(2,1)S(1)}, u32[]{:S(2)}, u32[]{:S(2)}) collective-permute-start(bf16[96,2560]{1,0:T(8,128)(2,1)S(1)} %get-tuple-element.108), channel_id=1, source_target_pairs={{0,1},{1,0},{2,3},{3,2},{4,5},{5,4},{6,7},{7,6},{8,9},{9,8},{10,11... | collective-permute-start | bytes 1474568 | tf_op jit(solution)/shard_map/ppermute | solution.py:236
  110.6 11.2 %collective-permute-start.10 = (bf16[192,2560]{1,0:T(8,128)(2,1)S(1)}, bf16[192,2560]{1,0:T(8,128)(2,1)S(1)}, u32[]{:S(2)}, u32[]{:S(2)}) collective-permute-start(bf16[192,2560]{1,0:T(8,128)(2,1)S(1)} %bitcast.45), channel_id=1, source_target_pairs={{0,1},{1,0},{2,3},{3,2},{4,5},{5,4},{6,7},{7,6},{8,9},{9,8},{10,11... | collective-permute-start | bytes 2949128 | tf_op jit(solution)/shard_map/ppermute | solution.py:236
  110.7 4.8 %collective-permute-start.3 = (bf16[192,2560]{1,0:T(8,128)(2,1)S(1)}, bf16[192,2560]{1,0:T(8,128)(2,1)S(1)}, u32[]{:S(2)}, u32[]{:S(2)}) collective-permute-start(bf16[192,2560]{1,0:T(8,128)(2,1)S(1)} %copy-done.28), channel_id=1, source_target_pairs={{0,1},{1,0},{2,3},{3,2},{4,5},{5,4},{6,7},{7,6},{8,9},{9,8},{10,11... | collective-permute-start | bytes 2949128 | tf_op jit(solution)/shard_map/ppermute | solution.py:236
  111.1 4.4 %copy-start.20 = (bf16[192,2560]{1,0:T(8,128)(2,1)S(1)}, bf16[192,2560]{1,0:T(8,128)(2,1)}, u32[]{:S(2)}) copy-start(bf16[192,2560]{1,0:T(8,128)(2,1)} %get-tuple-element.55) | copy-start | bytes 2949124
  113.9 34.8 %collective-permute-start.11 = (bf16[192,2560]{1,0:T(8,128)(2,1)}, bf16[192,2560]{1,0:T(8,128)(2,1)}, u32[]{:S(2)}, u32[]{:S(2)}) collective-permute-start(bf16[192,2560]{1,0:T(8,128)(2,1)} %pad_maximum_fusion.1), channel_id=1, source_target_pairs={{0,2},{1,3},{2,0},{3,1},{4,6},{5,7},{6,4},{7,5},{8,10},{9,11},{10,... | collective-permute-start | bytes 2949128 | tf_op jit(solution)/shard_map/ppermute | solution.py:236
  115.5 1.1 copy-start.22
  116.6 32.1 %all-to-all-start.2 = ((bf16[8,24,1280]{2,1,0:T(8,128)(2,1)}), bf16[8,24,1280]{2,1,0:T(8,128)(2,1)}, u32[]{:S(2)}, u32[]{:S(2)}) async-start(bf16[8,24,1280]{2,1,0:T(8,128)(2,1)} %bitcast.8), calls=%async_computation.2 | async-start | bytes 983040 | tf_op jit(solution)/shard_map/all_to_all | solution.py:288
  121.2 27.5 %collective-permute-start.15 = (bf16[192,1280]{1,0:T(8,128)(2,1)}, bf16[192,1280]{1,0:T(8,128)(2,1)}, u32[]{:S(2)}, u32[]{:S(2)}) collective-permute-start(bf16[192,1280]{1,0:T(8,128)(2,1)} %get-tuple-element.110), channel_id=1, source_target_pairs={{0,2},{1,3},{2,0},{3,1},{4,6},{5,7},{6,4},{7,5},{8,10},{9,11},{10,... | collective-permute-start | bytes 1474568 | tf_op jit(solution)/shard_map/ppermute | solution.py:236
  121.8 1.0 copy-start.9
  122.7 13.8 %copy-start.26 = (f32[1,2560]{1,0:T(1,128)S(1)}, f32[1,2560]{1,0:T(1,128)}, u32[]{:S(2)}) copy-start(f32[1,2560]{1,0:T(1,128)} %get-tuple-element.83) | copy-start | bytes 30724
  122.7 26.1 %copy-start.21 = (bf16[192,2560]{1,0:T(8,128)(2,1)S(1)}, bf16[192,2560]{1,0:T(8,128)(2,1)}, u32[]{:S(2)}) copy-start(bf16[192,2560]{1,0:T(8,128)(2,1)} %get-tuple-element.55) | copy-start | bytes 2949124
  136.5 19.3 %copy-start.23 = (bf16[192,2560]{1,0:T(8,128)(2,1)S(1)}, bf16[192,2560]{1,0:T(8,128)(2,1)}, u32[]{:S(2)}) copy-start(bf16[192,2560]{1,0:T(8,128)(2,1)} %get-tuple-element.79) | copy-start | bytes 2949124
  137.3 1.2 collective-permute-start.13
  138.6 10.1 %collective-permute-start.14 = (f32[1,2560]{1,0:T(1,128)S(1)}, f32[1,2560]{1,0:T(1,128)S(1)}, u32[]{:S(2)}, u32[]{:S(2)}) collective-permute-start(f32[1,2560]{1,0:T(1,128)S(1)} %add.82), channel_id=1, source_target_pairs={{0,2},{1,3},{2,0},{3,1},{4,6},{5,7},{6,4},{7,5},{8,10},{9,11},{10,... | collective-permute-start | bytes 30728 | tf_op jit(solution)/shard_map/ppermute | solution.py:236
  148.7 7.0 %collective-permute-start.12 = (bf16[192,2560]{1,0:T(8,128)(2,1)}, bf16[192,2560]{1,0:T(8,128)(2,1)}, u32[]{:S(2)}, u32[]{:S(2)}) collective-permute-start(bf16[192,2560]{1,0:T(8,128)(2,1)} %get-tuple-element.81), channel_id=1, source_target_pairs={{0,1},{1,0},{2,3},{3,2},{4,5},{5,4},{6,7},{7,6},{8,9},{9,8},{10,11... | collective-permute-start | bytes 2949128 | tf_op jit(solution)/shard_map/ppermute | solution.py:236
  151.0 19.2 %all-to-all-start.3 = ((bf16[8,24,1280]{2,1,0:T(8,128)(2,1)}), bf16[8,24,1280]{2,1,0:T(8,128)(2,1)}, u32[]{:S(2)}, u32[]{:S(2)}) async-start(bf16[8,24,1280]{2,1,0:T(8,128)(2,1)} %bitcast.12), calls=%async_computation.3 | async-start | bytes 983040 | tf_op jit(solution)/shard_map/all_to_all | solution.py:288
  170.2 6.5 %copy-start.18 = (bf16[192,1024]{1,0:T(8,128)(2,1)S(1)}, bf16[192,1024]{1,0:T(8,128)(2,1)}, u32[]{:S(2)}) copy-start(bf16[192,1024]{1,0:T(8,128)(2,1)} %get-tuple-element.96.refs_7_) | copy-start | bytes 1179652
  170.2 30.4 %all-to-all-start.4 = ((bf16[8,24,2816]{2,1,0:T(8,128)(2,1)}), bf16[8,24,2816]{2,1,0:T(8,128)(2,1)S(1)}, u32[]{:S(2)}, u32[]{:S(2)}) async-start(bf16[8,24,2816]{2,1,0:T(8,128)(2,1)} %pad_maximum_fusion), calls=%async_computation.4 | async-start | bytes 2162688 | tf_op jit(solution)/shard_map/all_to_all | solution.py:288
  174.0 2.7 %copy-start.2 = (bf16[8,24,2560]{2,1,0:T(8,128)(2,1)S(1)}, bf16[8,24,2560]{2,1,0:T(8,128)(2,1)}, u32[]{:S(2)}) copy-start(bf16[8,24,2560]{2,1,0:T(8,128)(2,1)} %copy-done.1) | copy-start | bytes 2949124
  174.0 2.7 %copy-start.6 = (bf16[192,2560]{1,0:T(8,128)(2,1)S(1)}, bf16[192,2560]{1,0:T(8,128)(2,1)}, u32[]{:S(2)}) copy-start(bf16[192,2560]{1,0:T(8,128)(2,1)} %copy-done.5) | copy-start | bytes 2949124
  174.0 2.7 %copy-start.15 = (bf16[192,1024]{1,0:T(8,128)(2,1)S(1)}, bf16[192,1024]{1,0:T(8,128)(2,1)}, u32[]{:S(2)}) copy-start(bf16[192,1024]{1,0:T(8,128)(2,1)} %get-tuple-element.93.refs_4_) | copy-start | bytes 1179652
  174.0 2.7 %copy-start.16 = (bf16[192,1024]{1,0:T(8,128)(2,1)S(1)}, bf16[192,1024]{1,0:T(8,128)(2,1)}, u32[]{:S(2)}) copy-start(bf16[192,1024]{1,0:T(8,128)(2,1)} %get-tuple-element.94.refs_5_) | copy-start | bytes 1179652
  174.0 2.7 %copy-start.17 = (bf16[192,1024]{1,0:T(8,128)(2,1)S(1)}, bf16[192,1024]{1,0:T(8,128)(2,1)}, u32[]{:S(2)}) copy-start(bf16[192,1024]{1,0:T(8,128)(2,1)} %get-tuple-element.95.refs_6_) | copy-start | bytes 1179652
  176.7 8.9 %copy-start.4 = (bf16[8,24,2560]{2,1,0:T(8,128)(2,1)S(1)}, bf16[8,24,2560]{2,1,0:T(8,128)(2,1)}, u32[]{:S(2)}) copy-start(bf16[8,24,2560]{2,1,0:T(8,128)(2,1)} %copy-done.3) | copy-start | bytes 2949124
  176.7 8.9 %copy-start.8 = (bf16[192,2560]{1,0:T(8,128)(2,1)S(1)}, bf16[192,2560]{1,0:T(8,128)(2,1)}, u32[]{:S(2)}) copy-start(bf16[192,2560]{1,0:T(8,128)(2,1)} %copy-done.7) | copy-start | bytes 2949124
  176.8 8.9 %copy-start.10 = (bf16[192,2560]{1,0:T(8,128)(2,1)S(1)}, bf16[192,2560]{1,0:T(8,128)(2,1)}, u32[]{:S(2)}) copy-start(bf16[192,2560]{1,0:T(8,128)(2,1)} %copy-done.9) | copy-start | bytes 2949124
  176.8 8.9 %copy-start.11 = (bf16[192,1024]{1,0:T(8,128)(2,1)S(1)}, bf16[192,1024]{1,0:T(8,128)(2,1)}, u32[]{:S(2)}) copy-start(bf16[192,1024]{1,0:T(8,128)(2,1)} %get-tuple-element.97.refs_4_.refs_0_) | copy-start | bytes 1179652
  176.8 8.9 %copy-start.12 = (bf16[192,1024]{1,0:T(8,128)(2,1)S(1)}, bf16[192,1024]{1,0:T(8,128)(2,1)}, u32[]{:S(2)}) copy-start(bf16[192,1024]{1,0:T(8,128)(2,1)} %get-tuple-element.98.refs_5_.refs_1_) | copy-start | bytes 1179652
  176.8 8.9 %copy-start.13 = (bf16[192,1024]{1,0:T(8,128)(2,1)S(1)}, bf16[192,1024]{1,0:T(8,128)(2,1)}, u32[]{:S(2)}) copy-start(bf16[192,1024]{1,0:T(8,128)(2,1)} %get-tuple-element.99.refs_4_.refs_2_) | copy-start | bytes 1179652
  176.8 8.9 %copy-start.14 = (bf16[192,1024]{1,0:T(8,128)(2,1)S(1)}, bf16[192,1024]{1,0:T(8,128)(2,1)}, u32[]{:S(2)}) copy-start(bf16[192,1024]{1,0:T(8,128)(2,1)} %get-tuple-element.100.refs_5_.refs_3_) | copy-start | bytes 1179652

commit v5 on v1

--- a/solution.py
+++ b/solution.py
@@ -315,7 +315,6 @@
         near_hidden_cot, near_term, near_column = backward(
             near, hidden[low:], active[low:], rows[low:], w_up, w_down, column
         )
-        back_near = sum_low([after(x, back_far) for x in near_term])
         cots, hidden_cot = cots + near, hidden_cot + near_hidden_cot
 
         columns = far_column + near_column
@@ -323,6 +322,8 @@
         while bit < n_tensor:
             columns = columns + cross(columns, bit)
             bit *= 2
+        back_far = after(back_far, columns)
+        back_near = sum_low([after(x, back_far) for x in near_term])
         columns = after(columns, out_home)
         lanes = -(-width // (most * 128)) * 128
         high = columns.astype(jnp.bfloat16)

time: 196 us -> 193 us (0.985)
  no operation moved by 1% of the time
where the time goes in v5:
time: 193 us
  waiting for transfers between devices  74.3 us (38%)
  Pallas kernels  60 us (31%)
  starting transfers between devices  29.3 us (15%)
  other arithmetic  13.5 us (7%)
  matrix products  8.74 us (5%)
  local copies, waits for them, and re-layouts  5.09 us (3%)
    ppermute x14, waiting for transfers between devices, cross(): return lax.ppermute(x, 'tensor', [(i, i ^ bit) for i in range(n_tensor)])  44.4 us
    all_to_all x4, waiting for transfers between devices, swap(): return lax.all_to_all(x, 'expert', split_axis=0, concat_axis=0, tiled=True)  30 us
    pallas_call x2, Pallas kernels, backward(): call(functools.partial(backward_kernel, n, steps, steps + wides - 1, tile...  27.3 us
    all_to_all x4, starting transfers between devices, swap(): return lax.all_to_all(x, 'expert', split_axis=0, concat_axis=0, tiled=True)  21.5 us
    pallas_call x2, Pallas kernels, gradient(): call(functools.partial(gradient_kernel, len(lefts)), height // tile, [pl....  17.6 us
    pallas_call x1, Pallas kernels, forward(): call(functools.partial(forward_kernel, n, steps, tile), steps + wides, [w...  15.1 us
    convert_element_type x4, other arithmetic, added(): return (a.astype(jnp.float32) + b.astype(jnp.float32)).astype(jnp.bfloat16)  8.77 us
    dot_general x6, matrix products, dot(): lax.dot_general(a, b, (dims, ((), ())), preferred_element_type=jnp.float32)  8.74 us
  transfers between devices with their start and end apart: 18, of which 10 were waited for; matrix products, arithmetic and copies ran while one was open for 7% of the time, Pallas kernels for 31%

profile of v5, /device:TPU:0, one launch (start us, length us, event | category | flops | bytes accessed | tf_op | source)
XLA Modules:
  0.0 192.5 jit_solution(6106244786247125585)
XLA Ops:
  0.6 0.0 copy-start
  0.6 0.0 copy-start.24
  1.4 0.7 fusion.13
  2.0 0.1 copy.12
  2.1 0.2 reduce_window_sum.11
  2.4 0.7 select_reduce_fusion
  3.1 0.7 compare_select_fusion
  3.7 1.4 convolution_convert_fusion.1
  5.1 7.3 %all-to-all-start = ((bf16[8,24,2560]{2,1,0:T(8,128)(2,1)}), bf16[8,24,2560]{2,1,0:T(8,128)(2,1)S(1)}, u32[]{:S(2)}, u32[]{:S(2)}) async-start(bf16[8,24,2560]{2,1,0:T(8,128)(2,1)} %bitcast.2), calls=%async_computation | async-start | bytes 1966080 | tf_op jit(solution)/shard_map/all_to_all | solution.py:277
  12.3 0.3 fusion.5
  12.6 1.5 convolution_convert_fusion
  14.1 22.6 %all-to-all-done = bf16[8,24,2560]{2,1,0:T(8,128)(2,1)S(1)} async-done(((bf16[8,24,2560]{2,1,0:T(8,128)(2,1)}), bf16[8,24,2560]{2,1,0:T(8,128)(2,1)S(1)}, u32[]{:S(2)}, u32[]{:S(2)}) %all-to-all-start) | async-done | bytes 983072 | tf_op jit(solution)/shard_map/all_to_all | solution.py:277
  36.7 3.6 %all-to-all-start.1 = ((bf16[8,24,2560]{2,1,0:T(8,128)(2,1)}), bf16[8,24,2560]{2,1,0:T(8,128)(2,1)S(1)}, u32[]{:S(2)}, u32[]{:S(2)}) async-start(bf16[8,24,2560]{2,1,0:T(8,128)(2,1)} %bitcast.53), calls=%async_computation.1 | async-start | bytes 1966080 | tf_op jit(solution)/shard_map/all_to_all | solution.py:277
  40.3 1.6 collective-permute-start
  41.9 0.0 collective-permute-start.2
  41.9 21.9 %collective-permute-done.refs_0_.refs_6_ = bf16[192,2560]{1,0:T(8,128)(2,1)} collective-permute-done((bf16[192,2560]{1,0:T(8,128)(2,1)S(1)}, bf16[192,2560]{1,0:T(8,128)(2,1)}, u32[]{:S(2)}, u32[]{:S(2)}) %collective-permute-start) | collective-permute-done | bytes 983072 | tf_op jit(solution)/shard_map/ppermute | solution.py:236
  63.8 1.0 all-to-all-done.1
  64.8 0.0 collective-permute-start.1
  64.8 1.5 collective-permute-start.5
  66.4 1.3 collective-permute-done.1.refs_1_.refs_7_
  67.6 0.9 copy-done.5
  68.6 15.1 %shard_map.110 = (f32[192,1024]{1,0:T(8,128)}, f32[192,1024]{1,0:T(8,128)}, f32[192,1024]{1,0:T(8,128)}, f32[192,1024]{1,0:T(8,128)}, bf16[192,1024]{1,0:T(8,128...) custom-call(bf16[192,2560]{1,0:T(8,128)(2,1)} %collective-permute-do, ...), custom_call_target="tpu_custom_call" | custom-call | flops 1 | bytes 1 | tf_op jit(solution)/shard_map/pallas_call | solution.py:157
  83.7 0.2 collective-permute-start.4
  83.9 5.2 %collective-permute-done.5.refs_0_.refs_4_ = bf16[192,2560]{1,0:T(8,128)(2,1)} collective-permute-done((bf16[192,2560]{1,0:T(8,128)(2,1)S(1)}, bf16[192,2560]{1,0:T(8,128)(2,1)}, u32[]{:S(2)}, u32[]{:S(2)}) %collective-permute-start.5) | collective-permute-done | bytes 983072 | tf_op jit(solution)/shard_map/ppermute | solution.py:236
  89.1 0.0 collective-permute-start.7
  89.1 0.0 collective-permute-done.4
  89.1 2.4 %add_convert_fusion.4 = bf16[192,2560]{1,0:T(8,128)(2,1)} fusion(bf16[192,2560]{1,0:T(8,128)(2,1)S(1)} %collective-permute-done.4, bf16[192,2560]{1,0:T(8,128)(2,1)} %get-tuple-element.55), kind=kLoop, calls=%fused_computation.11 | loop fusion | flops 1966080 | bytes 2949120 | tf_op jit(solution)/shard_map/convert_element_type | solution.py:24
  91.5 1.5 collective-permute-start.6
  93.0 0.2 collective-permute-start.3
  93.3 0.0 collective-permute-done.7.refs_1_.refs_5_
  93.3 0.7 broadcast_in_dim.15.refs_10_
  94.0 0.3 copy-done.7
  94.3 13.7 %shard_map.111 = (bf16[192,1024]{1,0:T(8,128)(2,1)}, bf16[192,1024]{1,0:T(8,128)(2,1)}, bf16[192,2560]{1,0:T(8,128)(2,1)}, bf16[192,2560]{1,0:T(8,128)(2,1)}, f32[1,2560]{1,0:T(1,128)}) custom-call(bf16[192,2560]{1,0:T(8,128)(2,1)} %collective-permute-done.5.refs_0_.refs_4_, bf16[192,2560]{1,0:T(8,128)(2,1)} %copy-done.7, ...), custom_call_target="tpu_custom_call" | custom-call | flops 1 | bytes 1 | tf_op jit(solution)/shard_map/pallas_call | solution.py:183
  108.0 0.3 collective-permute-start.8
  108.3 0.2 collective-permute-start.9
  108.5 7.4 %collective-permute-done.6 = bf16[192,2560]{1,0:T(8,128)(2,1)} collective-permute-done((bf16[192,2560]{1,0:T(8,128)(2,1)}, bf16[192,2560]{1,0:T(8,128)(2,1)}, u32[]{:S(2)}, u32[]{:S(2)}) %collective-permute-start.6) | collective-permute-done | bytes 983072 | tf_op jit(solution)/shard_map/ppermute | solution.py:236
  116.0 0.0 collective-permute-done.3
  116.0 2.8 %add_convert_fusion.3 = bf16[192,2560]{1,0:T(8,128)(2,1)} fusion(bf16[192,2560]{1,0:T(8,128)(2,1)} %collective-permute-done.6, bf16[192,2560]{1,0:T(8,128)(2,1)} %collective-permute-done.3, bf16[192,2560]{1,0:T(8,128)(2,1)S(1)} %copy-done.20), kind=kLoop, calls=%fused_computation.10 | loop fusion | flops 3932160 | bytes 3932160 | tf_op jit(solution)/shard_map/convert_element_type | solution.py:24
  118.8 4.7 %all-to-all-start.2 = ((bf16[8,24,2560]{2,1,0:T(8,128)(2,1)}), bf16[8,24,2560]{2,1,0:T(8,128)(2,1)}, u32[]{:S(2)}, u32[]{:S(2)}) async-start(bf16[8,24,2560]{2,1,0:T(8,128)(2,1)} %bitcast.54), calls=%async_computation.2 | async-start | bytes 1966080 | tf_op jit(solution)/shard_map/all_to_all | solution.py:277
  123.5 0.0 collective-permute-done.8
  123.5 1.7 add_convert_fusion.2
  125.2 1.6 collective-permute-start.10
  126.8 1.0 copy-done.9
  127.8 13.6 %shard_map.112 = (bf16[192,1024]{1,0:T(8,128)(2,1)}, bf16[192,1024]{1,0:T(8,128)(2,1)}, bf16[192,2560]{1,0:T(8,128)(2,1)}, bf16[192,2560]{1,0:T(8,128)(2,1)}, f32[1,2560]{1,0:T(1,128)}) custom-call(bf16[192,2560]{1,0:T(8,128)(2,1)} %bitcast.45, bf16[192,2560]{1,0:T(8,128)(2,1)} %copy-done.9, f32[192,1024]{1,0:T(8,128)} %get-tuple-element.71.refs_2_, ...), custom_call_target="tpu_custom_call" | custom-call | flops 1 | bytes 1 | tf_op jit(solution)/shard_map/pallas_call | solution.py:183
  141.4 0.7 add.69
  142.1 0.1 collective-permute-start.11
  142.2 1.2 collective-permute-done.11
  143.4 0.6 collective-permute-start.12
  144.0 4.7 %collective-permute-done.12 = f32[1,2560]{1,0:T(1,128)S(1)} collective-permute-done((f32[1,2560]{1,0:T(1,128)S(1)}, f32[1,2560]{1,0:T(1,128)S(1)}, u32[]{:S(2)}, u32[]{:S(2)}) %collective-permute-start.12) | collective-permute-done | bytes 10272 | tf_op jit(solution)/shard_map/ppermute | solution.py:236
  148.7 0.9 copy-done.21
  149.6 0.1 pad_reduce_fusion
  149.7 2.7 %collective-permute-done.13 = bf16[192,2560]{1,0:T(8,128)(2,1)S(1)} collective-permute-done((bf16[192,2560]{1,0:T(8,128)(2,1)}, bf16[192,2560]{1,0:T(8,128)(2,1)S(1)}, u32[]{:S(2)}, u32[]{:S(2)}) %collective-permute-start.13) | collective-permute-done | bytes 983072 | tf_op jit(solution)/shard_map/ppermute | solution.py:236
  152.4 1.8 add_convert_fusion
  154.3 1.1 pad_maximum_fusion
  155.3 6.0 %all-to-all-start.3 = ((bf16[8,24,2816]{2,1,0:T(8,128)(2,1)}), bf16[8,24,2816]{2,1,0:T(8,128)(2,1)}, u32[]{:S(2)}, u32[]{:S(2)}) async-start(bf16[8,24,2816]{2,1,0:T(8,128)(2,1)} %pad_maximum_fusion), calls=%async_computation.3 | async-start | bytes 2162688 | tf_op jit(solution)/shard_map/all_to_all | solution.py:277
  161.3 2.8 %fusion.4 = (f32[128]{0:T(128)S(1)}, bf16[128,2560]{1,0:T(8,128)(2,1)}) fusion(bf16[128,2560]{1,0:T(8,128)(2,1)} %param.13, f32[128]{0:T(128)S(1)} %add_divide_fusion, bf16[192,2560]{1,0:T(8,128)(2,1)} %bitcast.9, s32[128]{0:T(128)S(1)} %compare_select_fusion), kind=kOutput, calls=%fused_computation.16 | convolution fusion | flops 128147328 | bytes 2295296 | tf_op jit(solution)/shard_map/dot_general | solution.py:12
  164.2 0.0 copy-start.11
  164.2 8.9 %shard_map.113 = bf16[2560,1024]{1,0:T(8,128)(2,1)} custom-call(bf16[192,2560]{1,0:T(8,128)(2,1)} %collective-permute-done.refs_0_.refs_6_, bf16[192,2560]{1,0:T(8,128)(2,1)S(1)} %copy-done.6, bf16[192,2560]{1,0:T(8,128)(2,1)S(1)} %bitcast.42, bf16[192,2560]{1,0:T(8,128)(2,1)} %collective-permute-done.2.refs_3_.refs_7_, bf16[192,1024]{1,0:T(8,128)(2,1)S(1)} %copy-done.15, ...), custom_call_target="tpu_custom_call" | custom-call | flops 4026531840 | bytes 10747904 | tf_op jit(solution)/shard_map/pallas_call | solution.py:220
  173.1 8.7 %shard_map.114 = bf16[1024,2560]{1,0:T(8,128)(2,1)} custom-call(bf16[192,1024]{1,0:T(8,128)(2,1)S(1)} %copy-done.11, bf16[192,1024]{1,0:T(8,128)(2,1)S(1)} %copy-done.12, bf16[192,1024]{1,0:T(8,128)(2,1)S(1)} %copy-done.13, bf16[192,1024]{1,0:T(8,128)(2,1)S(1)} %copy-done.14, bf16[192,2560]{1,0:T(8,128)(2,1)} %collective-permute-done.5.refs_0_.refs_4_, ...), custom_call_target="tpu_custom_call" | custom-call | flops 4026531840 | bytes 10747904 | tf_op jit(solution)/shard_map/pallas_call | solution.py:220
  181.9 6.3 %all-to-all-done.3 = bf16[8,24,2816]{2,1,0:T(8,128)(2,1)} async-done(((bf16[8,24,2816]{2,1,0:T(8,128)(2,1)}), bf16[8,24,2816]{2,1,0:T(8,128)(2,1)}, u32[]{:S(2)}, u32[]{:S(2)}) %all-to-all-start.3) | async-done | bytes 1081376 | tf_op jit(solution)/shard_map/all_to_all | solution.py:277
  188.2 0.8 slice_bitcast_fusion.1
  189.0 1.6 fusion.8
  190.7 0.6 add_bitcast_fusion
  191.3 1.2 fusion.1
  (59 shorter events, 0.3 us)
Async XLA Ops:
  0.6 3.1 %copy-start = (bf16[128,2560]{1,0:T(8,128)(2,1)S(1)}, bf16[128,2560]{1,0:T(8,128)(2,1)}, u32[]{:S(2)}) copy-start(bf16[128,2560]{1,0:T(8,128)(2,1)} %param.7) | copy-start | bytes 1966084
  0.6 11.7 %copy-start.24 = (s32[128,1]{0,1:T(1,128)S(1)}, s32[128,1]{0,1:T(1,128)}, u32[]{:S(2)}) copy-start(s32[128,1]{0,1:T(1,128)} %param.8) | copy-start | bytes 1540
  0.7 11.7 %copy-start.22 = (bf16[2560,8]{0,1:T(8,128)(2,1)S(1)}, bf16[2560,8]{0,1:T(8,128)(2,1)}, u32[]{:S(2)}) copy-start(bf16[2560,8]{0,1:T(8,128)(2,1)} %param.10) | copy-start | bytes 122884
  3.7 8.9 %copy-start.19 = (bf16[128,2560]{1,0:T(8,128)(2,1)S(1)}, bf16[128,2560]{1,0:T(8,128)(2,1)}, u32[]{:S(2)}) copy-start(bf16[128,2560]{1,0:T(8,128)(2,1)} %param.13) | copy-start | bytes 1966084
  5.1 31.6 %all-to-all-start = ((bf16[8,24,2560]{2,1,0:T(8,128)(2,1)}), bf16[8,24,2560]{2,1,0:T(8,128)(2,1)S(1)}, u32[]{:S(2)}, u32[]{:S(2)}) async-start(bf16[8,24,2560]{2,1,0:T(8,128)(2,1)} %bitcast.2), calls=%async_computation | async-start | bytes 1966080 | tf_op jit(solution)/shard_map/all_to_all | solution.py:277
  36.7 30.9 %copy-start.1 = (bf16[8,24,2560]{2,1,0:T(8,128)(2,1)}, bf16[8,24,2560]{2,1,0:T(8,128)(2,1)S(1)}, u32[]{:S(2)}) copy-start(bf16[8,24,2560]{2,1,0:T(8,128)(2,1)S(1)} %all-to-all-done) | copy-start | bytes 2949124
  36.7 28.1 %all-to-all-start.1 = ((bf16[8,24,2560]{2,1,0:T(8,128)(2,1)}), bf16[8,24,2560]{2,1,0:T(8,128)(2,1)S(1)}, u32[]{:S(2)}, u32[]{:S(2)}) async-start(bf16[8,24,2560]{2,1,0:T(8,128)(2,1)} %bitcast.53), calls=%async_computation.1 | async-start | bytes 1966080 | tf_op jit(solution)/shard_map/all_to_all | solution.py:277
  40.3 23.5 %collective-permute-start = (bf16[192,2560]{1,0:T(8,128)(2,1)S(1)}, bf16[192,2560]{1,0:T(8,128)(2,1)}, u32[]{:S(2)}, u32[]{:S(2)}) collective-permute-start(bf16[192,2560]{1,0:T(8,128)(2,1)S(1)} %bitcast.38), channel_id=1, source_target_pairs={{0,2},{1,3},{2,0},{3,1},{4,6},{5,7},{6,4},{7,5},{8,10},{9,11},{10,... | collective-permute-start | bytes 2949128 | tf_op jit(solution)/shard_map/ppermute | solution.py:236
  41.9 24.5 %collective-permute-start.2 = (bf16[192,2560]{1,0:T(8,128)(2,1)S(1)}, bf16[192,2560]{1,0:T(8,128)(2,1)}, u32[]{:S(2)}, u32[]{:S(2)}) collective-permute-start(bf16[192,2560]{1,0:T(8,128)(2,1)S(1)} %bitcast.39), channel_id=1, source_target_pairs={{0,1},{1,0},{2,3},{3,2},{4,5},{5,4},{6,7},{7,6},{8,9},{9,8},{10,11... | collective-permute-start | bytes 2949128 | tf_op jit(solution)/shard_map/ppermute | solution.py:236
  64.8 43.5 %copy-start.3 = (bf16[8,24,2560]{2,1,0:T(8,128)(2,1)}, bf16[8,24,2560]{2,1,0:T(8,128)(2,1)S(1)}, u32[]{:S(2)}) copy-start(bf16[8,24,2560]{2,1,0:T(8,128)(2,1)S(1)} %all-to-all-done.1) | copy-start | bytes 2949124
  64.8 2.8 %collective-permute-start.1 = (bf16[192,2560]{1,0:T(8,128)(2,1)}, bf16[192,2560]{1,0:T(8,128)(2,1)S(1)}, u32[]{:S(2)}, u32[]{:S(2)}) collective-permute-start(bf16[192,2560]{1,0:T(8,128)(2,1)} %collective-permute-done.refs_0_.refs_6_), channel_id=1, source_target_pairs={{0,1},{1,0},{2,3},{3,2},{4,5},{5,4},{6,7},{7,6},{8,9},{9,8},{10,11... | collective-permute-start | bytes 2949128 | tf_op jit(solution)/shard_map/ppermute | solution.py:236
  64.8 24.3 %collective-permute-start.5 = (bf16[192,2560]{1,0:T(8,128)(2,1)S(1)}, bf16[192,2560]{1,0:T(8,128)(2,1)}, u32[]{:S(2)}, u32[]{:S(2)}) collective-permute-start(bf16[192,2560]{1,0:T(8,128)(2,1)S(1)} %bitcast.43), channel_id=1, source_target_pairs={{0,2},{1,3},{2,0},{3,1},{4,6},{5,7},{6,4},{7,5},{8,10},{9,11},{10,... | collective-permute-start | bytes 2949128 | tf_op jit(solution)/shard_map/ppermute | solution.py:236
  67.6 0.9 copy-start.5
  83.7 5.4 %collective-permute-start.4 = (bf16[192,2560]{1,0:T(8,128)(2,1)}, bf16[192,2560]{1,0:T(8,128)(2,1)S(1)}, u32[]{:S(2)}, u32[]{:S(2)}) collective-permute-start(bf16[192,2560]{1,0:T(8,128)(2,1)} %get-tuple-element.56), channel_id=1, source_target_pairs={{0,1},{1,0},{2,3},{3,2},{4,5},{5,4},{6,7},{7,6},{8,9},{9,8},{10,11... | collective-permute-start | bytes 2949128 | tf_op jit(solution)/shard_map/ppermute | solution.py:236
  89.1 4.2 %collective-permute-start.7 = (bf16[192,2560]{1,0:T(8,128)(2,1)}, bf16[192,2560]{1,0:T(8,128)(2,1)S(1)}, u32[]{:S(2)}, u32[]{:S(2)}) collective-permute-start(bf16[192,2560]{1,0:T(8,128)(2,1)} %collective-permute-done.5.refs_0_.refs_4_), channel_id=1, source_target_pairs={{0,1},{1,0},{2,3},{3,2},{4,5},{5,4},{6,7},{7,6},{8,9},{9,8},{10,11... | collective-permute-start | bytes 2949128 | tf_op jit(solution)/shard_map/ppermute | solution.py:236
  91.5 24.5 %collective-permute-start.6 = (bf16[192,2560]{1,0:T(8,128)(2,1)}, bf16[192,2560]{1,0:T(8,128)(2,1)}, u32[]{:S(2)}, u32[]{:S(2)}) collective-permute-start(bf16[192,2560]{1,0:T(8,128)(2,1)} %add_convert_fusion.4), channel_id=1, source_target_pairs={{0,2},{1,3},{2,0},{3,1},{4,6},{5,7},{6,4},{7,5},{8,10},{9,11},{10,... | collective-permute-start | bytes 2949128 | tf_op jit(solution)/shard_map/ppermute | solution.py:236
  93.0 23.0 %collective-permute-start.3 = (bf16[192,2560]{1,0:T(8,128)(2,1)}, bf16[192,2560]{1,0:T(8,128)(2,1)}, u32[]{:S(2)}, u32[]{:S(2)}) collective-permute-start(bf16[192,2560]{1,0:T(8,128)(2,1)} %get-tuple-element.54), channel_id=1, source_target_pairs={{0,1},{1,0},{2,3},{3,2},{4,5},{5,4},{6,7},{7,6},{8,9},{9,8},{10,11... | collective-permute-start | bytes 2949128 | tf_op jit(solution)/shard_map/ppermute | solution.py:236
  93.3 1.0 copy-start.7
  94.3 21.7 %copy-start.20 = (bf16[192,2560]{1,0:T(8,128)(2,1)S(1)}, bf16[192,2560]{1,0:T(8,128)(2,1)}, u32[]{:S(2)}) copy-start(bf16[192,2560]{1,0:T(8,128)(2,1)} %get-tuple-element.53) | copy-start | bytes 2949124
  108.0 15.5 %collective-permute-start.8 = (bf16[192,2560]{1,0:T(8,128)(2,1)}, bf16[192,2560]{1,0:T(8,128)(2,1)}, u32[]{:S(2)}, u32[]{:S(2)}) collective-permute-start(bf16[192,2560]{1,0:T(8,128)(2,1)} %get-tuple-element.66), channel_id=1, source_target_pairs={{0,1},{1,0},{2,3},{3,2},{4,5},{5,4},{6,7},{7,6},{8,9},{9,8},{10,11... | collective-permute-start | bytes 2949128 | tf_op jit(solution)/shard_map/ppermute | solution.py:236
  108.3 18.5 %collective-permute-start.9 = (bf16[192,2560]{1,0:T(8,128)(2,1)S(1)}, bf16[192,2560]{1,0:T(8,128)(2,1)S(1)}, u32[]{:S(2)}, u32[]{:S(2)}) collective-permute-start(bf16[192,2560]{1,0:T(8,128)(2,1)S(1)} %bitcast.44), channel_id=1, source_target_pairs={{0,1},{1,0},{2,3},{3,2},{4,5},{5,4},{6,7},{7,6},{8,9},{9,8},{10,11... | collective-permute-start | bytes 2949128 | tf_op jit(solution)/shard_map/ppermute | solution.py:236
  118.8 30.8 %all-to-all-start.2 = ((bf16[8,24,2560]{2,1,0:T(8,128)(2,1)}), bf16[8,24,2560]{2,1,0:T(8,128)(2,1)}, u32[]{:S(2)}, u32[]{:S(2)}) async-start(bf16[8,24,2560]{2,1,0:T(8,128)(2,1)} %bitcast.54), calls=%async_computation.2 | async-start | bytes 1966080 | tf_op jit(solution)/shard_map/all_to_all | solution.py:277
  125.2 23.4 %collective-permute-start.10 = (bf16[192,2560]{1,0:T(8,128)(2,1)S(1)}, bf16[192,2560]{1,0:T(8,128)(2,1)S(1)}, u32[]{:S(2)}, u32[]{:S(2)}) collective-permute-start(bf16[192,2560]{1,0:T(8,128)(2,1)S(1)} %add_convert_fusion.2), channel_id=1, source_target_pairs={{0,2},{1,3},{2,0},{3,1},{4,6},{5,7},{6,4},{7,5},{8,10},{9,11},{10,... | collective-permute-start | bytes 2949128 | tf_op jit(solution)/shard_map/ppermute | solution.py:236
  126.8 1.0 copy-start.9
  127.8 13.6 %copy-start.23 = (f32[1,2560]{1,0:T(1,128)S(1)}, f32[1,2560]{1,0:T(1,128)}, u32[]{:S(2)}) copy-start(f32[1,2560]{1,0:T(1,128)} %get-tuple-element.76) | copy-start | bytes 30724
  142.1 1.2 collective-permute-start.11
  143.4 5.2 %collective-permute-start.12 = (f32[1,2560]{1,0:T(1,128)S(1)}, f32[1,2560]{1,0:T(1,128)S(1)}, u32[]{:S(2)}, u32[]{:S(2)}) collective-permute-start(f32[1,2560]{1,0:T(1,128)S(1)} %add.70), channel_id=1, source_target_pairs={{0,2},{1,3},{2,0},{3,1},{4,6},{5,7},{6,4},{7,5},{8,10},{9,11},{10,... | collective-permute-start | bytes 30728 | tf_op jit(solution)/shard_map/ppermute | solution.py:236
  148.7 1.0 copy-start.21
  149.6 2.8 %collective-permute-start.13 = (bf16[192,2560]{1,0:T(8,128)(2,1)}, bf16[192,2560]{1,0:T(8,128)(2,1)S(1)}, u32[]{:S(2)}, u32[]{:S(2)}) collective-permute-start(bf16[192,2560]{1,0:T(8,128)(2,1)} %get-tuple-element.81), channel_id=1, source_target_pairs={{0,1},{1,0},{2,3},{3,2},{4,5},{5,4},{6,7},{7,6},{8,9},{9,8},{10,11... | collective-permute-start | bytes 2949128 | tf_op jit(solution)/shard_map/ppermute | solution.py:236
  155.3 8.8 %copy-start.2 = (bf16[8,24,2560]{2,1,0:T(8,128)(2,1)S(1)}, bf16[8,24,2560]{2,1,0:T(8,128)(2,1)}, u32[]{:S(2)}) copy-start(bf16[8,24,2560]{2,1,0:T(8,128)(2,1)} %copy-done.1) | copy-start | bytes 2949124
  155.3 8.8 %copy-start.6 = (bf16[192,2560]{1,0:T(8,128)(2,1)S(1)}, bf16[192,2560]{1,0:T(8,128)(2,1)}, u32[]{:S(2)}) copy-start(bf16[192,2560]{1,0:T(8,128)(2,1)} %copy-done.5) | copy-start | bytes 2949124
  155.3 8.8 %copy-start.15 = (bf16[192,1024]{1,0:T(8,128)(2,1)S(1)}, bf16[192,1024]{1,0:T(8,128)(2,1)}, u32[]{:S(2)}) copy-start(bf16[192,1024]{1,0:T(8,128)(2,1)} %get-tuple-element.89.refs_4_) | copy-start | bytes 1179652
  155.3 8.8 %copy-start.16 = (bf16[192,1024]{1,0:T(8,128)(2,1)S(1)}, bf16[192,1024]{1,0:T(8,128)(2,1)}, u32[]{:S(2)}) copy-start(bf16[192,1024]{1,0:T(8,128)(2,1)} %get-tuple-element.90.refs_5_) | copy-start | bytes 1179652
  155.3 32.8 %all-to-all-start.3 = ((bf16[8,24,2816]{2,1,0:T(8,128)(2,1)}), bf16[8,24,2816]{2,1,0:T(8,128)(2,1)}, u32[]{:S(2)}, u32[]{:S(2)}) async-start(bf16[8,24,2816]{2,1,0:T(8,128)(2,1)} %pad_maximum_fusion), calls=%async_computation.3 | async-start | bytes 2162688 | tf_op jit(solution)/shard_map/all_to_all | solution.py:277
  161.3 2.9 %copy-start.17 = (bf16[192,1024]{1,0:T(8,128)(2,1)S(1)}, bf16[192,1024]{1,0:T(8,128)(2,1)}, u32[]{:S(2)}) copy-start(bf16[192,1024]{1,0:T(8,128)(2,1)} %get-tuple-element.91.refs_6_) | copy-start | bytes 1179652
  161.3 2.9 %copy-start.18 = (bf16[192,1024]{1,0:T(8,128)(2,1)S(1)}, bf16[192,1024]{1,0:T(8,128)(2,1)}, u32[]{:S(2)}) copy-start(bf16[192,1024]{1,0:T(8,128)(2,1)} %get-tuple-element.92.refs_7_) | copy-start | bytes 1179652
  164.2 8.9 %copy-start.4 = (bf16[8,24,2560]{2,1,0:T(8,128)(2,1)S(1)}, bf16[8,24,2560]{2,1,0:T(8,128)(2,1)}, u32[]{:S(2)}) copy-start(bf16[8,24,2560]{2,1,0:T(8,128)(2,1)} %copy-done.3) | copy-start | bytes 2949124
  164.2 8.9 %copy-start.8 = (bf16[192,2560]{1,0:T(8,128)(2,1)S(1)}, bf16[192,2560]{1,0:T(8,128)(2,1)}, u32[]{:S(2)}) copy-start(bf16[192,2560]{1,0:T(8,128)(2,1)} %copy-done.7) | copy-start | bytes 2949124
  164.2 8.9 %copy-start.10 = (bf16[192,2560]{1,0:T(8,128)(2,1)S(1)}, bf16[192,2560]{1,0:T(8,128)(2,1)}, u32[]{:S(2)}) copy-start(bf16[192,2560]{1,0:T(8,128)(2,1)} %copy-done.9) | copy-start | bytes 2949124
  164.2 8.9 %copy-start.11 = (bf16[192,1024]{1,0:T(8,128)(2,1)S(1)}, bf16[192,1024]{1,0:T(8,128)(2,1)}, u32[]{:S(2)}) copy-start(bf16[192,1024]{1,0:T(8,128)(2,1)} %get-tuple-element.93.refs_4_.refs_0_) | copy-start | bytes 1179652
  164.2 8.9 %copy-start.12 = (bf16[192,1024]{1,0:T(8,128)(2,1)S(1)}, bf16[192,1024]{1,0:T(8,128)(2,1)}, u32[]{:S(2)}) copy-start(bf16[192,1024]{1,0:T(8,128)(2,1)} %get-tuple-element.94.refs_5_.refs_1_) | copy-start | bytes 1179652
  164.2 8.9 %copy-start.13 = (bf16[192,1024]{1,0:T(8,128)(2,1)S(1)}, bf16[192,1024]{1,0:T(8,128)(2,1)}, u32[]{:S(2)}) copy-start(bf16[192,1024]{1,0:T(8,128)(2,1)} %get-tuple-element.95.refs_4_.refs_2_) | copy-start | bytes 1179652
  164.2 8.9 %copy-start.14 = (bf16[192,1024]{1,0:T(8,128)(2,1)S(1)}, bf16[192,1024]{1,0:T(8,128)(2,1)}, u32[]{:S(2)}) copy-start(bf16[192,1024]{1,0:T(8,128)(2,1)} %get-tuple-element.96.refs_5_.refs_3_) | copy-start | bytes 1179652

commit v6 on v5

--- a/solution.py
+++ b/solution.py
@@ -267,8 +267,10 @@
         ids = expert_ids[:, 0]
         live = lax.iota(jnp.int32, tok_rows) < live_counts[0]
         chosen = ids[:, None] == lax.iota(jnp.int32, experts)[None, :]
-        chosen_int = chosen.astype(jnp.int32)
-        rank = jnp.sum(jnp.cumsum(chosen_int, axis=0) * chosen_int, axis=1) - 1
+        place = lax.iota(jnp.int32, tok_rows)
+        ahead = (place[None, :] < place[:, None]).astype(jnp.bfloat16)
+        counts = dot(ahead, chosen.astype(jnp.bfloat16))
+        rank = jnp.sum(jnp.where(chosen, counts, 0.0), axis=1).astype(jnp.int32)
         target = jnp.where(live, ids * most + rank, -1)
         placing = (lax.iota(jnp.int32, slots)[:, None] == target[None, :]).astype(jnp.bfloat16)
         w_up, w_down = up_weight[0], down_weight[0]

time: 193 us -> 193 us (level)
    dot_general x6 -> x7, matrix products: 8.74 us -> 9.62 us  [dot(): lax.dot_general(a, b, (dims, ((), ())), preferred_element_type=jnp.float32)]
where the time goes in v6:
time: 193 us; the launch traced here: 192 us
  waiting for transfers between devices  74.2 us (38%)
  Pallas kernels  60 us (31%)
  starting transfers between devices  29.3 us (15%)
  other arithmetic  11.9 us (6%)
  matrix products  9.62 us (5%)
  local copies, waits for them, and re-layouts  4.96 us (3%)
    ppermute x14, waiting for transfers between devices, cross(): return lax.ppermute(x, 'tensor', [(i, i ^ bit) for i in range(n_tensor)])  44.3 us
    all_to_all x4, waiting for transfers between devices, swap(): return lax.all_to_all(x, 'expert', split_axis=0, concat_axis=0, tiled=True)  29.9 us
    pallas_call x2, Pallas kernels, backward(): call(functools.partial(backward_kernel, n, steps, steps + wides - 1, tile...  27.3 us
    all_to_all x4, starting transfers between devices, swap(): return lax.all_to_all(x, 'expert', split_axis=0, concat_axis=0, tiled=True)  21.5 us
    pallas_call x2, Pallas kernels, gradient(): call(functools.partial(gradient_kernel, len(lefts)), height // tile, [pl....  17.6 us
    pallas_call x1, Pallas kernels, forward(): call(functools.partial(forward_kernel, n, steps, tile), steps + wides, [w...  15.1 us
    dot_general x7, matrix products, dot(): lax.dot_general(a, b, (dims, ((), ())), preferred_element_type=jnp.float32)  9.62 us
    convert_element_type x4, other arithmetic, added(): return (a.astype(jnp.float32) + b.astype(jnp.float32)).astype(jnp.bfloat16)  8.77 us
  transfers between devices with their start and end apart: 18, of which 10 were waited for; matrix products, arithmetic and copies ran while one was open for 7% of the time, Pallas kernels for 31%

profile of v6, /device:TPU:0, one launch (start us, length us, event | category | flops | bytes accessed | tf_op | source)
XLA Modules:
  0.0 191.8 jit_solution(6943187752289419222)
XLA Ops:
  0.6 0.0 copy-start
  0.6 0.0 copy-start.24
  1.4 0.9 fusion.6
  2.3 0.7 compare_select_fusion
  2.9 1.4 convolution_convert_fusion.1
  4.3 7.3 %all-to-all-start = ((bf16[8,24,2560]{2,1,0:T(8,128)(2,1)}), bf16[8,24,2560]{2,1,0:T(8,128)(2,1)S(1)}, u32[]{:S(2)}, u32[]{:S(2)}) async-start(bf16[8,24,2560]{2,1,0:T(8,128)(2,1)} %bitcast.2), calls=%async_computation | async-start | bytes 1966080 | tf_op jit(solution)/shard_map/all_to_all | solution.py:279
  11.6 0.3 fusion.5
  11.9 1.5 convolution_convert_fusion
  13.3 22.6 %all-to-all-done = bf16[8,24,2560]{2,1,0:T(8,128)(2,1)S(1)} async-done(((bf16[8,24,2560]{2,1,0:T(8,128)(2,1)}), bf16[8,24,2560]{2,1,0:T(8,128)(2,1)S(1)}, u32[]{:S(2)}, u32[]{:S(2)}) %all-to-all-start) | async-done | bytes 983072 | tf_op jit(solution)/shard_map/all_to_all | solution.py:279
  35.9 3.6 %all-to-all-start.1 = ((bf16[8,24,2560]{2,1,0:T(8,128)(2,1)}), bf16[8,24,2560]{2,1,0:T(8,128)(2,1)S(1)}, u32[]{:S(2)}, u32[]{:S(2)}) async-start(bf16[8,24,2560]{2,1,0:T(8,128)(2,1)} %bitcast.53), calls=%async_computation.1 | async-start | bytes 1966080 | tf_op jit(solution)/shard_map/all_to_all | solution.py:279
  39.5 1.6 collective-permute-start
  41.1 0.0 collective-permute-start.2
  41.1 21.9 %collective-permute-done.refs_0_.refs_6_ = bf16[192,2560]{1,0:T(8,128)(2,1)} collective-permute-done((bf16[192,2560]{1,0:T(8,128)(2,1)S(1)}, bf16[192,2560]{1,0:T(8,128)(2,1)}, u32[]{:S(2)}, u32[]{:S(2)}) %collective-permute-start) | collective-permute-done | bytes 983072 | tf_op jit(solution)/shard_map/ppermute | solution.py:236
  63.0 1.0 all-to-all-done.1
  64.0 0.0 collective-permute-start.1
  64.1 1.5 collective-permute-start.5
  65.6 0.0 collective-permute-done.2.refs_3_.refs_7_
  65.6 1.3 collective-permute-done.1.refs_1_.refs_7_
  66.8 0.9 copy-done.5
  67.8 15.1 %shard_map.110 = (f32[192,1024]{1,0:T(8,128)}, f32[192,1024]{1,0:T(8,128)}, f32[192,1024]{1,0:T(8,128)}, f32[192,1024]{1,0:T(8,128)}, bf16[192,1024]{1,0:T(8,128...) custom-call(bf16[192,2560]{1,0:T(8,128)(2,1)} %collective-permute-do, ...), custom_call_target="tpu_custom_call" | custom-call | flops 1 | bytes 1 | tf_op jit(solution)/shard_map/pallas_call | solution.py:157
  82.9 0.2 collective-permute-start.4
  83.1 5.2 %collective-permute-done.5.refs_0_.refs_4_ = bf16[192,2560]{1,0:T(8,128)(2,1)} collective-permute-done((bf16[192,2560]{1,0:T(8,128)(2,1)S(1)}, bf16[192,2560]{1,0:T(8,128)(2,1)}, u32[]{:S(2)}, u32[]{:S(2)}) %collective-permute-start.5) | collective-permute-done | bytes 983072 | tf_op jit(solution)/shard_map/ppermute | solution.py:236
  88.3 0.0 collective-permute-start.7
  88.3 0.0 collective-permute-done.4
  88.3 2.4 %add_convert_fusion.4 = bf16[192,2560]{1,0:T(8,128)(2,1)} fusion(bf16[192,2560]{1,0:T(8,128)(2,1)S(1)} %collective-permute-done.4, bf16[192,2560]{1,0:T(8,128)(2,1)} %get-tuple-element.55), kind=kLoop, calls=%fused_computation.11 | loop fusion | flops 1966080 | bytes 2949120 | tf_op jit(solution)/shard_map/convert_element_type | solution.py:24
  90.7 1.5 collective-permute-start.6
  92.2 0.2 collective-permute-start.3
  92.5 0.0 collective-permute-done.7.refs_1_.refs_5_
  92.5 0.7 broadcast_in_dim.36.refs_10_
  93.2 0.3 copy-done.7
  93.5 13.7 %shard_map.111 = (bf16[192,1024]{1,0:T(8,128)(2,1)}, bf16[192,1024]{1,0:T(8,128)(2,1)}, bf16[192,2560]{1,0:T(8,128)(2,1)}, bf16[192,2560]{1,0:T(8,128)(2,1)}, f32[1,2560]{1,0:T(1,128)}) custom-call(bf16[192,2560]{1,0:T(8,128)(2,1)} %collective-permute-done.5.refs_0_.refs_4_, bf16[192,2560]{1,0:T(8,128)(2,1)} %copy-done.7, ...), custom_call_target="tpu_custom_call" | custom-call | flops 1 | bytes 1 | tf_op jit(solution)/shard_map/pallas_call | solution.py:183
  107.2 0.3 collective-permute-start.8
  107.5 0.2 collective-permute-start.9
  107.7 7.5 %collective-permute-done.6 = bf16[192,2560]{1,0:T(8,128)(2,1)} collective-permute-done((bf16[192,2560]{1,0:T(8,128)(2,1)}, bf16[192,2560]{1,0:T(8,128)(2,1)}, u32[]{:S(2)}, u32[]{:S(2)}) %collective-permute-start.6) | collective-permute-done | bytes 983072 | tf_op jit(solution)/shard_map/ppermute | solution.py:236
  115.2 0.0 collective-permute-done.3
  115.2 2.8 %add_convert_fusion.3 = bf16[192,2560]{1,0:T(8,128)(2,1)} fusion(bf16[192,2560]{1,0:T(8,128)(2,1)} %collective-permute-done.6, bf16[192,2560]{1,0:T(8,128)(2,1)} %collective-permute-done.3, bf16[192,2560]{1,0:T(8,128)(2,1)S(1)} %copy-done.20), kind=kLoop, calls=%fused_computation.10 | loop fusion | flops 3932160 | bytes 3932160 | tf_op jit(solution)/shard_map/convert_element_type | solution.py:24
  118.0 4.7 %all-to-all-start.2 = ((bf16[8,24,2560]{2,1,0:T(8,128)(2,1)}), bf16[8,24,2560]{2,1,0:T(8,128)(2,1)}, u32[]{:S(2)}, u32[]{:S(2)}) async-start(bf16[8,24,2560]{2,1,0:T(8,128)(2,1)} %bitcast.54), calls=%async_computation.2 | async-start | bytes 1966080 | tf_op jit(solution)/shard_map/all_to_all | solution.py:279
  122.7 0.0 collective-permute-done.8
  122.7 1.7 add_convert_fusion.2
  124.4 1.6 collective-permute-start.10
  126.0 1.0 copy-done.9
  127.0 13.6 %shard_map.112 = (bf16[192,1024]{1,0:T(8,128)(2,1)}, bf16[192,1024]{1,0:T(8,128)(2,1)}, bf16[192,2560]{1,0:T(8,128)(2,1)}, bf16[192,2560]{1,0:T(8,128)(2,1)}, f32[1,2560]{1,0:T(1,128)}) custom-call(bf16[192,2560]{1,0:T(8,128)(2,1)} %bitcast.45, bf16[192,2560]{1,0:T(8,128)(2,1)} %copy-done.9, f32[192,1024]{1,0:T(8,128)} %get-tuple-element.71.refs_2_, ...), custom_call_target="tpu_custom_call" | custom-call | flops 1 | bytes 1 | tf_op jit(solution)/shard_map/pallas_call | solution.py:183
  140.7 0.7 add.64
  141.4 0.1 collective-permute-start.11
  141.5 1.2 collective-permute-done.11
  142.7 0.6 collective-permute-start.12
  143.3 4.6 %collective-permute-done.12 = f32[1,2560]{1,0:T(1,128)S(1)} collective-permute-done((f32[1,2560]{1,0:T(1,128)S(1)}, f32[1,2560]{1,0:T(1,128)S(1)}, u32[]{:S(2)}, u32[]{:S(2)}) %collective-permute-start.12) | collective-permute-done | bytes 10272 | tf_op jit(solution)/shard_map/ppermute | solution.py:236
  147.9 0.9 copy-done.21
  148.8 0.0 collective-permute-start.13
  148.8 0.0 all-to-all-done.2
  148.9 0.1 pad_reduce_fusion
  148.9 2.7 %collective-permute-done.13 = bf16[192,2560]{1,0:T(8,128)(2,1)S(1)} collective-permute-done((bf16[192,2560]{1,0:T(8,128)(2,1)}, bf16[192,2560]{1,0:T(8,128)(2,1)S(1)}, u32[]{:S(2)}, u32[]{:S(2)}) %collective-permute-start.13) | collective-permute-done | bytes 983072 | tf_op jit(solution)/shard_map/ppermute | solution.py:236
  151.6 1.8 add_convert_fusion
  153.5 1.1 pad_maximum_fusion
  154.5 6.0 %all-to-all-start.3 = ((bf16[8,24,2816]{2,1,0:T(8,128)(2,1)}), bf16[8,24,2816]{2,1,0:T(8,128)(2,1)}, u32[]{:S(2)}, u32[]{:S(2)}) async-start(bf16[8,24,2816]{2,1,0:T(8,128)(2,1)} %pad_maximum_fusion), calls=%async_computation.3 | async-start | bytes 2162688 | tf_op jit(solution)/shard_map/all_to_all | solution.py:279
  160.5 2.8 %fusion.4 = (f32[128]{0:T(128)S(1)}, bf16[128,2560]{1,0:T(8,128)(2,1)}) fusion(bf16[128,2560]{1,0:T(8,128)(2,1)} %param.13, f32[128]{0:T(128)S(1)} %add_divide_fusion, bf16[192,2560]{1,0:T(8,128)(2,1)} %bitcast.9, s32[128]{0:T(128)S(1)} %compare_select_fusion), kind=kOutput, calls=%fused_computation.16 | convolution fusion | flops 128147328 | bytes 2295296 | tf_op jit(solution)/shard_map/dot_general | solution.py:12
  163.4 0.0 copy-start.11
  163.5 8.9 %shard_map.113 = bf16[2560,1024]{1,0:T(8,128)(2,1)} custom-call(bf16[192,2560]{1,0:T(8,128)(2,1)} %collective-permute-done.refs_0_.refs_6_, bf16[192,2560]{1,0:T(8,128)(2,1)S(1)} %copy-done.6, bf16[192,2560]{1,0:T(8,128)(2,1)S(1)} %bitcast.42, bf16[192,2560]{1,0:T(8,128)(2,1)} %collective-permute-done.2.refs_3_.refs_7_, bf16[192,1024]{1,0:T(8,128)(2,1)S(1)} %copy-done.15, ...), custom_call_target="tpu_custom_call" | custom-call | flops 4026531840 | bytes 10747904 | tf_op jit(solution)/shard_map/pallas_call | solution.py:220
  172.4 8.7 %shard_map.114 = bf16[1024,2560]{1,0:T(8,128)(2,1)} custom-call(bf16[192,1024]{1,0:T(8,128)(2,1)S(1)} %copy-done.11, bf16[192,1024]{1,0:T(8,128)(2,1)S(1)} %copy-done.12, bf16[192,1024]{1,0:T(8,128)(2,1)S(1)} %copy-done.13, bf16[192,1024]{1,0:T(8,128)(2,1)S(1)} %copy-done.14, bf16[192,2560]{1,0:T(8,128)(2,1)} %collective-permute-done.5.refs_0_.refs_4_, ...), custom_call_target="tpu_custom_call" | custom-call | flops 4026531840 | bytes 10747904 | tf_op jit(solution)/shard_map/pallas_call | solution.py:220
  181.1 6.3 %all-to-all-done.3 = bf16[8,24,2816]{2,1,0:T(8,128)(2,1)} async-done(((bf16[8,24,2816]{2,1,0:T(8,128)(2,1)}), bf16[8,24,2816]{2,1,0:T(8,128)(2,1)}, u32[]{:S(2)}, u32[]{:S(2)}) %all-to-all-start.3) | async-done | bytes 1081376 | tf_op jit(solution)/shard_map/all_to_all | solution.py:279
  187.4 0.8 slice_bitcast_fusion.1
  188.3 1.6 fusion.9
  189.9 0.6 add_bitcast_fusion
  190.6 1.2 fusion.1
  (55 shorter events, 0.2 us)
Async XLA Ops:
  0.6 2.3 %copy-start = (bf16[128,2560]{1,0:T(8,128)(2,1)S(1)}, bf16[128,2560]{1,0:T(8,128)(2,1)}, u32[]{:S(2)}) copy-start(bf16[128,2560]{1,0:T(8,128)(2,1)} %param.7) | copy-start | bytes 1966084
  0.6 10.9 %copy-start.24 = (s32[128,1]{0,1:T(1,128)S(1)}, s32[128,1]{0,1:T(1,128)}, u32[]{:S(2)}) copy-start(s32[128,1]{0,1:T(1,128)} %param.8) | copy-start | bytes 1540
  0.7 10.9 %copy-start.22 = (bf16[2560,8]{0,1:T(8,128)(2,1)S(1)}, bf16[2560,8]{0,1:T(8,128)(2,1)}, u32[]{:S(2)}) copy-start(bf16[2560,8]{0,1:T(8,128)(2,1)} %param.10) | copy-start | bytes 122884
  2.9 8.9 %copy-start.19 = (bf16[128,2560]{1,0:T(8,128)(2,1)S(1)}, bf16[128,2560]{1,0:T(8,128)(2,1)}, u32[]{:S(2)}) copy-start(bf16[128,2560]{1,0:T(8,128)(2,1)} %param.13) | copy-start | bytes 1966084
  4.3 31.6 %all-to-all-start = ((bf16[8,24,2560]{2,1,0:T(8,128)(2,1)}), bf16[8,24,2560]{2,1,0:T(8,128)(2,1)S(1)}, u32[]{:S(2)}, u32[]{:S(2)}) async-start(bf16[8,24,2560]{2,1,0:T(8,128)(2,1)} %bitcast.2), calls=%async_computation | async-start | bytes 1966080 | tf_op jit(solution)/shard_map/all_to_all | solution.py:279
  35.9 30.9 %copy-start.1 = (bf16[8,24,2560]{2,1,0:T(8,128)(2,1)}, bf16[8,24,2560]{2,1,0:T(8,128)(2,1)S(1)}, u32[]{:S(2)}) copy-start(bf16[8,24,2560]{2,1,0:T(8,128)(2,1)S(1)} %all-to-all-done) | copy-start | bytes 2949124
  35.9 28.1 %all-to-all-start.1 = ((bf16[8,24,2560]{2,1,0:T(8,128)(2,1)}), bf16[8,24,2560]{2,1,0:T(8,128)(2,1)S(1)}, u32[]{:S(2)}, u32[]{:S(2)}) async-start(bf16[8,24,2560]{2,1,0:T(8,128)(2,1)} %bitcast.53), calls=%async_computation.1 | async-start | bytes 1966080 | tf_op jit(solution)/shard_map/all_to_all | solution.py:279
  39.5 23.5 %collective-permute-start = (bf16[192,2560]{1,0:T(8,128)(2,1)S(1)}, bf16[192,2560]{1,0:T(8,128)(2,1)}, u32[]{:S(2)}, u32[]{:S(2)}) collective-permute-start(bf16[192,2560]{1,0:T(8,128)(2,1)S(1)} %bitcast.38), channel_id=1, source_target_pairs={{0,2},{1,3},{2,0},{3,1},{4,6},{5,7},{6,4},{7,5},{8,10},{9,11},{10,... | collective-permute-start | bytes 2949128 | tf_op jit(solution)/shard_map/ppermute | solution.py:236
  41.1 24.5 %collective-permute-start.2 = (bf16[192,2560]{1,0:T(8,128)(2,1)S(1)}, bf16[192,2560]{1,0:T(8,128)(2,1)}, u32[]{:S(2)}, u32[]{:S(2)}) collective-permute-start(bf16[192,2560]{1,0:T(8,128)(2,1)S(1)} %bitcast.39), channel_id=1, source_target_pairs={{0,1},{1,0},{2,3},{3,2},{4,5},{5,4},{6,7},{7,6},{8,9},{9,8},{10,11... | collective-permute-start | bytes 2949128 | tf_op jit(solution)/shard_map/ppermute | solution.py:236
  64.0 43.5 %copy-start.3 = (bf16[8,24,2560]{2,1,0:T(8,128)(2,1)}, bf16[8,24,2560]{2,1,0:T(8,128)(2,1)S(1)}, u32[]{:S(2)}) copy-start(bf16[8,24,2560]{2,1,0:T(8,128)(2,1)S(1)} %all-to-all-done.1) | copy-start | bytes 2949124
  64.0 2.8 %collective-permute-start.1 = (bf16[192,2560]{1,0:T(8,128)(2,1)}, bf16[192,2560]{1,0:T(8,128)(2,1)S(1)}, u32[]{:S(2)}, u32[]{:S(2)}) collective-permute-start(bf16[192,2560]{1,0:T(8,128)(2,1)} %collective-permute-done.refs_0_.refs_6_), channel_id=1, source_target_pairs={{0,1},{1,0},{2,3},{3,2},{4,5},{5,4},{6,7},{7,6},{8,9},{9,8},{10,11... | collective-permute-start | bytes 2949128 | tf_op jit(solution)/shard_map/ppermute | solution.py:236
  64.1 24.3 %collective-permute-start.5 = (bf16[192,2560]{1,0:T(8,128)(2,1)S(1)}, bf16[192,2560]{1,0:T(8,128)(2,1)}, u32[]{:S(2)}, u32[]{:S(2)}) collective-permute-start(bf16[192,2560]{1,0:T(8,128)(2,1)S(1)} %bitcast.43), channel_id=1, source_target_pairs={{0,2},{1,3},{2,0},{3,1},{4,6},{5,7},{6,4},{7,5},{8,10},{9,11},{10,... | collective-permute-start | bytes 2949128 | tf_op jit(solution)/shard_map/ppermute | solution.py:236
  66.8 0.9 copy-start.5
  82.9 5.4 %collective-permute-start.4 = (bf16[192,2560]{1,0:T(8,128)(2,1)}, bf16[192,2560]{1,0:T(8,128)(2,1)S(1)}, u32[]{:S(2)}, u32[]{:S(2)}) collective-permute-start(bf16[192,2560]{1,0:T(8,128)(2,1)} %get-tuple-element.56), channel_id=1, source_target_pairs={{0,1},{1,0},{2,3},{3,2},{4,5},{5,4},{6,7},{7,6},{8,9},{9,8},{10,11... | collective-permute-start | bytes 2949128 | tf_op jit(solution)/shard_map/ppermute | solution.py:236
  88.3 4.2 %collective-permute-start.7 = (bf16[192,2560]{1,0:T(8,128)(2,1)}, bf16[192,2560]{1,0:T(8,128)(2,1)S(1)}, u32[]{:S(2)}, u32[]{:S(2)}) collective-permute-start(bf16[192,2560]{1,0:T(8,128)(2,1)} %collective-permute-done.5.refs_0_.refs_4_), channel_id=1, source_target_pairs={{0,1},{1,0},{2,3},{3,2},{4,5},{5,4},{6,7},{7,6},{8,9},{9,8},{10,11... | collective-permute-start | bytes 2949128 | tf_op jit(solution)/shard_map/ppermute | solution.py:236
  90.7 24.5 %collective-permute-start.6 = (bf16[192,2560]{1,0:T(8,128)(2,1)}, bf16[192,2560]{1,0:T(8,128)(2,1)}, u32[]{:S(2)}, u32[]{:S(2)}) collective-permute-start(bf16[192,2560]{1,0:T(8,128)(2,1)} %add_convert_fusion.4), channel_id=1, source_target_pairs={{0,2},{1,3},{2,0},{3,1},{4,6},{5,7},{6,4},{7,5},{8,10},{9,11},{10,... | collective-permute-start | bytes 2949128 | tf_op jit(solution)/shard_map/ppermute | solution.py:236
  92.2 23.0 %collective-permute-start.3 = (bf16[192,2560]{1,0:T(8,128)(2,1)}, bf16[192,2560]{1,0:T(8,128)(2,1)}, u32[]{:S(2)}, u32[]{:S(2)}) collective-permute-start(bf16[192,2560]{1,0:T(8,128)(2,1)} %get-tuple-element.54), channel_id=1, source_target_pairs={{0,1},{1,0},{2,3},{3,2},{4,5},{5,4},{6,7},{7,6},{8,9},{9,8},{10,11... | collective-permute-start | bytes 2949128 | tf_op jit(solution)/shard_map/ppermute | solution.py:236
  92.5 1.0 copy-start.7
  93.5 21.7 %copy-start.20 = (bf16[192,2560]{1,0:T(8,128)(2,1)S(1)}, bf16[192,2560]{1,0:T(8,128)(2,1)}, u32[]{:S(2)}) copy-start(bf16[192,2560]{1,0:T(8,128)(2,1)} %get-tuple-element.53) | copy-start | bytes 2949124
  107.2 15.5 %collective-permute-start.8 = (bf16[192,2560]{1,0:T(8,128)(2,1)}, bf16[192,2560]{1,0:T(8,128)(2,1)}, u32[]{:S(2)}, u32[]{:S(2)}) collective-permute-start(bf16[192,2560]{1,0:T(8,128)(2,1)} %get-tuple-element.66), channel_id=1, source_target_pairs={{0,1},{1,0},{2,3},{3,2},{4,5},{5,4},{6,7},{7,6},{8,9},{9,8},{10,11... | collective-permute-start | bytes 2949128 | tf_op jit(solution)/shard_map/ppermute | solution.py:236
  107.5 18.5 %collective-permute-start.9 = (bf16[192,2560]{1,0:T(8,128)(2,1)S(1)}, bf16[192,2560]{1,0:T(8,128)(2,1)S(1)}, u32[]{:S(2)}, u32[]{:S(2)}) collective-permute-start(bf16[192,2560]{1,0:T(8,128)(2,1)S(1)} %bitcast.44), channel_id=1, source_target_pairs={{0,1},{1,0},{2,3},{3,2},{4,5},{5,4},{6,7},{7,6},{8,9},{9,8},{10,11... | collective-permute-start | bytes 2949128 | tf_op jit(solution)/shard_map/ppermute | solution.py:236
  118.0 30.8 %all-to-all-start.2 = ((bf16[8,24,2560]{2,1,0:T(8,128)(2,1)}), bf16[8,24,2560]{2,1,0:T(8,128)(2,1)}, u32[]{:S(2)}, u32[]{:S(2)}) async-start(bf16[8,24,2560]{2,1,0:T(8,128)(2,1)} %bitcast.54), calls=%async_computation.2 | async-start | bytes 1966080 | tf_op jit(solution)/shard_map/all_to_all | solution.py:279
  124.4 23.4 %collective-permute-start.10 = (bf16[192,2560]{1,0:T(8,128)(2,1)S(1)}, bf16[192,2560]{1,0:T(8,128)(2,1)S(1)}, u32[]{:S(2)}, u32[]{:S(2)}) collective-permute-start(bf16[192,2560]{1,0:T(8,128)(2,1)S(1)} %add_convert_fusion.2), channel_id=1, source_target_pairs={{0,2},{1,3},{2,0},{3,1},{4,6},{5,7},{6,4},{7,5},{8,10},{9,11},{10,... | collective-permute-start | bytes 2949128 | tf_op jit(solution)/shard_map/ppermute | solution.py:236
  126.0 1.0 copy-start.9
  127.0 13.7 %copy-start.23 = (f32[1,2560]{1,0:T(1,128)S(1)}, f32[1,2560]{1,0:T(1,128)}, u32[]{:S(2)}) copy-start(f32[1,2560]{1,0:T(1,128)} %get-tuple-element.76) | copy-start | bytes 30724
  141.4 1.2 collective-permute-start.11
  142.7 5.2 %collective-permute-start.12 = (f32[1,2560]{1,0:T(1,128)S(1)}, f32[1,2560]{1,0:T(1,128)S(1)}, u32[]{:S(2)}, u32[]{:S(2)}) collective-permute-start(f32[1,2560]{1,0:T(1,128)S(1)} %add.65), channel_id=1, source_target_pairs={{0,2},{1,3},{2,0},{3,1},{4,6},{5,7},{6,4},{7,5},{8,10},{9,11},{10,... | collective-permute-start | bytes 30728 | tf_op jit(solution)/shard_map/ppermute | solution.py:236
  147.9 1.0 copy-start.21
  148.8 2.8 %collective-permute-start.13 = (bf16[192,2560]{1,0:T(8,128)(2,1)}, bf16[192,2560]{1,0:T(8,128)(2,1)S(1)}, u32[]{:S(2)}, u32[]{:S(2)}) collective-permute-start(bf16[192,2560]{1,0:T(8,128)(2,1)} %get-tuple-element.81), channel_id=1, source_target_pairs={{0,1},{1,0},{2,3},{3,2},{4,5},{5,4},{6,7},{7,6},{8,9},{9,8},{10,11... | collective-permute-start | bytes 2949128 | tf_op jit(solution)/shard_map/ppermute | solution.py:236
  154.5 8.8 %copy-start.2 = (bf16[8,24,2560]{2,1,0:T(8,128)(2,1)S(1)}, bf16[8,24,2560]{2,1,0:T(8,128)(2,1)}, u32[]{:S(2)}) copy-start(bf16[8,24,2560]{2,1,0:T(8,128)(2,1)} %copy-done.1) | copy-start | bytes 2949124
  154.5 8.8 %copy-start.6 = (bf16[192,2560]{1,0:T(8,128)(2,1)S(1)}, bf16[192,2560]{1,0:T(8,128)(2,1)}, u32[]{:S(2)}) copy-start(bf16[192,2560]{1,0:T(8,128)(2,1)} %copy-done.5) | copy-start | bytes 2949124
  154.5 8.8 %copy-start.15 = (bf16[192,1024]{1,0:T(8,128)(2,1)S(1)}, bf16[192,1024]{1,0:T(8,128)(2,1)}, u32[]{:S(2)}) copy-start(bf16[192,1024]{1,0:T(8,128)(2,1)} %get-tuple-element.89.refs_4_) | copy-start | bytes 1179652
  154.5 8.8 %copy-start.16 = (bf16[192,1024]{1,0:T(8,128)(2,1)S(1)}, bf16[192,1024]{1,0:T(8,128)(2,1)}, u32[]{:S(2)}) copy-start(bf16[192,1024]{1,0:T(8,128)(2,1)} %get-tuple-element.90.refs_5_) | copy-start | bytes 1179652
  154.5 32.8 %all-to-all-start.3 = ((bf16[8,24,2816]{2,1,0:T(8,128)(2,1)}), bf16[8,24,2816]{2,1,0:T(8,128)(2,1)}, u32[]{:S(2)}, u32[]{:S(2)}) async-start(bf16[8,24,2816]{2,1,0:T(8,128)(2,1)} %pad_maximum_fusion), calls=%async_computation.3 | async-start | bytes 2162688 | tf_op jit(solution)/shard_map/all_to_all | solution.py:279
  160.5 2.9 %copy-start.17 = (bf16[192,1024]{1,0:T(8,128)(2,1)S(1)}, bf16[192,1024]{1,0:T(8,128)(2,1)}, u32[]{:S(2)}) copy-start(bf16[192,1024]{1,0:T(8,128)(2,1)} %get-tuple-element.91.refs_6_) | copy-start | bytes 1179652
  160.5 2.9 %copy-start.18 = (bf16[192,1024]{1,0:T(8,128)(2,1)S(1)}, bf16[192,1024]{1,0:T(8,128)(2,1)}, u32[]{:S(2)}) copy-start(bf16[192,1024]{1,0:T(8,128)(2,1)} %get-tuple-element.92.refs_7_) | copy-start | bytes 1179652
  163.4 8.9 %copy-start.4 = (bf16[8,24,2560]{2,1,0:T(8,128)(2,1)S(1)}, bf16[8,24,2560]{2,1,0:T(8,128)(2,1)}, u32[]{:S(2)}) copy-start(bf16[8,24,2560]{2,1,0:T(8,128)(2,1)} %copy-done.3) | copy-start | bytes 2949124
  163.4 8.9 %copy-start.8 = (bf16[192,2560]{1,0:T(8,128)(2,1)S(1)}, bf16[192,2560]{1,0:T(8,128)(2,1)}, u32[]{:S(2)}) copy-start(bf16[192,2560]{1,0:T(8,128)(2,1)} %copy-done.7) | copy-start | bytes 2949124
  163.4 8.9 %copy-start.10 = (bf16[192,2560]{1,0:T(8,128)(2,1)S(1)}, bf16[192,2560]{1,0:T(8,128)(2,1)}, u32[]{:S(2)}) copy-start(bf16[192,2560]{1,0:T(8,128)(2,1)} %copy-done.9) | copy-start | bytes 2949124
  163.4 8.9 %copy-start.11 = (bf16[192,1024]{1,0:T(8,128)(2,1)S(1)}, bf16[192,1024]{1,0:T(8,128)(2,1)}, u32[]{:S(2)}) copy-start(bf16[192,1024]{1,0:T(8,128)(2,1)} %get-tuple-element.93.refs_4_.refs_0_) | copy-start | bytes 1179652
  163.4 8.9 %copy-start.12 = (bf16[192,1024]{1,0:T(8,128)(2,1)S(1)}, bf16[192,1024]{1,0:T(8,128)(2,1)}, u32[]{:S(2)}) copy-start(bf16[192,1024]{1,0:T(8,128)(2,1)} %get-tuple-element.94.refs_5_.refs_1_) | copy-start | bytes 1179652
  163.4 8.9 %copy-start.13 = (bf16[192,1024]{1,0:T(8,128)(2,1)S(1)}, bf16[192,1024]{1,0:T(8,128)(2,1)}, u32[]{:S(2)}) copy-start(bf16[192,1024]{1,0:T(8,128)(2,1)} %get-tuple-element.95.refs_4_.refs_2_) | copy-start | bytes 1179652
  163.4 8.9 %copy-start.14 = (bf16[192,1024]{1,0:T(8,128)(2,1)S(1)}, bf16[192,1024]{1,0:T(8,128)(2,1)}, u32[]{:S(2)}) copy-start(bf16[192,1024]{1,0:T(8,128)(2,1)} %get-tuple-element.96.refs_5_.refs_3_) | copy-start | bytes 1179652
